TPU v7x, 256 devices: a whole 4x4x8 slice. The times are simulated.
256 devices in a mesh: ky: 16 (over x, y_hi, core), kx: 16 (over z, y_lo).
Axes of the slice: x: 4, y: 4 (y_hi: 2, y_lo: 2; y = y_hi * 2 + y_lo), z: 8, core: 2. Of those that a mesh axis runs over, the one named last changes fastest.
Arguments:
- spectrum: bfloat16 [2, 8192, 8192], P(None, 'ky', 'kx'), may hold values from -6 to 6
- pupil_field: bfloat16 [2, 1024, 1024], replicated, may hold values from -3 to 3
- amplitude: bfloat16 [16384, 16384], P('ky', 'kx'), may hold values from 0 to 2
- offsets: int32 [16, 16, 2], P('ky', 'kx'), may hold values from -384 to 7552, as said below
Outputs:
- spectrum_grad: float32 [2, 8192, 8192], P(None, 'ky', 'kx')
- pupil_grad: float32 [2097152], P(('ky', 'kx'))
Inputs may be any that keep to these rules, and one draw needn't show every extreme that they name: offsets[i, j] = (i * 512 - 512/2 + dy, j * 512 - 512/2 + dx) with whole numbers dy, dx from -128 to 128; both ends of this range are taken in every draw.
All inputs are finite; a program needn't handle non-finite values.
Results may differ from a plain program's by a relative error of at most 0.0028.
Values may be sent and summed in bfloat16 or wider, within the bound.
No kernel may reach another device: no remote copies, remote signals or barrier semaphores. Data moves between devices by JAX's collectives and lax.ppermute only.
A program may use at most 192 MiB of HBM per device.

v0:
```python
import math

import jax
import jax.numpy as jnp
from jax import lax
from jax.sharding import PartitionSpec as P

AMP_FLOOR = 0.25


def extended_2(array, sides, width):
    for axis, dim in sides:
        devices, length = (lax.axis_size(axis), array.shape[dim])
        up = [(i, (i + 1) % devices) for i in range(devices - 1)]
        down = [(j, i) for i, j in up]
        last = lax.slice_in_dim(array, length - width, length, axis=dim)
        leading = lax.slice_in_dim(array, 0, width, axis=dim)
        before = lax.ppermute(last, axis, up)
        after = lax.ppermute(leading, axis, down)
        array = jnp.concatenate([before, array, after], axis=dim)
    return array


def factors(length):
    base_size = 128
    return (length // base_size, base_size)


def phase_table(rows_count, cols_count, modulus, angle_sign):
    left_index = jnp.arange(rows_count, dtype=jnp.int32)[:, None]
    right_index = jnp.arange(cols_count, dtype=jnp.int32)[None, :]
    products = left_index * right_index % modulus
    angles = angle_sign * 2.0 * math.pi / modulus * products.astype(jnp.float32)
    return (jnp.cos(angles), jnp.sin(angles))


def block_table(table_real, table_imag):
    first_row = jnp.stack([table_real, table_imag], axis=1)
    second_row = jnp.stack([-table_imag, table_real], axis=1)
    return jnp.stack([first_row, second_row], axis=0)


def complex_section(stacked, table, left_spec, table_spec, out_spec):
    full_form = "p" + left_spec + ",p" + table_spec[0] + "q" + table_spec[1] + "->q" + out_spec
    return jnp.einsum(full_form, stacked, table, precision=lax.Precision.HIGHEST)


def twist(stacked, table_real, table_imag):
    real_part = stacked[0] * table_real - stacked[1] * table_imag
    imag_part = stacked[0] * table_imag + stacked[1] * table_real
    return jnp.stack([real_part, imag_part])


def transform(stacked, angle_sign, along_rows, scrambled_out):
    length = stacked.shape[1]
    size_a, size_b = factors(length)
    short_table = block_table(*phase_table(size_a, size_a, size_a, angle_sign))
    long_table = block_table(*phase_table(size_b, size_b, size_b, angle_sign))
    twist_real, twist_imag = phase_table(size_a, size_b, length, angle_sign)
    if along_rows:
        split_shape = (2, size_a, size_b, length)
        twist_real = twist_real[:, :, None]
        twist_imag = twist_imag[:, :, None]
        if scrambled_out:
            first_forms = ("abw", "ac", "cbw")
            second_forms = ("cbw", "bd", "cdw")
        else:
            first_forms = ("abw", "bd", "adw")
            second_forms = ("adw", "ac", "cdw")
    else:
        split_shape = (2, length, size_a, size_b)
        if scrambled_out:
            first_forms = ("wab", "ac", "wcb")
            second_forms = ("wcb", "bd", "wcd")
        else:
            first_forms = ("wab", "bd", "wad")
            second_forms = ("wad", "ac", "wcd")
    if scrambled_out:
        first_table, second_table = (short_table, long_table)
    else:
        first_table, second_table = (long_table, short_table)
    parts = stacked.reshape(split_shape)
    parts = complex_section(parts, first_table, first_forms[0], first_forms[1], first_forms[2])
    parts = twist(parts, twist_real, twist_imag)
    parts = complex_section(parts, second_table, second_forms[0], second_forms[1], second_forms[2])
    return parts.reshape(2, length, length)


def fold_rims(extended, axis, tile_side, rim_width):
    middle = lax.slice_in_dim(extended, 2 * rim_width, 2 * rim_width + tile_side, axis=axis).astype(
        jnp.float32
    )
    left_rim = lax.slice_in_dim(extended, 0, rim_width, axis=axis).astype(jnp.float32)
    right_rim = lax.slice_in_dim(
        extended, 3 * rim_width + tile_side, 4 * rim_width + tile_side, axis=axis
    ).astype(jnp.float32)
    left_pads = [(0, 0)] * extended.ndim
    right_pads = [(0, 0)] * extended.ndim
    left_pads[axis] = (0, tile_side - rim_width)
    right_pads[axis] = (tile_side - rim_width, 0)
    return middle + jnp.pad(left_rim, left_pads) + jnp.pad(right_rim, right_pads)


def body(spectrum, pupil_field, amplitude, offsets):
    tile_side = spectrum.shape[1]
    rim_width = 3 * tile_side // 4
    win_side = 2 * tile_side
    region = extended_2(spectrum, (("ky", 1), ("kx", 2)), rim_width)
    led_row = lax.axis_index("ky")
    led_col = lax.axis_index("kx")
    row_start = offsets[0, 0, 0] - (led_row * tile_side - rim_width)
    col_start = offsets[0, 0, 1] - (led_col * tile_side - rim_width)
    zero_index = jnp.zeros((), jnp.int32)
    window = lax.dynamic_slice(
        region, (zero_index, row_start, col_start), (2, win_side, win_side)
    ).astype(jnp.float32)
    pupil_real = pupil_field[0].astype(jnp.float32)
    pupil_imag = pupil_field[1].astype(jnp.float32)
    field = jnp.stack(
        [
            pupil_real * window[0] - pupil_imag * window[1],
            pupil_real * window[1] + pupil_imag * window[0],
        ]
    )
    scale = 1.0 / win_side
    image = transform(field, 1.0, False, True)
    image = transform(image, 1.0, True, True) * scale
    size_a, size_b = factors(win_side)
    measured = (
        amplitude.reshape(size_b, size_a, size_b, size_a)
        .transpose(1, 0, 3, 2)
        .reshape(win_side, win_side)
        .astype(jnp.float32)
    )
    magnitude = jnp.sqrt(image[0] * image[0] + image[1] * image[1])
    ratio = measured / jnp.maximum(magnitude, AMP_FLOOR)
    resid = image - ratio[None] * image
    spec = transform(resid, -1.0, False, False)
    spec = transform(spec, -1.0, True, False) * scale
    grad_real = (pupil_real * spec[0] + pupil_imag * spec[1]).astype(jnp.bfloat16)
    grad_imag = (pupil_real * spec[1] - pupil_imag * spec[0]).astype(jnp.bfloat16)
    term_real = window[0] * spec[0] + window[1] * spec[1]
    term_imag = window[0] * spec[1] - window[1] * spec[0]
    led_count = lax.axis_size("ky") * lax.axis_size("kx")
    pupil_terms = jnp.stack([term_real, term_imag]).reshape(-1) / led_count
    pupil_grad = lax.psum_scatter(pupil_terms, ("ky", "kx"), scatter_dimension=0, tiled=True)
    frame_side = tile_side + 2 * rim_width
    frame = jnp.zeros((2, frame_side, frame_side), jnp.bfloat16)
    frame = lax.dynamic_update_slice(
        frame, jnp.stack([grad_real, grad_imag]), (zero_index, row_start, col_start)
    )
    extended = extended_2(frame, (("ky", 1), ("kx", 2)), rim_width)
    spectrum_grad = fold_rims(fold_rims(extended, 1, tile_side, rim_width), 2, tile_side, rim_width)
    return (spectrum_grad, pupil_grad)


def solution(mesh):
    return jax.shard_map(
        body,
        mesh=mesh,
        in_specs=(P(None, "ky", "kx"), P(), P("ky", "kx"), P("ky", "kx", None)),
        out_specs=(P(None, "ky", "kx"), P(("ky", "kx"))),
        check_vma=False,
    )
```

profile of v0, /device:TPU:1, one launch (start us, length us, event | category | flops | bytes accessed | tf_op | source)
XLA Modules:
  0.0 792.2 jit_solution(4740893011711712782)
XLA Ops:
  7.2 1.6 fusion.102
  8.8 6.2 collective-permute-start
  15.0 1.9 collective-permute-start.1
  16.9 40.4 %collective-permute-done = bf16[2,384,512]{2,1,0:T(8,128)(2,1)S(1)} collective-permute-done((bf16[2,384,512]{2,1,0:T(8,128)(2,1)S(1)}, bf16[2,384,512]{2,1,0:T(8,128)(2,1)S(1)}, u32[]{:S(2)}, u32[]{:S(2)}) %collective-permute-start) | collective-permute-done | bytes 786464 | tf_op jit(solution)/shard_map/ppermute | solution.py:18
  57.5 2.3 fusion.101
  59.9 2.6 collective-permute-start.2
  62.5 1.3 collective-permute-start.3
  63.8 0.6 fusion.103
  66.2 42.2 %reshape.376 = f32[128,8,128,8]{3,2,1,0:T(8,128)} reshape(bf16[1024,1024]{1,0:T(8,128)(2,1)} %param.6) | data formatting | bytes 6291456 | tf_op jit(solution)/shard_map/convert_element_type | solution.py:133
  108.4 35.0 %copy.76 = f32[8,128,8,128]{3,2,1,0:T(8,128)} copy(f32[8,128,8,128]{2,3,0,1:T(8,128)} %bitcast.38) | data formatting | bytes 8388608 | tf_op jit(solution)/shard_map/convert_element_type | solution.py:133
  143.4 5.0 reshape.373
  149.2 0.3 multiply_sine_fusion
  149.5 0.3 multiply_sine_fusion.1
  149.8 6.2 fusion.32
  156.1 2.4 fusion.34
  158.5 1.8 copy-done
  160.4 1.0 copy.102
  161.4 1.0 copy.103
  162.4 8.1 %fusion.68 = f32[2,1024,8,128]{3,2,1,0:T(8,128)S(1)} fusion(f32[1,1024,8,128]{3,2,0,1:T(8,128)S(1)} %bitcast.185, f32[1,1024,8,128]{3,2,0,1:T(8,128)S(1)} %bitcast.184, f32[1,8,2,8]{1,3,0,2:T(8,128)S(1)} %copy.69, f32[1,8,2,8]{1,3,0,2:T(8,128)S(1)} %copy.68), kind=kOutput, calls=%fused_computation.96 | convolution fusion | flops 404750592 | bytes 16778240 | tf_op jit(solution)/shard_map/pwab,paqc->qwcb/dot_general | solution.py:45
  170.5 0.9 multiply_subtract_fusion.3
  171.4 0.5 pad_maximum_fusion
  171.9 9.7 %fusion.20 = f32[2,128,1024,8,1]{2,1,4,3,0:T(8,128)S(1)} fusion(f32[2,1024,8,128]{3,2,1,0:T(8,128)S(1)} %pad_maximum_fusion, f32[1,128,2,128]{1,3,0,2:T(8,128)S(1)} %get-tuple-element.31, f32[1,128,2,128]{1,3,0,2:T(8,128)S(1)} %get-tuple-element.30), kind=kOutput, calls=%fused_computation.28 | convolution fusion | flops 6442516480 | bytes 17039360 | tf_op jit(solution)/shard_map/pwcb,pbqd->qwcd/dot_general | solution.py:45
  181.7 5.3 copy.104
  187.0 8.8 %copy.71 = f32[2,8,128,1024]{3,1,0,2:T(8,128)} copy(f32[2,8,128,1024]{2,1,3,0:T(8,128)} %bitcast.182) | data formatting | bytes 16777216 | tf_op jit(solution)/shard_map/reshape;reshape | solution.py:82
  195.8 11.7 %fusion.56 = f32[2,8,128,1024]{3,1,2,0:T(8,128)S(1)} fusion(f32[2,8,128,1024]{3,1,0,2:T(8,128)} %copy.71, f32[1,8,2,8]{1,3,0,2:T(8,128)S(1)} %copy.69, f32[1,8,2,8]{1,3,0,2:T(8,128)S(1)} %copy.68), kind=kOutput, calls=%fused_computation.92 | convolution fusion | flops 402653440 | bytes 16778240 | tf_op jit(solution)/shard_map/pabw,paqc->qcbw/dot_general | solution.py:45
  207.5 1.1 multiply_subtract_fusion.2
  208.6 1.7 pad_maximum_fusion.1
  210.3 13.1 %bitcast_multiply_fusion = (f32[2,8,128,1024]{3,2,1,0:T(8,128)}, f32[2,128,8,1024,1]{3,1,4,2,0:T(8,128)S(1)}) fusion(f32[2,8,128,1024]{3,1,2,0:T(8,128)S(1)} %pad_maximum_fusion.1, f32[1,128,2,128]{1,3,0,2:T(8,128)S(1)} %get-tuple-element.31, f32[1,128,2,128]{1,3,0,2:T(8,128)S(1)} %get-tuple-element.30), kind=kOutput, calls=%fused_computation.23 | convolution fusion | flops 6444613632 | bytes 25427968 | tf_op jit(solution)/shard_map/pcbw,pbqd->qcdw/dot_general | solution.py:45
  223.4 5.1 fusion.47
  228.5 1.0 fusion.50
  229.5 1.0 copy.106
  230.5 0.8 copy.77
  231.3 2.1 copy.105
  233.4 10.0 %fusion.65 = f32[2,1024,8,128]{1,3,2,0:T(8,128)S(1)} fusion(f32[2,1024,8,128]{3,2,1,0:T(8,128)S(1)} %bitcast.183, f32[1024,8,128]{2,0,1:T(8,128)S(1)} %copy.77, f32[1,128,2,128]{1,3,2,0:T(8,128)S(1)} %get-tuple-element.29, f32[1,128,2,128]{1,3,2,0:T(8,128)S(1)} %get-tuple-element.28), kind=kOutput, calls=%fused_computation.95 | convolution fusion | flops 6448807936 | bytes 21233664 | tf_op jit(solution)/shard_map/pwab,pbqd->qwad/dot_general | solution.py:45
  243.4 1.1 multiply_subtract_fusion.1
  244.5 4.1 pad_maximum_fusion.2
  248.7 9.2 %copy.80 = f32[2,1024,8,128]{3,2,0,1:T(8,128)} copy(f32[2,1024,8,128]{1,3,2,0:T(8,128)} %pad_maximum_fusion.2) | data formatting | bytes 16777216 | tf_op jit(solution)/shard_map/stack | solution.py:51
  257.8 12.1 %fusion.59 = f32[2,1024,8,128]{3,2,1,0:T(8,128)} fusion(f32[2,1024,8,128]{3,2,0,1:T(8,128)} %copy.80, f32[1,8,2,8]{1,3,0,2:T(8,128)S(1)} %copy.66, f32[1,8,2,8]{1,3,0,2:T(8,128)S(1)} %copy.65), kind=kOutput, calls=%fused_computation.93 | convolution fusion | flops 402653440 | bytes 16778240 | tf_op jit(solution)/shard_map/pwad,paqc->qwcd/dot_general | solution.py:45
  270.0 9.2 %reshape_reshape.7 = f32[2,8,128,1024]{3,2,1,0:T(8,128)} reshape(f32[2,1024,8,128]{3,2,1,0:T(8,128)} %fusion.59) | data formatting | bytes 16777216 | tf_op jit(solution)/shard_map/reshape;reshape | solution.py:82
  279.2 9.7 %fusion.53 = f32[2,8,128,1024]{3,2,1,0:T(8,128)S(1)} fusion(f32[2,8,128,1024]{3,2,1,0:T(8,128)} %reshape_reshape.7, f32[1,128,2,128]{1,3,2,0:T(8,128)S(1)} %get-tuple-element.29, f32[1,128,2,128]{1,3,2,0:T(8,128)S(1)} %get-tuple-element.28), kind=kOutput, calls=%fused_computation.91 | convolution fusion | flops 6442516480 | bytes 17039360 | tf_op jit(solution)/shard_map/pabw,pbqd->qadw/dot_general | solution.py:45
  288.9 1.3 multiply_subtract_fusion
  290.2 1.7 pad_maximum_fusion.3
  291.9 12.0 %fusion.62 = f32[2,8,128,1024]{3,1,2,0:T(8,128)S(1)} fusion(f32[2,8,128,1024]{3,2,1,0:T(8,128)S(1)} %pad_maximum_fusion.3, f32[1,8,2,8]{1,3,0,2:T(8,128)S(1)} %copy.66, f32[1,8,2,8]{1,3,0,2:T(8,128)S(1)} %copy.65), kind=kOutput, calls=%fused_computation.94 | convolution fusion | flops 402653440 | bytes 16778240 | tf_op jit(solution)/shard_map/padw,paqc->qcdw/dot_general | solution.py:45
  303.9 8.5 %copy_multiply_fusion = f32[2,8,128,1024]{3,2,1,0:T(8,128)} fusion(f32[2,8,128,1024]{3,1,2,0:T(8,128)S(1)} %fusion.62), kind=kLoop, calls=%fused_computation.30 | loop fusion | flops 2097152 | bytes 16777216 | tf_op jit(solution)/shard_map/mul | solution.py:139
  312.4 4.5 fusion.99
  317.1 1.3 copy-done.3
  318.4 7.2 fusion.48
  325.5 4.6 pad_maximum_fusion.4
  330.2 3.2 broadcast_in_dim.2
  333.3 45.4 %dynamic_update_slice.3 = bf16[2,1280,1280]{2,1,0:T(8,128)(2,1)} dynamic-update-slice(bf16[2,1280,1280]{2,1,0:T(8,128)(2,1)} %broadcast_in_dim.2, bf16[2,1024,1024]{2,1,0:T(8,128)(2,1)} %pad_maximum_fusion.4, s32[]{:T(128)} %constant.92.clone.1, s32[]{:T(128)S(6)} %select_n.185, s32[]{:T(128)S(6)} %select_n.186) | dynamic-update-slice | bytes 8388612 | tf_op jit(solution)/shard_map/dynamic_update_slice | solution.py:149
  378.7 4.5 fusion.100
  383.3 6.2 collective-permute-start.4
  389.5 2.2 collective-permute-start.5
  391.7 3.6 maximum_multiply_fusion
  395.3 5.3 copy.107
  400.7 29.3 %collective-permute-done.4 = bf16[2,384,1280]{2,1,0:T(8,128)(2,1)S(1)} collective-permute-done((bf16[2,384,1280]{2,1,0:T(8,128)(2,1)}, bf16[2,384,1280]{2,1,0:T(8,128)(2,1)S(1)}, u32[]{:S(2)}, u32[]{:S(2)}) %collective-permute-start.4) | collective-permute-done | bytes 1966112 | tf_op jit(solution)/shard_map/ppermute | solution.py:18
  430.0 29.5 %collective-permute-done.5 = bf16[2,384,1280]{2,1,0:T(8,128)(2,1)} collective-permute-done((bf16[2,384,1280]{2,1,0:T(8,128)(2,1)}, bf16[2,384,1280]{2,1,0:T(8,128)(2,1)}, u32[]{:S(2)}, u32[]{:S(2)}) %collective-permute-start.5) | collective-permute-done | bytes 1966112 | tf_op jit(solution)/shard_map/ppermute | solution.py:19
  459.5 4.8 pad_maximum_fusion.7
  464.2 3.0 collective-permute-start.6
  467.3 1.3 collective-permute-start.7
  468.6 296.3 %all-reduce.5.cloned.1.call-done = f32[2097152]{0:T(1024)} async-done(((f32[2097152]{0:T(1024)}), f32[2097152]{0:T(1024)}) %all-reduce.5.cloned.1.call-update) | async-done | bytes 8388624
  764.9 1.4 dynamic-slice
  766.3 16.7 %convert_add_fusion = f32[2,512,2048]{2,1,0:T(8,128)S(1)} fusion(bf16[2,2048,384]{2,1,0:T(8,128)(2,1)} %collective-permute-done.7, bf16[2,2048,384]{2,1,0:T(8,128)(2,1)} %collective-permute-done.6, bf16[2,384,1280]{2,1,0:T(8,128)(2,1)} %collective-permute-done.5, bf16[2,1280,1280]{2,1,0:T(8,128)(2,1)} %dynamic_update_slice.3, ...), kind=kLoop, calls=%fused_computation.35 | loop fusion | flops 83886080 | bytes 25166336 | tf_op jit(solution)/shard_map/add | solution.py:101
  783.2 1.7 fusion.70
  (48 shorter events, 1.9 us)
Async XLA Ops:
  7.2 757.7 %all-reduce.5.cloned.1.call-start = ((), (), s32[]{:S(2)}) async-start(), calls=%async_computation | async-start | bytes 16777216
  7.2 50.1 %copy-start.5 = (bf16[2,512,512]{2,1,0:T(8,128)(2,1)S(1)}, bf16[2,512,512]{2,1,0:T(8,128)(2,1)}, u32[]{:S(2)}) copy-start(bf16[2,512,512]{2,1,0:T(8,128)(2,1)} %param.4) | copy-start | bytes 3145732
  8.8 48.5 %collective-permute-start = (bf16[2,384,512]{2,1,0:T(8,128)(2,1)S(1)}, bf16[2,384,512]{2,1,0:T(8,128)(2,1)S(1)}, u32[]{:S(2)}, u32[]{:S(2)}) collective-permute-start(bf16[2,384,512]{2,1,0:T(8,128)(2,1)S(1)} %get-tuple-element.27), channel_id=1, source_target_pairs={{0,16},{16,32},{32,48},{48,64},{64,80},{80,96},{96,112},{112,128},... | collective-permute-start | bytes 2359304 | tf_op jit(solution)/shard_map/ppermute | solution.py:18
  15.0 42.4 %collective-permute-start.1 = (bf16[2,384,512]{2,1,0:T(8,128)(2,1)S(1)}, bf16[2,384,512]{2,1,0:T(8,128)(2,1)S(1)}, u32[]{:S(2)}, u32[]{:S(2)}) collective-permute-start(bf16[2,384,512]{2,1,0:T(8,128)(2,1)S(1)} %get-tuple-element.26), channel_id=1, source_target_pairs={{16,0},{32,16},{48,32},{64,48},{80,64},{96,80},{112,96},{128,112},... | collective-permute-start | bytes 2359304 | tf_op jit(solution)/shard_map/ppermute | solution.py:19
  57.5 6.3 copy-start.7
  59.9 90.0 %collective-permute-start.2 = (bf16[2,1280,384]{2,1,0:T(8,128)(2,1)}, bf16[2,1280,384]{2,1,0:T(8,128)(2,1)}, u32[]{:S(2)}, u32[]{:S(2)}) collective-permute-start(bf16[2,1280,384]{2,1,0:T(8,128)(2,1)} %get-tuple-element.25), channel_id=1, source_target_pairs={{0,1},{1,2},{2,3},{3,4},{4,5},{5,6},{6,7},{7,8},{8,9},{9,10},{10,1... | collective-permute-start | bytes 5898248 | tf_op jit(solution)/shard_map/ppermute | solution.py:18
  62.5 87.4 %collective-permute-start.3 = (bf16[2,1280,384]{2,1,0:T(8,128)(2,1)}, bf16[2,1280,384]{2,1,0:T(8,128)(2,1)}, u32[]{:S(2)}, u32[]{:S(2)}) collective-permute-start(bf16[2,1280,384]{2,1,0:T(8,128)(2,1)} %get-tuple-element.24), channel_id=1, source_target_pairs={{1,0},{2,1},{3,2},{4,3},{5,4},{6,5},{7,6},{8,7},{9,8},{10,9},{11,1... | collective-permute-start | bytes 5898248 | tf_op jit(solution)/shard_map/ppermute | solution.py:19
  149.8 6.3 copy-start.2
  156.1 4.3 copy-start
  223.4 5.1 copy-start.1
  303.9 13.0 %slice-start = ((s8[8388608]{0:T(1024)(128)(4,1)}), s8[4194304]{0:T(1024)(128)(4,1)S(1)}, s32[]{:S(2)}) async-start(s8[8388608]{0:T(1024)(128)(4,1)} %bitcast.176), calls=%async_computation.1 | async-start | bytes 8388608
  312.4 4.6 slice-start.1
  312.4 5.9 copy-start.3
  378.7 13.0 %copy-start.4 = (f32[1,1024,1024]{2,1,0:T(8,128)S(1)}, f32[1,1024,1024]{2,1,0:T(8,128)}, u32[]{:S(2)}) copy-start(f32[1,1024,1024]{2,1,0:T(8,128)} %get-tuple-element.2) | copy-start | bytes 12582916
  383.3 46.7 %collective-permute-start.4 = (bf16[2,384,1280]{2,1,0:T(8,128)(2,1)}, bf16[2,384,1280]{2,1,0:T(8,128)(2,1)S(1)}, u32[]{:S(2)}, u32[]{:S(2)}) collective-permute-start(bf16[2,384,1280]{2,1,0:T(8,128)(2,1)} %get-tuple-element.22), channel_id=1, source_target_pairs={{0,16},{16,32},{32,48},{48,64},{64,80},{80,96},{96,112},{112,128},... | collective-permute-start | bytes 5898248 | tf_op jit(solution)/shard_map/ppermute | solution.py:18
  389.5 70.0 %collective-permute-start.5 = (bf16[2,384,1280]{2,1,0:T(8,128)(2,1)}, bf16[2,384,1280]{2,1,0:T(8,128)(2,1)}, u32[]{:S(2)}, u32[]{:S(2)}) collective-permute-start(bf16[2,384,1280]{2,1,0:T(8,128)(2,1)} %get-tuple-element.23), channel_id=1, source_target_pairs={{16,0},{32,16},{48,32},{64,48},{80,64},{96,80},{112,96},{128,112},... | collective-permute-start | bytes 5898248 | tf_op jit(solution)/shard_map/ppermute | solution.py:19
  400.7 365.6 %copy-start.6 = (pred[512]{0:T(512)(128)(4,1)S(1)}, pred[512]{0:T(512)(128)(4,1)}, u32[]{:S(2)}) copy-start(pred[512]{0:T(512)(128)(4,1)} %constant.112.clone.1) | copy-start | bytes 1540
  464.2 302.0 %collective-permute-start.6 = (bf16[2,2048,384]{2,1,0:T(8,128)(2,1)}, bf16[2,2048,384]{2,1,0:T(8,128)(2,1)}, u32[]{:S(2)}, u32[]{:S(2)}) collective-permute-start(bf16[2,2048,384]{2,1,0:T(8,128)(2,1)} %get-tuple-element.8), channel_id=1, source_target_pairs={{0,1},{1,2},{2,3},{3,4},{4,5},{5,6},{6,7},{7,8},{8,9},{9,10},{10,1... | collective-permute-start | bytes 9437192 | tf_op jit(solution)/shard_map/ppermute | solution.py:18
  467.3 299.0 %collective-permute-start.7 = (bf16[2,2048,384]{2,1,0:T(8,128)(2,1)}, bf16[2,2048,384]{2,1,0:T(8,128)(2,1)}, u32[]{:S(2)}, u32[]{:S(2)}) collective-permute-start(bf16[2,2048,384]{2,1,0:T(8,128)(2,1)} %get-tuple-element.9), channel_id=1, source_target_pairs={{1,0},{2,1},{3,2},{4,3},{5,4},{6,5},{7,6},{8,7},{9,8},{10,9},{11,1... | collective-permute-start | bytes 9437192 | tf_op jit(solution)/shard_map/ppermute | solution.py:19
Sparse Core Ops, SparseCore 0:
  400.8 364.0 all-reduce.4
where the time goes:
time: 802 us; the launch traced here: 792 us
  waiting for transfers between devices  396 us (49%)
  local copies, waits for them, and re-layouts  193 us (24%)
  matrix products  86.5 us (11%)
  other arithmetic  75.7 us (9%)
  starting transfers between devices  24.8 us (3%)
  between operations  16.3 us (2%)
    unnamed x2, waiting for transfers between devices  296 us
    dot_general x8, matrix products, complex_section(): jnp.einsum(full_form, stacked, table, precision=lax.Precision.HIGHEST)  86.5 us
    convert_element_type x3, local copies, waits for them, and re-layouts, body(): measured = amplitude.reshape(size_b, size_a, size_b, size_a).transpose(1,...  82.2 us
    ppermute x4, waiting for transfers between devices, extended_2(): before = lax.ppermute(last, axis, up)  69.7 us
    dynamic_update_slice x1, local copies, waits for them, and re-layouts, body(): lax.dynamic_update_slice(frame, jnp.stack([grad_real, grad_imag]), (zero_...  45.4 us
    ppermute x4, waiting for transfers between devices, extended_2(): after = lax.ppermute(leading, axis, down)  29.5 us
    unnamed x29, local copies, waits for them, and re-layouts  20.6 us
    add x2, other arithmetic, fold_rims(): middle + jnp.pad(left_rim, left_pads) + jnp.pad(right_rim, right_pads)  18.5 us
  transfers between devices with their start and end apart: 9, of which 4 were waited for; matrix products, arithmetic and copies ran while one was open for 13% of the time, Pallas kernels for 0%

commit v1 on v0

v1 whole, which is shorter than its diff:
```python
import math

import jax
import jax.numpy as jnp
import ml_dtypes
import numpy as np
from jax import lax
from jax.experimental import pallas as pl
from jax.experimental.pallas import tpu as pltpu
from jax.sharding import Mesh
from jax.sharding import PartitionSpec as P

F32 = jnp.float32
BF16 = jnp.bfloat16
N = 1024
TILE = 512
RIM = 384
REGION = TILE + 2 * RIM
FLOOR2 = 0.0625


def split_np(t):
    hi = t.astype(np.float32).astype(ml_dtypes.bfloat16)
    lo = (t - hi.astype(np.float64)).astype(np.float32).astype(ml_dtypes.bfloat16)
    return hi, lo


def tables():
    b = np.arange(128)
    ang = 2.0 * np.pi / 128 * ((b[:, None] * b[None, :]) % 128)
    out = {}
    for name, sign in (("inv", 1.0), ("fwd", -1.0)):
        cr, ci = np.cos(ang) / 32.0, sign * np.sin(ang) / 32.0
        block = np.block([[cr, ci], [-ci, cr]])
        hi, lo = split_np(block)
        out["lane_" + name] = np.concatenate([hi, hi, lo], axis=0)
        out["row_" + name] = np.concatenate([hi.T, hi.T, lo.T], axis=1)
    tw = 2.0 * np.pi / N * (np.arange(8)[:, None] * b[None, :])
    tw = np.stack([np.cos(tw), np.sin(tw)]).astype(np.float32)
    out["tw_lane"] = tw.reshape(2, 8, 1, 128)
    out["tw_row"] = np.ascontiguousarray(np.broadcast_to(tw[:, :, :, None], (2, 8, 128, 128)))
    s = np.arange(N)
    perm = np.zeros((N, N), ml_dtypes.bfloat16)
    perm[s, (s // 128) + 8 * (s % 128)] = 1
    out["perm"] = perm
    return out


def cadd(p, q):
    return (p[0] + q[0], p[1] + q[1])


def csub(p, q):
    return (p[0] - q[0], p[1] - q[1])


def crot(p, sign):
    return (-p[1], p[0]) if sign > 0 else (p[1], -p[0])


def fft4(x0, x1, x2, x3, sign):
    t0, t1 = cadd(x0, x2), csub(x0, x2)
    t2, t3 = cadd(x1, x3), crot(csub(x1, x3), sign)
    return [cadd(t0, t2), cadd(t1, t3), csub(t0, t2), csub(t1, t3)]


def fft8(x, sign):
    even = fft4(x[0], x[2], x[4], x[6], sign)
    odd = fft4(x[1], x[3], x[5], x[7], sign)
    h = math.sqrt(0.5)
    r, i = odd[1]
    odd[1] = ((r - i) * h, (r + i) * h) if sign > 0 else ((r + i) * h, (i - r) * h)
    odd[2] = crot(odd[2], sign)
    r, i = odd[3]
    odd[3] = ((-r - i) * h, (r - i) * h) if sign > 0 else ((i - r) * h, (-r - i) * h)
    return [cadd(e, o) for e, o in zip(even, odd)] + [csub(e, o) for e, o in zip(even, odd)]


def split(x):
    hi = x.astype(BF16)
    return hi, (x - hi.astype(F32)).astype(BF16)


def dot(a, b):
    return jnp.dot(a, b, preferred_element_type=F32)


RB = 256
CB = 256


def led_body(
    pos_ref, own_ref, l_ref, r_ref, v_ref, vl_ref, vr_ref, i_ref, il_ref, ir_ref, pup_ref, ampl_ref,
    li_ref, lf_ref, ri_ref, rf_ref, twl_ref, twr_ref,
    oc_ref, ol_ref, or_ref, ov_ref, ovl_ref, ovr_ref, oi_ref, oil_ref, oir_ref, mine_ref, other_ref,
    w_ref, p_ref, amp_ref, a_ref, s_ref, s2_ref, z_ref, z2_ref, t_ref, in_sem, out_sem,
):
    r0, c0, core = pos_ref[0], pos_ref[1], pos_ref[2]
    outer = pl.multiple_of((RIM + TILE) * core, 128)
    inner = pl.multiple_of((RIM + TILE) * (1 - core), 128)
    places = []
    for start, count in ((RIM, TILE), (outer, RIM), (inner, RIM)):
        for col, wide in ((RIM, TILE), (0, RIM), (RIM + TILE, RIM)):
            places.append(w_ref.at[:, pl.ds(start, count), pl.ds(col, wide)])
    arrivals = (own_ref, l_ref, r_ref, v_ref, vl_ref, vr_ref, i_ref, il_ref, ir_ref)
    loads = [pltpu.make_async_copy(x, y, in_sem.at[k]) for k, (x, y) in enumerate(zip(arrivals, places))]
    loads.append(pltpu.make_async_copy(pup_ref, p_ref, in_sem.at[9]))
    amp_load = pltpu.make_async_copy(ampl_ref, amp_ref, in_sem.at[10])
    for load in loads:
        load.start()
    amp_load.start()

    def lane_tile(k):
        return pl.ds(k * 128, 128)

    lane = lax.broadcasted_iota(jnp.int32, (16, 128), 1)
    line = lax.broadcasted_iota(jnp.int32, (16, 128), 0)
    for load in loads:
        load.wait()

    @pl.loop(0, REGION // 16)
    def _(i):
        rows = pl.ds(pl.multiple_of(i * 16, 16), 16)
        for q in range(2):
            for a in range(2):
                here, there = w_ref[q, rows, lane_tile(a)].astype(F32), w_ref[q, rows, lane_tile(a + 8)].astype(F32)
                w_ref[q, rows, lane_tile(a)] = jnp.where(lane + 128 * a >= c0, here, there).astype(BF16)

    @pl.loop(0, 16)
    def _(i):
        k = pl.multiple_of(i * 16, 16)
        for q in range(2):
            for a in range(8):
                here = w_ref[q, pl.ds(k, 16), lane_tile(a)].astype(F32)
                there = w_ref[q, pl.ds(k + N, 16), lane_tile(a)].astype(F32)
                w_ref[q, pl.ds(k, 16), lane_tile(a)] = jnp.where(line + k >= r0, here, there).astype(BF16)

    @pl.loop(0, N // RB)
    def _(rb):
        @pl.loop(0, RB // 16)
        def _(i):
            rows = pl.ds(pl.multiple_of(rb * RB + i * 16, 16), 16)
            sub = pl.ds(pl.multiple_of(i * 16, 16), 16)
            x = []
            for a in range(8):
                pr, pi = p_ref[0, rows, lane_tile(a)].astype(F32), p_ref[1, rows, lane_tile(a)].astype(F32)
                wr, wi = w_ref[0, rows, lane_tile(a)].astype(F32), w_ref[1, rows, lane_tile(a)].astype(F32)
                x.append((pr * wr - pi * wi, pr * wi + pi * wr))
            for c, (yr, yi) in enumerate(fft8(x, 1)):
                if c > 0:
                    tr, ti = twl_ref[0, c], twl_ref[1, c]
                    yr, yi = yr * tr - yi * ti, yr * ti + yi * tr
                (hr, lr), (hi, li) = split(yr), split(yi)
                s_ref[c, sub, 0:128] = hr
                s_ref[c, sub, 128:256] = hi
                s_ref[c, sub, 256:384] = lr
                s_ref[c, sub, 384:512] = li

        rows = pl.ds(pl.multiple_of(rb * RB, RB), RB)
        for c in range(8):
            acc = dot(s_ref[c], li_ref[0:512]) + dot(s_ref[c, :, 0:256], li_ref[512:768])
            a_ref[0, rows, lane_tile(c)] = acc[:, 0:128]
            a_ref[1, rows, lane_tile(c)] = acc[:, 128:256]

    amp_load.wait()

    @pl.loop(0, N // CB)
    def _(cb):
        def lanes(h):
            return pl.ds(pl.multiple_of(cb * CB + h * 128, 128), 128)

        @pl.loop(0, 8)
        def _(i):
            b = pl.multiple_of(i * 16, 16)
            for h in range(CB // 128):
                hs = pl.ds(h * 128, 128)
                x = [tuple(a_ref[q, pl.ds(a * 128 + b, 16), lanes(h)] for q in range(2)) for a in range(8)]
                for c, (yr, yi) in enumerate(fft8(x, 1)):
                    if c > 0:
                        tr, ti = twr_ref[0, c, pl.ds(b, 16)], twr_ref[1, c, pl.ds(b, 16)]
                        yr, yi = yr * tr - yi * ti, yr * ti + yi * tr
                    (hr, lr), (hi, li) = split(yr), split(yi)
                    s2_ref[c, pl.ds(b, 16), hs] = hr
                    s2_ref[c, pl.ds(128 + b, 16), hs] = hi
                    s2_ref[c, pl.ds(256 + b, 16), hs] = lr
                    s2_ref[c, pl.ds(384 + b, 16), hs] = li

        wide = pl.ds(pl.multiple_of(cb * CB, CB), CB)
        for c in range(8):
            acc = dot(ri_ref[:, 0:512], s2_ref[c]) + dot(ri_ref[:, 512:768], s2_ref[c, 0:256])
            ir, ii = acc[0:128], acc[128:256]
            amp = amp_ref[pl.ds(c * 128, 128), wide].astype(F32)
            keep = 1.0 - amp * lax.rsqrt(jnp.maximum(ir * ir + ii * ii, FLOOR2))
            (hr, lr), (hi, li) = split(ir * keep), split(ii * keep)
            s3 = jnp.concatenate([hr, hi, lr, li], axis=0)
            acc = dot(rf_ref[:, 0:512], s3) + dot(rf_ref[:, 512:768], s3[0:256])
            z2_ref[c] = acc

        @pl.loop(0, 16)
        def _(i):
            b = pl.multiple_of(i * 8, 8)
            for h in range(CB // 128):
                hs = pl.ds(h * 128, 128)
                x = []
                for c in range(8):
                    zr, zi = z2_ref[c, pl.ds(b, 8), hs], z2_ref[c, pl.ds(128 + b, 8), hs]
                    if c > 0:
                        tr, ti = twr_ref[0, c, pl.ds(b, 8)], twr_ref[1, c, pl.ds(b, 8)]
                        zr, zi = zr * tr + zi * ti, zi * tr - zr * ti
                    x.append((zr, zi))
                for a, (yr, yi) in enumerate(fft8(x, -1)):
                    a_ref[0, pl.ds(a * 128 + b, 8), lanes(h)] = yr
                    a_ref[1, pl.ds(a * 128 + b, 8), lanes(h)] = yi

    back = jnp.bitwise_and(N - c0, N - 1)

    @pl.loop(0, N // RB)
    def _(rb):
        rows = pl.ds(pl.multiple_of(rb * RB, RB), RB)
        for c in range(8):
            (hr, lr), (hi, li) = split(a_ref[0, rows, lane_tile(c)]), split(a_ref[1, rows, lane_tile(c)])
            h = jnp.concatenate([hr, hi], axis=1)
            acc = dot(h, lf_ref[0:256]) + dot(jnp.concatenate([lr, li], axis=1), lf_ref[256:512])
            z_ref[c] = acc + dot(h, lf_ref[512:768])

        @pl.loop(0, RB // 16)
        def _(i):
            rows = pl.ds(pl.multiple_of(rb * RB + i * 16, 16), 16)
            sub = pl.ds(pl.multiple_of(i * 16, 16), 16)
            x = []
            for c in range(8):
                zr, zi = z_ref[c, sub, 0:128], z_ref[c, sub, 128:256]
                if c > 0:
                    tr, ti = twl_ref[0, c], twl_ref[1, c]
                    zr, zi = zr * tr + zi * ti, zi * tr - zr * ti
                x.append((zr, zi))
            for a, (sr, si) in enumerate(fft8(x, -1)):
                pr, pi = p_ref[0, rows, lane_tile(a)].astype(F32), p_ref[1, rows, lane_tile(a)].astype(F32)
                wr, wi = w_ref[0, rows, lane_tile(a)].astype(F32), w_ref[1, rows, lane_tile(a)].astype(F32)
                w_ref[0, rows, lane_tile(a)] = (pr * sr + pi * si).astype(BF16)
                w_ref[1, rows, lane_tile(a)] = (pr * si - pi * sr).astype(BF16)
                a_ref[0, rows, lane_tile(a)] = (wr * sr + wi * si) * (1.0 / 256)
                a_ref[1, rows, lane_tile(a)] = (wr * si - wi * sr) * (1.0 / 256)
            for q in range(2):
                a_ref[q, rows, :] = pltpu.roll(a_ref[q, rows, :], back, 1)

    @pl.loop(0, N // 16)
    def _(i):
        rows = pl.ds(pl.multiple_of(i * 16, 16), 16)
        for q in range(2):
            for a in range(2):
                x = w_ref[q, rows, lane_tile(a)].astype(F32)
                ahead = lane + 128 * a >= c0
                w_ref[q, rows, lane_tile(a)] = jnp.where(ahead, x, 0.0).astype(BF16)
                w_ref[q, rows, lane_tile(a + 8)] = jnp.where(ahead, 0.0, x).astype(BF16)

    @pl.loop(0, 16)
    def _(i):
        k = pl.multiple_of(i * 16, 16)
        for q in range(2):
            for a in range(10):
                x = w_ref[q, pl.ds(k, 16), lane_tile(a)].astype(F32)
                ahead = line + k >= r0
                w_ref[q, pl.ds(k, 16), lane_tile(a)] = jnp.where(ahead, x, 0.0).astype(BF16)
                w_ref[q, pl.ds(k + N, 16), lane_tile(a)] = jnp.where(ahead, 0.0, x).astype(BF16)

    results = (oc_ref, ol_ref, or_ref, ov_ref, ovl_ref, ovr_ref, oi_ref, oil_ref, oir_ref)
    stores = [pltpu.make_async_copy(x, y, out_sem.at[k]) for k, (x, y) in enumerate(zip(places, results))]
    for store in stores:
        store.start()

    a_ref[:, N:N + 256, :] = a_ref[:, 0:256, :]
    shift = jnp.bitwise_and(r0, 7)
    base = r0 - shift
    up = jnp.bitwise_and(8 - shift, 7)
    inside = lax.broadcasted_iota(jnp.int32, (8, N), 0) < 8 - shift
    for s, (out_ref, bit) in enumerate(((other_ref, 1 - core), (mine_ref, core))):
        @pl.loop(0, 8)
        def _(i):
            u = jnp.right_shift(i, 1) * 256 + bit * 128 + jnp.bitwise_and(i, 1) * 64
            start = pl.multiple_of(u + base, 8)
            for q in range(2):
                to = pl.multiple_of(q * 512 + i * 64, 64)
                turned = [pltpu.roll(a_ref[q, pl.ds(start + 8 * j, 8), :], up, 0) for j in range(9)]
                for j in range(8):
                    t_ref[s, pl.ds(to + 8 * j, 8), :] = jnp.where(inside, turned[j], turned[j + 1])

        store = pltpu.make_async_copy(t_ref.at[s], out_ref, out_sem.at[9 + s])
        store.start()
        stores.append(store)
    for store in stores:
        store.wait()


def led(pos, pieces, p, amp, tb):
    vm = pl.BlockSpec(memory_space=pltpu.VMEM)
    hbm = pl.BlockSpec(memory_space=pl.ANY)

    def rims(rows):
        return [jax.ShapeDtypeStruct((2, rows, cols), BF16) for cols in (TILE, RIM, RIM)]

    return pl.pallas_call(
        led_body,
        out_shape=rims(TILE) + rims(RIM) + rims(RIM) + [jax.ShapeDtypeStruct((N, N), F32)] * 2,
        in_specs=[pl.BlockSpec(memory_space=pltpu.SMEM)] + [hbm] * 11 + [vm] * 6,
        out_specs=[hbm] * 11,
        scratch_shapes=[
            pltpu.VMEM((2, REGION, REGION), BF16),
            pltpu.VMEM((2, N, N), BF16),
            pltpu.VMEM((N, N), BF16),
            pltpu.VMEM((2, N + 264, N), F32),
            pltpu.VMEM((8, RB, 512), BF16),
            pltpu.VMEM((8, 512, CB), BF16),
            pltpu.VMEM((8, RB, 256), F32),
            pltpu.VMEM((8, 256, CB), F32),
            pltpu.VMEM((2, N, N), F32),
            pltpu.SemaphoreType.DMA((11,)),
            pltpu.SemaphoreType.DMA((11,)),
        ],
        compiler_params=pltpu.CompilerParams(vmem_limit_bytes=60 * 2**20),
        cost_estimate=pl.CostEstimate(flops=13 * 10**9, bytes_accessed=30 * 2**20, transcendentals=N * N),
        name="led",
    )(pos, *pieces, p, amp, tb["lane_inv"], tb["lane_fwd"], tb["row_inv"], tb["row_fwd"], tb["tw_lane"], tb["tw_row"])


def turn_body(pos_ref, p_ref, po_ref, x_ref):
    r0, c0 = pos_ref[0], pos_ref[1]

    @pl.loop(0, N // 16)
    def _(i):
        u = pl.multiple_of(i * 16, 16)
        for q in range(2):
            x_ref[q, pl.ds(u + 256, 16), :] = pltpu.roll(p_ref[q, pl.ds(u, 16), :].astype(F32), c0, 1)

    x_ref[:, 0:256, :] = x_ref[:, N:N + 256, :]
    start = 256 - r0
    shift = jnp.bitwise_and(start, 7)
    base = start - shift
    up = jnp.bitwise_and(8 - shift, 7)
    inside = lax.broadcasted_iota(jnp.int32, (8, N), 0) < 8 - shift

    @pl.loop(0, N // 64)
    def _(i):
        u = pl.multiple_of(i * 64, 64)
        first = pl.multiple_of(u + base, 8)
        for q in range(2):
            turned = [pltpu.roll(x_ref[q, pl.ds(first + 8 * j, 8), :], up, 0) for j in range(9)]
            rows = [jnp.where(inside, turned[j], turned[j + 1]) for j in range(8)]
            po_ref[q, pl.ds(u, 64), :] = jnp.concatenate(rows, axis=0).astype(BF16)


def turn(pos, pupil):
    vm = pl.BlockSpec(memory_space=pltpu.VMEM)
    return pl.pallas_call(
        turn_body,
        out_shape=jax.ShapeDtypeStruct((2, N, N), BF16),
        in_specs=[pl.BlockSpec(memory_space=pltpu.SMEM), vm],
        out_specs=vm,
        scratch_shapes=[pltpu.VMEM((2, N + 264, N), F32)],
        compiler_params=pltpu.CompilerParams(vmem_limit_bytes=40 * 2**20),
        cost_estimate=pl.CostEstimate(flops=N**3, bytes_accessed=24 * 2**20, transcendentals=0),
        name="turn",
    )(pos, pupil)


def order_body(pos_ref, amp_ref, perm_ref, spec_ref, ao_ref, v_ref, vl_ref, vr_ref, i_ref, sem):
    core = pos_ref[2]
    gap = TILE - RIM
    outer = pl.multiple_of(core * gap, 128)
    inner = pl.multiple_of((1 - core) * gap, 128)
    ends = ((v_ref, outer, 0, TILE), (vl_ref, outer, gap, RIM), (vr_ref, outer, 0, RIM), (i_ref, inner, 0, TILE))
    copies = [
        pltpu.make_async_copy(spec_ref.at[:, pl.ds(row, RIM), pl.ds(col, wide)], out, sem.at[k])
        for k, (out, row, col, wide) in enumerate(ends)
    ]
    for copy in copies:
        copy.start()
    for i in range(4):
        part = dot(perm_ref[i * 256:(i + 1) * 256, :], amp_ref[...]).astype(BF16)
        part = lax.dot_general(part, perm_ref[...], (((1,), (1,)), ((), ())), preferred_element_type=F32)
        ao_ref[i * 256:(i + 1) * 256, :] = part.astype(BF16)
    for copy in copies:
        copy.wait()


def order(pos, amplitude, perm, spectrum):
    vm = pl.BlockSpec(memory_space=pltpu.VMEM)
    hbm = pl.BlockSpec(memory_space=pl.ANY)
    ends = [jax.ShapeDtypeStruct((2, RIM, wide), BF16) for wide in (TILE, RIM, RIM, TILE)]
    return pl.pallas_call(
        order_body,
        out_shape=[jax.ShapeDtypeStruct((N, N), BF16)] + ends,
        in_specs=[pl.BlockSpec(memory_space=pltpu.SMEM), vm, vm, hbm],
        out_specs=[vm] + [hbm] * 4,
        scratch_shapes=[pltpu.SemaphoreType.DMA((4,))],
        compiler_params=pltpu.CompilerParams(vmem_limit_bytes=40 * 2**20),
        cost_estimate=pl.CostEstimate(flops=4 * N**3, bytes_accessed=12 * 2**20, transcendentals=0),
        name="order",
    )(pos, amplitude, perm, spectrum)


def sides_body(pos_ref, l_ref, r_ref, il_ref, ir_ref, ol_ref, or_ref):
    at = (1 - pos_ref[2]) * (TILE - RIM)
    for mid_ref, add_ref, out_ref in ((l_ref, il_ref, ol_ref), (r_ref, ir_ref, or_ref)):
        out_ref[...] = mid_ref[...]

        @pl.loop(0, RIM // 32)
        def _(i):
            src = pl.ds(pl.multiple_of(i * 32, 32), 32)
            dst = pl.ds(pl.multiple_of(at + i * 32, 32), 32)
            for q in range(2):
                out_ref[q, dst, :] = (mid_ref[q, dst, :].astype(F32) + add_ref[q, src, :].astype(F32)).astype(BF16)


def sides(pos, l, r, il, ir):
    vm = pl.BlockSpec(memory_space=pltpu.VMEM)
    return pl.pallas_call(
        sides_body,
        out_shape=[jax.ShapeDtypeStruct(l.shape, BF16)] * 2,
        in_specs=[pl.BlockSpec(memory_space=pltpu.SMEM)] + [vm] * 4,
        out_specs=[vm] * 2,
        compiler_params=pltpu.CompilerParams(vmem_limit_bytes=32 * 2**20),
        cost_estimate=pl.CostEstimate(flops=2**20, bytes_accessed=6 * 2**20, transcendentals=0),
        name="sides",
    )(pos, l, r, il, ir)


def tile_body(pos_ref, c_ref, i_ref, v_ref, l_ref, r_ref, vl_ref, vr_ref, out_ref):
    core = pos_ref[2]
    gap = TILE - RIM
    out_ref[...] = c_ref[...].astype(F32)
    out_ref[0, :, gap:] += l_ref[0].astype(F32)
    out_ref[0, :, :RIM] += r_ref[0].astype(F32)
    at_i = (1 - core) * gap
    at_v = core * gap

    @pl.loop(0, RIM // 32)
    def _(i):
        src = pl.ds(pl.multiple_of(i * 32, 32), 32)
        out_ref[0, pl.ds(pl.multiple_of(at_i + i * 32, 32), 32), :] += i_ref[0, src, :].astype(F32)
        dst = pl.ds(pl.multiple_of(at_v + i * 32, 32), 32)
        out_ref[0, dst, :] += v_ref[0, src, :].astype(F32)
        out_ref[0, dst, gap:] += vl_ref[0, src, :].astype(F32)
        out_ref[0, dst, :RIM] += vr_ref[0, src, :].astype(F32)


def tile_sum(pos, parts):
    def block(x):
        return pl.BlockSpec((1,) + x.shape[1:], lambda q: (q, 0, 0))

    return pl.pallas_call(
        tile_body,
        grid=(2,),
        out_shape=jax.ShapeDtypeStruct((2, TILE, TILE), F32),
        in_specs=[pl.BlockSpec(memory_space=pltpu.SMEM)] + [block(x) for x in parts],
        out_specs=pl.BlockSpec((1, TILE, TILE), lambda q: (q, 0, 0)),
        compiler_params=pltpu.CompilerParams(vmem_limit_bytes=32 * 2**20),
        cost_estimate=pl.CostEstimate(flops=2**21, bytes_accessed=8 * 2**20, transcendentals=0),
        name="tile_sum",
    )(pos, *parts)


CUT = 640


def pair_body(mine_ref, other_ref, token_ref, a_ref, b_ref):
    total = mine_ref[...] + other_ref[...]
    a_ref[...] = total[:, :CUT].astype(BF16)
    for z in range(8):
        b_ref[z, 0] = total[z * 16:(z + 1) * 16, CUT:].astype(BF16)


def pair_sum(mine, other, token):
    rows = pl.BlockSpec((128, N), lambda i: (i, 0))
    return pl.pallas_call(
        pair_body,
        grid=(8,),
        out_shape=[jax.ShapeDtypeStruct((N, CUT), BF16), jax.ShapeDtypeStruct((8, 8, 16, N - CUT), BF16)],
        in_specs=[rows, rows, pl.BlockSpec(memory_space=pl.ANY)],
        out_specs=[pl.BlockSpec((128, CUT), lambda i: (i, 0)), pl.BlockSpec((8, 1, 16, N - CUT), lambda i: (0, i, 0, 0))],
        cost_estimate=pl.CostEstimate(flops=N * N, bytes_accessed=10 * 2**20, transcendentals=0),
        name="pair_sum",
    )(mine, other, token)


KY, KX = ("x", "yh", "core"), ("z", "yl")
ALL = KY + KX


def chain(n):
    up = [(i, i + 1) for i in range(n - 1)]
    return up, [(j, i) for i, j in up]


def between_chips(n):
    return [(i, i + 1) for i in range(1, n - 1, 2)] + [(i, i - 1) for i in range(2, n, 2)]


def both(rows, cols, n_cols):
    return [(a * n_cols + b, c * n_cols + d) for a, c in rows for b, d in cols]


def body(spectrum, pupil, amplitude, offsets):
    tb = {k: jnp.asarray(v) for k, v in tables().items()}
    n_ky, n_kx = lax.axis_size(KY), lax.axis_size(KX)
    iy, ix, core = lax.axis_index(KY), lax.axis_index(KX), lax.axis_index("core")
    first = core == 0
    r0 = offsets[0, 0, 0] - (iy * TILE - RIM)
    c0 = offsets[0, 0, 1] - (ix * TILE - RIM)
    pos = jnp.stack([r0, c0, core])
    right, left = chain(n_kx)
    vert = between_chips(n_ky)
    vert_l, vert_r = both(vert, left, n_kx), both(vert, right, n_kx)
    swap = [(0, 1), (1, 0)]

    in_l = lax.ppermute(spectrum[:, :, TILE - RIM:], KX, right)
    in_r = lax.ppermute(spectrum[:, :, :RIM], KX, left)
    amp, out_v, out_vl, out_vr, out_i = order(pos, amplitude, tb["perm"], spectrum)
    in_v = lax.ppermute(out_v, KY, vert)
    in_vl = lax.ppermute(out_vl, ALL, vert_r)
    in_vr = lax.ppermute(out_vr, ALL, vert_l)
    in_i = lax.ppermute(out_i, "core", swap)
    pupil = turn(pos, pupil)
    in_il = lax.ppermute(jnp.where(first, in_l[:, TILE - RIM:], in_l[:, :RIM]), "core", swap)
    in_ir = lax.ppermute(jnp.where(first, in_r[:, TILE - RIM:], in_r[:, :RIM]), "core", swap)
    pieces = (spectrum, in_l, in_r, in_v, in_vl, in_vr, in_i, in_il, in_ir)
    c, l, r, v, vl, vr, i, il, ir, mine, other = led(pos, pieces, pupil, amp, tb)

    il = lax.ppermute(il, "core", swap)
    ir = lax.ppermute(ir, "core", swap)
    v = lax.ppermute(v, KY, vert)
    vl = lax.ppermute(vl, ALL, vert_l)
    vr = lax.ppermute(vr, ALL, vert_r)
    i = lax.ppermute(i, "core", swap)
    other = lax.ppermute(other, "core", swap)
    l, r = sides(pos, l, r, il, ir)
    part_a, part_b = pair_sum(mine, other, l)
    l = lax.ppermute(l, KX, left)
    r = lax.ppermute(r, KX, right)

    part_a = lax.all_to_all(part_a.reshape(4, N // 4, CUT), "x", 0, 0)
    part_b = lax.all_to_all(part_b.reshape(8, N // 8, N - CUT), "z", 0, 0)
    part_a = jnp.sum(part_a.astype(F32), axis=0).reshape(2, 8, 16, CUT).transpose(1, 0, 2, 3).reshape(8, 32, CUT)
    part_b = jnp.sum(part_b.astype(F32), axis=0).reshape(4, 32, N - CUT)
    part_a = jnp.sum(lax.all_to_all(part_a, "z", 0, 0), axis=0)
    part_b = jnp.sum(lax.all_to_all(part_b, "x", 0, 0), axis=0)
    rest = jnp.concatenate([part_a, part_b], axis=1).reshape(4, 8, N)
    pupil_grad = jnp.sum(lax.all_to_all(rest, ("yh", "yl"), 0, 0), axis=0).reshape(-1)
    return tile_sum(pos, (c, i, v, l, r, vl, vr)), pupil_grad


def solution(mesh):
    fine = Mesh(mesh.devices.reshape(4, 2, 2, 8, 2), ALL)
    return jax.shard_map(
        body,
        mesh=fine,
        in_specs=(P(None, KY, KX), P(), P(KY, KX), P(KY, KX, None)),
        out_specs=(P(None, KY, KX), P(ALL)),
        check_vma=False,
    )
```

time: 802 us -> 296 us (0.37)
  waiting for transfers between devices: 396 us -> 87 us
  local copies, waits for them, and re-layouts: 193 us -> 20.9 us
  matrix products: 86.5 us -> 0 us
  Pallas kernels: 0 us -> 78.2 us
  other arithmetic: 75.7 us -> 6.47 us
  starting transfers between devices: 24.8 us -> 64.2 us
  blocking collectives: 0 us -> 31.7 us
  between operations: 16.3 us -> 2.22 us
    unnamed x2 -> x0, waiting for transfers between devices: 296 us -> none
    dot_general x8 -> x0, matrix products: 86.5 us -> none  [complex_section(): jnp.einsum(full_form, stacked, table, precision=lax.Precision.HIGHEST)]
    convert_element_type x3 -> x0, local copies, waits for them, and re-layouts: 82.2 us -> none  [body(): measured = amplitude.reshape(size_b, size_a, size_b, size_a).transpose(1,...]
    pallas_call x0 -> x6, Pallas kernels: none -> 78.2 us  [the longest x1 54.1 us: led(): pl.pallas_call(led_body, out_shape=rims(TILE) + rims(RIM) + rims(RIM) + [...]
    dynamic_update_slice x1 -> x0, local copies, waits for them, and re-layouts: 45.4 us -> none  [body(): lax.dynamic_update_slice(frame, jnp.stack([grad_real, grad_imag]), (zero_...]
    ppermute x8 -> x17, waiting for transfers between devices: 99.2 us -> 66.6 us  [the longest x1 25.5 us: body(): in_vl = lax.ppermute(out_vl, ALL, vert_r)]
    all_to_all x0 -> x1, blocking collectives: none -> 31.7 us  [body(): part_b = lax.all_to_all(part_b.reshape(8, N // 8, N - CUT), 'z', 0, 0)]
    another operation x7 -> x0, local copies, waits for them, and re-layouts: 27.5 us -> none  [the longest x2 18 us: transform(): parts = stacked.reshape(split_shape)]
  transfers between devices with their start and end apart: 9 -> 21, of which waited for: 4 -> 9; matrix products, arithmetic and copies ran while one was open for 13% -> 3% of each run, Pallas kernels for 0% -> 6%
where the time goes in v1:
time: 296 us; the launch traced here: 291 us
  waiting for transfers between devices  87 us (29%)
  Pallas kernels  78.2 us (26%)
  starting transfers between devices  64.2 us (22%)
  blocking collectives  31.7 us (11%)
  local copies, waits for them, and re-layouts  20.9 us (7%)
  other arithmetic  6.47 us (2%)
    pallas_call x1, Pallas kernels, led(): pl.pallas_call(led_body, out_shape=rims(TILE) + rims(RIM) + rims(RIM) + [...  54.1 us
    all_to_all x1, blocking collectives, body(): part_b = lax.all_to_all(part_b.reshape(8, N // 8, N - CUT), 'z', 0, 0)  31.7 us
    ppermute x1, waiting for transfers between devices, body(): in_vl = lax.ppermute(out_vl, ALL, vert_r)  25.5 us
    unnamed x51, local copies, waits for them, and re-layouts  16.5 us
    all_to_all x1, waiting for transfers between devices, body(): part_a = lax.all_to_all(part_a.reshape(4, N // 4, CUT), 'x', 0, 0)  16.4 us
    ppermute x1, starting transfers between devices, body(): vr = lax.ppermute(vr, ALL, vert_r)  16 us
    ppermute x1, waiting for transfers between devices, body(): in_l = lax.ppermute(spectrum[:, :, TILE - RIM:], KX, right)  10.8 us
    ppermute x1, waiting for transfers between devices, body(): vr = lax.ppermute(vr, ALL, vert_r)  8.05 us
  transfers between devices with their start and end apart: 21, of which 9 were waited for; matrix products, arithmetic and copies ran while one was open for 3% of the time, Pallas kernels for 6%

profile of v1, /device:TPU:1, one launch (start us, length us, event | category | flops | bytes accessed | tf_op | source)
XLA Modules:
  0.0 290.8 jit_solution(10724029518122440664)
XLA Ops:
  0.6 0.0 copy-start.2
  0.7 2.9 fusion
  3.5 1.3 collective-permute-start.1
  4.8 5.6 %collective-permute-start = (bf16[2,512,384]{2,1,0:T(8,128)(2,1)}, bf16[2,512,384]{2,1,0:T(8,128)(2,1)}, u32[]{:S(2)}, u32[]{:S(2)}) collective-permute-start(bf16[2,512,384]{2,1,0:T(8,128)(2,1)} %get-tuple-element.43), channel_id=1, source_target_pairs={{0,1},{1,2},{2,3},{3,4},{4,5},{5,6},{6,7},{7,8},{8,9},{9,10},{10,1... | collective-permute-start | bytes 2359304 | tf_op jit(solution)/shard_map/ppermute | solution.py:516
  10.4 0.6 fusion.1
  12.3 0.1 pad_add_fusion.pos_ref
  12.4 1.6 copy-done.15
  14.0 5.2 %order.1 = (bf16[1024,1024]{1,0:T(8,128)(2,1)S(1)}, bf16[2,384,512]{2,1,0:T(8,128)(2,1)}, bf16[2,384,384]{2,1,0:T(8,128)(2,1)}, bf16[2,384,384]{2,1,0:T(8,128)(2,1)}, bf16[2,384,512]{2,1,0:T(8,128)(2,1)S(1)}) custom-call(s32[3]{0:T(128)S(1)} %pad_add_fusion.pos_ref, bf16[1024,1024]{1,0:T(8,128)(2,1)S(1)} %copy-done.12, bf16[1024,1024]{1,0:T(8,128)(2,1)S(1)} %copy-done.15, ...), custom_call_target="tpu_custom_call" | custom-call | flops 4294967296 | bytes 12582912 | tf_op jit(solution)/shard_map/order/pallas_call | solution.py:390
  19.2 0.9 copy-done.14
  20.1 1.3 copy-done.16
  21.4 6.0 %collective-permute-start.3 = (bf16[2,384,384]{2,1,0:T(8,128)(2,1)}, bf16[2,384,384]{2,1,0:T(8,128)(2,1)S(1)}, u32[]{:S(2)}, u32[]{:S(2)}) collective-permute-start(bf16[2,384,384]{2,1,0:T(8,128)(2,1)} %get-tuple-element.23), channel_id=1, source_target_pairs={{16,33},{17,34},{18,35},{19,36},{20,37},{21,38},{22,39},{23,40},{2... | collective-permute-start | bytes 1769480 | tf_op jit(solution)/shard_map/ppermute | solution.py:520
  27.3 1.3 collective-permute-start.4
  28.6 1.9 collective-permute-start.2
  30.6 0.0 collective-permute-done.1.r_ref
  30.6 0.1 collective-permute-start.5
  30.7 1.4 slice_select_fusion
  32.1 10.8 %collective-permute-done.l_ref = bf16[2,512,384]{2,1,0:T(8,128)(2,1)} collective-permute-done((bf16[2,512,384]{2,1,0:T(8,128)(2,1)}, bf16[2,512,384]{2,1,0:T(8,128)(2,1)}, u32[]{:S(2)}, u32[]{:S(2)}) %collective-permute-start) | collective-permute-done | bytes 786464 | tf_op jit(solution)/shard_map/ppermute | solution.py:516
  42.9 0.6 collective-permute-start.7
  43.5 1.3 slice_select_fusion.1
  44.8 25.5 %collective-permute-done.3.vl_ref = bf16[2,384,384]{2,1,0:T(8,128)(2,1)S(1)} collective-permute-done((bf16[2,384,384]{2,1,0:T(8,128)(2,1)}, bf16[2,384,384]{2,1,0:T(8,128)(2,1)S(1)}, u32[]{:S(2)}, u32[]{:S(2)}) %collective-permute-start.3) | collective-permute-done | bytes 589856 | tf_op jit(solution)/shard_map/ppermute | solution.py:520
  70.2 0.0 collective-permute-start.6
  70.3 2.4 copy-done
  72.6 7.7 %turn.1.pup_ref = bf16[2,1024,1024]{2,1,0:T(8,128)(2,1)S(1)} custom-call(s32[3]{0:T(128)S(1)} %pad_add_fusion.pos_ref, bf16[2,1024,1024]{2,1,0:T(8,128)(2,1)S(1)} %copy-done), custom_call_target="tpu_custom_call" | custom-call | flops 1073741824 | bytes 25165824 | tf_op jit(solution)/shard_map/turn/pallas_call | solution.py:354
  80.4 2.0 copy-done.1
  82.5 0.9 copy-done.23
  83.4 0.8 copy-done.24
  84.2 54.1 %led.1 = (bf16[2,512,512]{2,1,0:T(8,128)(2,1)}, bf16[2,512,384]{2,1,0:T(8,128)(2,1)}, bf16[2,512,384]{2,1,0:T(8,128)(2,1)}, bf16[2,384,512]{2,1,0:T(8,128)(2,1)}...) custom-call(s32[3]{0:T(128)} %copy-done.10, ...), custom_call_target="tpu_custom_call" | custom-call | flops 12999999488 | bytes 31457280 | tf_op jit(solution)/shard_map/led/pallas_call | solution.py:302
  138.3 0.4 collective-permute-start.16
  138.7 0.2 collective-permute-start.10
  138.9 0.3 collective-permute-start.11
  139.2 5.2 %collective-permute-done.10.il_ref = bf16[2,384,384]{2,1,0:T(8,128)(2,1)S(1)} collective-permute-done((bf16[2,384,384]{2,1,0:T(8,128)(2,1)}, bf16[2,384,384]{2,1,0:T(8,128)(2,1)S(1)}, u32[]{:S(2)}, u32[]{:S(2)}) %collective-permute-start.10) | collective-permute-done | bytes 589856 | tf_op jit(solution)/shard_map/ppermute | solution.py:529
  144.4 1.7 collective-permute-done.11.ir_ref
  146.1 1.1 copy-done.6
  147.2 1.1 copy-done.7
  148.4 1.1 sides.1
  149.5 0.9 copy-done.4
  150.4 0.9 copy-done.13
  151.3 6.9 %pair_sum.1 = (bf16[1024,640]{1,0:T(8,128)(2,1)}, bf16[8,8,16,384]{3,2,1,0:T(8,128)(2,1)}) custom-call(f32[1024,1024]{1,0:T(8,128)} %get-tuple-element.38.mine_ref, f32[1024,1024]{1,0:T(8,128)} %collective-permute-done.16.other_ref, bf16[2,512,384]{2,1,0:T(8,128)(2,1)} %copy-done.4), custom_call_target="tpu_custom_call" | custom-call | flops 1048576 | bytes 10485760 | tf_op jit(solution)/shard_map/pair_sum/pallas_call | solution.py:475
  158.2 31.7 %all_to_all.25 = bf16[8,128,384]{2,1,0:T(8,128)(2,1)S(1)} all-to-all(bf16[8,128,384]{2,1,0:T(8,128)(2,1)} %bitcast.20), channel_id=1, replica_groups=mesh['x'=4,'yh'=2,'core'=2,'z'=8,'yl'=2] {'z'}, dimensions={0} | all-to-all | bytes 1572864 | tf_op jit(solution)/shard_map/all_to_all | solution.py:542
  190.0 4.0 %all-to-all-start = ((bf16[4,256,640]{2,1,0:T(8,128)(2,1)}), bf16[4,256,640]{2,1,0:T(8,128)(2,1)S(1)}, u32[]{:S(2)}, u32[]{:S(2)}) async-start(bf16[4,256,640]{2,1,0:T(8,128)(2,1)} %bitcast.19), calls=%async_computation | async-start | bytes 2621440 | tf_op jit(solution)/shard_map/all_to_all | solution.py:541
  193.9 0.8 convert_reduce_fusion.1
  194.7 16.4 %all-to-all-done = bf16[4,256,640]{2,1,0:T(8,128)(2,1)S(1)} async-done(((bf16[4,256,640]{2,1,0:T(8,128)(2,1)}), bf16[4,256,640]{2,1,0:T(8,128)(2,1)S(1)}, u32[]{:S(2)}, u32[]{:S(2)}) %all-to-all-start) | async-done | bytes 1310752 | tf_op jit(solution)/shard_map/all_to_all | solution.py:541
  211.1 3.4 %all-to-all-start.3 = ((f32[4,32,384]{2,1,0:T(8,128)}), f32[4,32,384]{2,1,0:T(8,128)S(1)}, u32[]{:S(2)}, u32[]{:S(2)}) async-start(f32[4,32,384]{2,1,0:T(8,128)} %bitcast.10), calls=%async_computation.3 | async-start | bytes 393216 | tf_op jit(solution)/shard_map/all_to_all | solution.py:546
  214.5 0.2 convert_reduce_fusion
  214.7 0.9 copy.14
  215.5 4.0 %all-to-all-done.3 = f32[4,32,384]{2,1,0:T(8,128)S(1)} async-done(((f32[4,32,384]{2,1,0:T(8,128)}), f32[4,32,384]{2,1,0:T(8,128)S(1)}, u32[]{:S(2)}, u32[]{:S(2)}) %all-to-all-start.3) | async-done | bytes 196640 | tf_op jit(solution)/shard_map/all_to_all | solution.py:546
  219.6 4.2 %all-to-all-start.1 = ((f32[8,32,640]{2,1,0:T(8,128)}), f32[8,32,640]{2,1,0:T(8,128)}, u32[]{:S(2)}, u32[]{:S(2)}) async-start(f32[8,32,640]{2,1,0:T(8,128)} %bitcast.8), calls=%async_computation.1 | async-start | bytes 1310720 | tf_op jit(solution)/shard_map/all_to_all | solution.py:545
  223.8 1.3 collective-permute-start.14
  225.1 2.4 collective-permute-start.8
  227.5 1.9 collective-permute-start.9
  229.4 7.5 %collective-permute-start.13 = (bf16[2,512,384]{2,1,0:T(8,128)(2,1)}, bf16[2,512,384]{2,1,0:T(8,128)(2,1)}, u32[]{:S(2)}, u32[]{:S(2)}) collective-permute-start(bf16[2,512,384]{2,1,0:T(8,128)(2,1)} %copy-done.13), channel_id=1, source_target_pairs={{0,1},{1,2},{2,3},{3,4},{4,5},{5,6},{6,7},{7,8},{8,9},{9,10},{10,1... | collective-permute-start | bytes 2359304 | tf_op jit(solution)/shard_map/ppermute | solution.py:539
  236.9 1.3 collective-permute-start.12
  238.2 7.7 %collective-permute-done.14.vl_ref = bf16[2,384,384]{2,1,0:T(8,128)(2,1)S(1)} collective-permute-done((bf16[2,384,384]{2,1,0:T(8,128)(2,1)}, bf16[2,384,384]{2,1,0:T(8,128)(2,1)S(1)}, u32[]{:S(2)}, u32[]{:S(2)}) %collective-permute-start.14) | collective-permute-done | bytes 589856 | tf_op jit(solution)/shard_map/ppermute | solution.py:532
  245.9 0.8 copy-done.8
  246.7 16.0 %collective-permute-start.15 = (bf16[2,384,384]{2,1,0:T(8,128)(2,1)}, bf16[2,384,384]{2,1,0:T(8,128)(2,1)}, u32[]{:S(2)}, u32[]{:S(2)}) collective-permute-start(bf16[2,384,384]{2,1,0:T(8,128)(2,1)} %get-tuple-element.37), channel_id=1, source_target_pairs={{16,33},{17,34},{18,35},{19,36},{20,37},{21,38},{22,39},{23,40},{2... | collective-permute-start | bytes 1769480 | tf_op jit(solution)/shard_map/ppermute | solution.py:533
  262.8 0.9 reduce_sum.48
  263.7 1.1 reduce_sum.46
  264.9 0.7 maximum_bitcast_fusion
  265.5 4.6 %all-to-all-start.4 = ((f32[4,8,1024]{2,1,0:T(8,128)}), f32[4,8,1024]{2,1,0:T(8,128)S(1)}, u32[]{:S(2)}, u32[]{:S(2)}) async-start(f32[4,8,1024]{2,1,0:T(8,128)} %maximum_bitcast_fusion), calls=%async_computation.4 | async-start | bytes 262144 | tf_op jit(solution)/shard_map/all_to_all | solution.py:548
  270.1 8.0 %collective-permute-done.15.vr_ref = bf16[2,384,384]{2,1,0:T(8,128)(2,1)} collective-permute-done((bf16[2,384,384]{2,1,0:T(8,128)(2,1)}, bf16[2,384,384]{2,1,0:T(8,128)(2,1)}, u32[]{:S(2)}, u32[]{:S(2)}) %collective-permute-start.15) | collective-permute-done | bytes 589856 | tf_op jit(solution)/shard_map/ppermute | solution.py:533
  278.2 7.6 %collective-permute-done.13.r_ref = bf16[2,512,384]{2,1,0:T(8,128)(2,1)} collective-permute-done((bf16[2,512,384]{2,1,0:T(8,128)(2,1)}, bf16[2,512,384]{2,1,0:T(8,128)(2,1)}, u32[]{:S(2)}, u32[]{:S(2)}) %collective-permute-start.13) | collective-permute-done | bytes 786464 | tf_op jit(solution)/shard_map/ppermute | solution.py:539
  285.8 1.1 copy-done.9
  286.9 3.2 %tile_sum.1 = f32[2,512,512]{2,1,0:T(8,128)} custom-call(s32[3]{0:T(128)S(1)} %copy-done.11, bf16[2,512,512]{2,1,0:T(8,128)(2,1)S(1)} %copy-done.3, bf16[2,384,512]{2,1,0:T(8,128)(2,1)S(1)} %collective-permute-done.8.i_ref, bf16[2,384,512]{2,1,0:T(8,128)(2,1)S(1)} %collective-permute-done.9.v_ref, bf16[2,512,384]{2,1,0:T(8,128)(2,1)} %collective-permute-done.12.l_ref, ...), custom_call_target="tpu_custom_call" | custom-call | flops 2097152 | bytes 8388608 | tf_op jit(solution)/shard_map/tile_sum/pallas_call | solution.py:451
  290.1 0.6 copy.17
  (48 shorter events, 0.1 us)
Async XLA Ops:
  0.6 11.8 %copy-start.2 = (bf16[2,512,512]{2,1,0:T(8,128)(2,1)S(1)}, bf16[2,512,512]{2,1,0:T(8,128)(2,1)}, u32[]{:S(2)}) copy-start(bf16[2,512,512]{2,1,0:T(8,128)(2,1)} %own_ref.1) | copy-start | bytes 3145732
  0.6 9.8 %copy-start.18 = (s32[1,1,2]{2,1,0:T(1,128)S(1)}, s32[1,1,2]{2,1,0:T(1,128)}, u32[]{:S(2)}) copy-start(s32[1,1,2]{2,1,0:T(1,128)} %param.14) | copy-start | bytes 28
  0.7 11.7 %copy-start.12 = (bf16[1024,1024]{1,0:T(8,128)(2,1)S(1)}, bf16[1024,1024]{1,0:T(8,128)(2,1)}, u32[]{:S(2)}) copy-start(bf16[1024,1024]{1,0:T(8,128)(2,1)} %amp_ref.1) | copy-start | bytes 6291460
  3.5 27.0 %collective-permute-start.1 = (bf16[2,512,384]{2,1,0:T(8,128)(2,1)}, bf16[2,512,384]{2,1,0:T(8,128)(2,1)}, u32[]{:S(2)}, u32[]{:S(2)}) collective-permute-start(bf16[2,512,384]{2,1,0:T(8,128)(2,1)} %get-tuple-element.42), channel_id=1, source_target_pairs={{1,0},{2,1},{3,2},{4,3},{5,4},{6,5},{7,6},{8,7},{9,8},{10,9},{11,1... | collective-permute-start | bytes 2359304 | tf_op jit(solution)/shard_map/ppermute | solution.py:517
  4.8 38.1 %collective-permute-start = (bf16[2,512,384]{2,1,0:T(8,128)(2,1)}, bf16[2,512,384]{2,1,0:T(8,128)(2,1)}, u32[]{:S(2)}, u32[]{:S(2)}) collective-permute-start(bf16[2,512,384]{2,1,0:T(8,128)(2,1)} %get-tuple-element.43), channel_id=1, source_target_pairs={{0,1},{1,2},{2,3},{3,4},{4,5},{5,6},{6,7},{7,8},{8,9},{9,10},{10,1... | collective-permute-start | bytes 2359304 | tf_op jit(solution)/shard_map/ppermute | solution.py:516
  12.4 1.6 copy-start.15
  14.0 56.3 %copy-start.10 = (s32[3]{0:T(128)}, s32[3]{0:T(128)S(1)}, u32[]{:S(2)}) copy-start(s32[3]{0:T(128)S(1)} %pad_add_fusion.pos_ref) | copy-start | bytes 40
  19.2 0.9 copy-start.14
  20.1 1.3 copy-start.16
  21.4 48.9 %collective-permute-start.3 = (bf16[2,384,384]{2,1,0:T(8,128)(2,1)}, bf16[2,384,384]{2,1,0:T(8,128)(2,1)S(1)}, u32[]{:S(2)}, u32[]{:S(2)}) collective-permute-start(bf16[2,384,384]{2,1,0:T(8,128)(2,1)} %get-tuple-element.23), channel_id=1, source_target_pairs={{16,33},{17,34},{18,35},{19,36},{20,37},{21,38},{22,39},{23,40},{2... | collective-permute-start | bytes 1769480 | tf_op jit(solution)/shard_map/ppermute | solution.py:520
  27.3 55.1 %collective-permute-start.4 = (bf16[2,384,384]{2,1,0:T(8,128)(2,1)}, bf16[2,384,384]{2,1,0:T(8,128)(2,1)S(1)}, u32[]{:S(2)}, u32[]{:S(2)}) collective-permute-start(bf16[2,384,384]{2,1,0:T(8,128)(2,1)} %get-tuple-element.24), channel_id=1, source_target_pairs={{17,32},{18,33},{19,34},{20,35},{21,36},{22,37},{23,38},{24,39},{2... | collective-permute-start | bytes 1769480 | tf_op jit(solution)/shard_map/ppermute | solution.py:521
  28.6 53.8 %collective-permute-start.2 = (bf16[2,384,512]{2,1,0:T(8,128)(2,1)}, bf16[2,384,512]{2,1,0:T(8,128)(2,1)S(1)}, u32[]{:S(2)}, u32[]{:S(2)}) collective-permute-start(bf16[2,384,512]{2,1,0:T(8,128)(2,1)} %get-tuple-element.22), channel_id=1, source_target_pairs={{16,32},{48,64},{80,96},{112,128},{144,160},{176,192},{208,224},{3... | collective-permute-start | bytes 2359304 | tf_op jit(solution)/shard_map/ppermute | solution.py:519
  30.6 51.9 %collective-permute-start.5 = (bf16[2,384,512]{2,1,0:T(8,128)(2,1)}, bf16[2,384,512]{2,1,0:T(8,128)(2,1)S(1)}, u32[]{:S(2)}, u32[]{:S(2)}) collective-permute-start(bf16[2,384,512]{2,1,0:T(8,128)(2,1)} %copy-done.14), channel_id=1, source_target_pairs={{0,16},{16,0},{1,17},{17,1},{2,18},{18,2},{3,19},{19,3},{4,20},{20... | collective-permute-start | bytes 2359304 | tf_op jit(solution)/shard_map/ppermute | solution.py:522
  42.9 39.6 %collective-permute-start.7 = (bf16[2,384,384]{2,1,0:T(8,128)(2,1)S(1)}, bf16[2,384,384]{2,1,0:T(8,128)(2,1)S(1)}, u32[]{:S(2)}, u32[]{:S(2)}) collective-permute-start(bf16[2,384,384]{2,1,0:T(8,128)(2,1)S(1)} %slice_select_fusion), channel_id=1, source_target_pairs={{0,16},{16,0},{1,17},{17,1},{2,18},{18,2},{3,19},{19,3},{4,20},{20... | collective-permute-start | bytes 1769480 | tf_op jit(solution)/shard_map/ppermute | solution.py:525
  70.2 10.2 %copy-start.21 = (bf16[2,384,384]{2,1,0:T(8,128)(2,1)}, bf16[2,384,384]{2,1,0:T(8,128)(2,1)S(1)}, u32[]{:S(2)}) copy-start(bf16[2,384,384]{2,1,0:T(8,128)(2,1)S(1)} %collective-permute-done.3.vl_ref) | copy-start | bytes 1769476
  70.2 12.3 %collective-permute-start.6 = (bf16[2,384,384]{2,1,0:T(8,128)(2,1)S(1)}, bf16[2,384,384]{2,1,0:T(8,128)(2,1)S(1)}, u32[]{:S(2)}, u32[]{:S(2)}) collective-permute-start(bf16[2,384,384]{2,1,0:T(8,128)(2,1)S(1)} %slice_select_fusion.1), channel_id=1, source_target_pairs={{0,16},{16,0},{1,17},{17,1},{2,18},{18,2},{3,19},{19,3},{4,20},{20... | collective-permute-start | bytes 1769480 | tf_op jit(solution)/shard_map/ppermute | solution.py:524
  70.2 2.4 copy-start
  80.4 2.0 copy-start.1
  82.4 1.8 copy-start.22
  82.4 1.8 copy-start.19
  82.5 1.8 copy-start.20
  82.5 0.9 copy-start.23
  83.4 0.8 copy-start.24
  84.2 61.9 %copy-start.11 = (s32[3]{0:T(128)S(1)}, s32[3]{0:T(128)}, u32[]{:S(2)}) copy-start(s32[3]{0:T(128)} %copy-done.10) | copy-start | bytes 40
  138.3 13.0 %collective-permute-start.16 = (f32[1024,1024]{1,0:T(8,128)}, f32[1024,1024]{1,0:T(8,128)}, u32[]{:S(2)}, u32[]{:S(2)}) collective-permute-start(f32[1024,1024]{1,0:T(8,128)} %get-tuple-element.39), channel_id=1, source_target_pairs={{0,16},{16,0},{1,17},{17,1},{2,18},{18,2},{3,19},{19,3},{4,20},{20... | collective-permute-start | bytes 12582920 | tf_op jit(solution)/shard_map/ppermute | solution.py:535
  138.7 5.7 %collective-permute-start.10 = (bf16[2,384,384]{2,1,0:T(8,128)(2,1)}, bf16[2,384,384]{2,1,0:T(8,128)(2,1)S(1)}, u32[]{:S(2)}, u32[]{:S(2)}) collective-permute-start(bf16[2,384,384]{2,1,0:T(8,128)(2,1)} %get-tuple-element.32), channel_id=1, source_target_pairs={{0,16},{16,0},{1,17},{17,1},{2,18},{18,2},{3,19},{19,3},{4,20},{20... | collective-permute-start | bytes 1769480 | tf_op jit(solution)/shard_map/ppermute | solution.py:529
  138.9 7.2 %collective-permute-start.11 = (bf16[2,384,384]{2,1,0:T(8,128)(2,1)}, bf16[2,384,384]{2,1,0:T(8,128)(2,1)S(1)}, u32[]{:S(2)}, u32[]{:S(2)}) collective-permute-start(bf16[2,384,384]{2,1,0:T(8,128)(2,1)} %get-tuple-element.33), channel_id=1, source_target_pairs={{0,16},{16,0},{1,17},{17,1},{2,18},{18,2},{3,19},{19,3},{4,20},{20... | collective-permute-start | bytes 1769480 | tf_op jit(solution)/shard_map/ppermute | solution.py:530
  146.1 1.1 copy-start.6
  147.2 1.1 copy-start.7
  149.5 0.9 copy-start.4
  150.4 0.9 copy-start.13
  190.0 21.1 %all-to-all-start = ((bf16[4,256,640]{2,1,0:T(8,128)(2,1)}), bf16[4,256,640]{2,1,0:T(8,128)(2,1)S(1)}, u32[]{:S(2)}, u32[]{:S(2)}) async-start(bf16[4,256,640]{2,1,0:T(8,128)(2,1)} %bitcast.19), calls=%async_computation | async-start | bytes 2621440 | tf_op jit(solution)/shard_map/all_to_all | solution.py:541
  211.1 8.5 %all-to-all-start.3 = ((f32[4,32,384]{2,1,0:T(8,128)}), f32[4,32,384]{2,1,0:T(8,128)S(1)}, u32[]{:S(2)}, u32[]{:S(2)}) async-start(f32[4,32,384]{2,1,0:T(8,128)} %bitcast.10), calls=%async_computation.3 | async-start | bytes 393216 | tf_op jit(solution)/shard_map/all_to_all | solution.py:546
  214.4 22.5 %copy-start.5 = (bf16[2,512,384]{2,1,0:T(8,128)(2,1)S(1)}, bf16[2,512,384]{2,1,0:T(8,128)(2,1)}, u32[]{:S(2)}) copy-start(bf16[2,512,384]{2,1,0:T(8,128)(2,1)} %copy-done.4) | copy-start | bytes 2359300
  214.6 71.2 %copy-start.3 = (bf16[2,512,512]{2,1,0:T(8,128)(2,1)S(1)}, bf16[2,512,512]{2,1,0:T(8,128)(2,1)}, u32[]{:S(2)}) copy-start(bf16[2,512,512]{2,1,0:T(8,128)(2,1)} %get-tuple-element.27.c_ref) | copy-start | bytes 3145732
  219.6 7.9 %copy-start.17 = (f32[4,32,384]{2,1,0:T(8,128)}, f32[4,32,384]{2,1,0:T(8,128)S(1)}, u32[]{:S(2)}) copy-start(f32[4,32,384]{2,1,0:T(8,128)S(1)} %all-to-all-done.3) | copy-start | bytes 589828
  219.6 44.1 %all-to-all-start.1 = ((f32[8,32,640]{2,1,0:T(8,128)}), f32[8,32,640]{2,1,0:T(8,128)}, u32[]{:S(2)}, u32[]{:S(2)}) async-start(f32[8,32,640]{2,1,0:T(8,128)} %bitcast.8), calls=%async_computation.1 | async-start | bytes 1310720 | tf_op jit(solution)/shard_map/all_to_all | solution.py:545
  223.8 22.1 %collective-permute-start.14 = (bf16[2,384,384]{2,1,0:T(8,128)(2,1)}, bf16[2,384,384]{2,1,0:T(8,128)(2,1)S(1)}, u32[]{:S(2)}, u32[]{:S(2)}) collective-permute-start(bf16[2,384,384]{2,1,0:T(8,128)(2,1)} %get-tuple-element.36), channel_id=1, source_target_pairs={{17,32},{18,33},{19,34},{20,35},{21,36},{22,37},{23,38},{24,39},{2... | collective-permute-start | bytes 1769480 | tf_op jit(solution)/shard_map/ppermute | solution.py:532
  225.1 53.1 %collective-permute-start.8 = (bf16[2,384,512]{2,1,0:T(8,128)(2,1)}, bf16[2,384,512]{2,1,0:T(8,128)(2,1)S(1)}, u32[]{:S(2)}, u32[]{:S(2)}) collective-permute-start(bf16[2,384,512]{2,1,0:T(8,128)(2,1)} %get-tuple-element.28), channel_id=1, source_target_pairs={{0,16},{16,0},{1,17},{17,1},{2,18},{18,2},{3,19},{19,3},{4,20},{20... | collective-permute-start | bytes 2359304 | tf_op jit(solution)/shard_map/ppermute | solution.py:534
  227.5 50.7 %collective-permute-start.9 = (bf16[2,384,512]{2,1,0:T(8,128)(2,1)}, bf16[2,384,512]{2,1,0:T(8,128)(2,1)S(1)}, u32[]{:S(2)}, u32[]{:S(2)}) collective-permute-start(bf16[2,384,512]{2,1,0:T(8,128)(2,1)} %get-tuple-element.29), channel_id=1, source_target_pairs={{16,32},{48,64},{80,96},{112,128},{144,160},{176,192},{208,224},{3... | collective-permute-start | bytes 2359304 | tf_op jit(solution)/shard_map/ppermute | solution.py:531
  229.4 56.4 %collective-permute-start.13 = (bf16[2,512,384]{2,1,0:T(8,128)(2,1)}, bf16[2,512,384]{2,1,0:T(8,128)(2,1)}, u32[]{:S(2)}, u32[]{:S(2)}) collective-permute-start(bf16[2,512,384]{2,1,0:T(8,128)(2,1)} %copy-done.13), channel_id=1, source_target_pairs={{0,1},{1,2},{2,3},{3,4},{4,5},{5,6},{6,7},{7,8},{8,9},{9,10},{10,1... | collective-permute-start | bytes 2359304 | tf_op jit(solution)/shard_map/ppermute | solution.py:539
  236.9 48.9 %collective-permute-start.12 = (bf16[2,512,384]{2,1,0:T(8,128)(2,1)S(1)}, bf16[2,512,384]{2,1,0:T(8,128)(2,1)}, u32[]{:S(2)}, u32[]{:S(2)}) collective-permute-start(bf16[2,512,384]{2,1,0:T(8,128)(2,1)S(1)} %copy-done.5), channel_id=1, source_target_pairs={{1,0},{2,1},{3,2},{4,3},{5,4},{6,5},{7,6},{8,7},{9,8},{10,9},{11,1... | collective-permute-start | bytes 2359304 | tf_op jit(solution)/shard_map/ppermute | solution.py:538
  245.9 0.8 copy-start.8
  246.7 31.4 %collective-permute-start.15 = (bf16[2,384,384]{2,1,0:T(8,128)(2,1)}, bf16[2,384,384]{2,1,0:T(8,128)(2,1)}, u32[]{:S(2)}, u32[]{:S(2)}) collective-permute-start(bf16[2,384,384]{2,1,0:T(8,128)(2,1)} %get-tuple-element.37), channel_id=1, source_target_pairs={{16,33},{17,34},{18,35},{19,36},{20,37},{21,38},{22,39},{23,40},{2... | collective-permute-start | bytes 1769480 | tf_op jit(solution)/shard_map/ppermute | solution.py:533
  265.5 24.6 %all-to-all-start.4 = ((f32[4,8,1024]{2,1,0:T(8,128)}), f32[4,8,1024]{2,1,0:T(8,128)S(1)}, u32[]{:S(2)}, u32[]{:S(2)}) async-start(f32[4,8,1024]{2,1,0:T(8,128)} %maximum_bitcast_fusion), calls=%async_computation.4 | async-start | bytes 262144 | tf_op jit(solution)/shard_map/all_to_all | solution.py:548
  285.8 1.1 copy-start.9

commit v2 on v1

--- a/solution.py
+++ b/solution.py
@@ -90,20 +90,24 @@
 
 
 def led_body(
-    pos_ref, own_ref, l_ref, r_ref, v_ref, vl_ref, vr_ref, i_ref, il_ref, ir_ref, pup_ref, ampl_ref,
+    pos_ref, own_ref, l_ref, r_ref, v_ref, vl_ref, vr_ref, i_ref, c_ref, pup_ref, ampl_ref,
     li_ref, lf_ref, ri_ref, rf_ref, twl_ref, twr_ref,
-    oc_ref, ol_ref, or_ref, ov_ref, ovl_ref, ovr_ref, oi_ref, oil_ref, oir_ref, mine_ref, other_ref,
-    w_ref, p_ref, amp_ref, a_ref, s_ref, s2_ref, z_ref, z2_ref, t_ref, in_sem, out_sem,
+    oc_ref, ol_ref, or_ref, ov_ref, ovl_ref, ovr_ref, oi_ref, mine_ref, other_ref,
+    w_ref, p_ref, amp_ref, a_ref, s_ref, s2_ref, z_ref, z2_ref, to_ref, tm_ref, in_sem, out_sem,
 ):
     r0, c0, core = pos_ref[0], pos_ref[1], pos_ref[2]
     outer = pl.multiple_of((RIM + TILE) * core, 128)
     inner = pl.multiple_of((RIM + TILE) * (1 - core), 128)
     places = []
-    for start, count in ((RIM, TILE), (outer, RIM), (inner, RIM)):
+    for start, count in ((RIM, TILE), (outer, RIM)):
         for col, wide in ((RIM, TILE), (0, RIM), (RIM + TILE, RIM)):
             places.append(w_ref.at[:, pl.ds(start, count), pl.ds(col, wide)])
-    arrivals = (own_ref, l_ref, r_ref, v_ref, vl_ref, vr_ref, i_ref, il_ref, ir_ref)
-    loads = [pltpu.make_async_copy(x, y, in_sem.at[k]) for k, (x, y) in enumerate(zip(arrivals, places))]
+    arrivals = [own_ref, l_ref, r_ref, v_ref, vl_ref, vr_ref]
+    arrivals.append(i_ref.at[:, pl.ds(pl.multiple_of(core * (TILE - RIM), 128), RIM), :])
+    arrivals += [c_ref.at[:, :, pl.ds(0, RIM)], c_ref.at[:, :, pl.ds(RIM, RIM)]]
+    sides = [w_ref.at[:, pl.ds(inner, RIM), pl.ds(col, wide)] for col, wide in ((RIM, TILE), (0, RIM), (RIM + TILE, RIM))]
+    loads = [pltpu.make_async_copy(x, y, in_sem.at[k]) for k, (x, y) in enumerate(zip(arrivals, places + sides))]
+    places.append(w_ref.at[:, pl.ds(inner, RIM), :])
     loads.append(pltpu.make_async_copy(pup_ref, p_ref, in_sem.at[9]))
     amp_load = pltpu.make_async_copy(ampl_ref, amp_ref, in_sem.at[10])
     for load in loads:
@@ -264,7 +268,7 @@
                 w_ref[q, pl.ds(k, 16), lane_tile(a)] = jnp.where(ahead, x, 0.0).astype(BF16)
                 w_ref[q, pl.ds(k + N, 16), lane_tile(a)] = jnp.where(ahead, 0.0, x).astype(BF16)
 
-    results = (oc_ref, ol_ref, or_ref, ov_ref, ovl_ref, ovr_ref, oi_ref, oil_ref, oir_ref)
+    results = (oc_ref, ol_ref, or_ref, ov_ref, ovl_ref, ovr_ref, oi_ref)
     stores = [pltpu.make_async_copy(x, y, out_sem.at[k]) for k, (x, y) in enumerate(zip(places, results))]
     for store in stores:
         store.start()
@@ -274,7 +278,7 @@
     base = r0 - shift
     up = jnp.bitwise_and(8 - shift, 7)
     inside = lax.broadcasted_iota(jnp.int32, (8, N), 0) < 8 - shift
-    for s, (out_ref, bit) in enumerate(((other_ref, 1 - core), (mine_ref, core))):
+    for s, (out_ref, t_ref, bit) in enumerate(((other_ref, to_ref, 1 - core), (mine_ref, tm_ref, core))):
         @pl.loop(0, 8)
         def _(i):
             u = jnp.right_shift(i, 1) * 256 + bit * 128 + jnp.bitwise_and(i, 1) * 64
@@ -282,10 +286,11 @@
             for q in range(2):
                 to = pl.multiple_of(q * 512 + i * 64, 64)
                 turned = [pltpu.roll(a_ref[q, pl.ds(start + 8 * j, 8), :], up, 0) for j in range(9)]
-                for j in range(8):
-                    t_ref[s, pl.ds(to + 8 * j, 8), :] = jnp.where(inside, turned[j], turned[j + 1])
-
-        store = pltpu.make_async_copy(t_ref.at[s], out_ref, out_sem.at[9 + s])
+                lines = [jnp.where(inside, turned[j], turned[j + 1]) for j in range(8)]
+                for j in range(0, 8, 2):
+                    t_ref[pl.ds(to + 8 * j, 16), :] = jnp.concatenate(lines[j:j + 2], axis=0).astype(t_ref.dtype)
+
+        store = pltpu.make_async_copy(t_ref, out_ref, out_sem.at[7 + s])
         store.start()
         stores.append(store)
     for store in stores:
@@ -301,9 +306,10 @@
 
     return pl.pallas_call(
         led_body,
-        out_shape=rims(TILE) + rims(RIM) + rims(RIM) + [jax.ShapeDtypeStruct((N, N), F32)] * 2,
-        in_specs=[pl.BlockSpec(memory_space=pltpu.SMEM)] + [hbm] * 11 + [vm] * 6,
-        out_specs=[hbm] * 11,
+        out_shape=rims(TILE) + rims(RIM) + [jax.ShapeDtypeStruct((2, RIM, REGION), BF16)]
+        + [jax.ShapeDtypeStruct((N, N), F32), jax.ShapeDtypeStruct((N, N), BF16)],
+        in_specs=[pl.BlockSpec(memory_space=pltpu.SMEM)] + [hbm] * 10 + [vm] * 6,
+        out_specs=[hbm] * 9,
         scratch_shapes=[
             pltpu.VMEM((2, REGION, REGION), BF16),
             pltpu.VMEM((2, N, N), BF16),
@@ -313,9 +319,10 @@
             pltpu.VMEM((8, 512, CB), BF16),
             pltpu.VMEM((8, RB, 256), F32),
             pltpu.VMEM((8, 256, CB), F32),
-            pltpu.VMEM((2, N, N), F32),
+            pltpu.VMEM((N, N), BF16),
+            pltpu.VMEM((N, N), F32),
             pltpu.SemaphoreType.DMA((11,)),
-            pltpu.SemaphoreType.DMA((11,)),
+            pltpu.SemaphoreType.DMA((9,)),
         ],
         compiler_params=pltpu.CompilerParams(vmem_limit_bytes=60 * 2**20),
         cost_estimate=pl.CostEstimate(flops=13 * 10**9, bytes_accessed=30 * 2**20, transcendentals=N * N),
@@ -323,7 +330,7 @@
     )(pos, *pieces, p, amp, tb["lane_inv"], tb["lane_fwd"], tb["row_inv"], tb["row_fwd"], tb["tw_lane"], tb["tw_row"])
 
 
-def turn_body(pos_ref, p_ref, po_ref, x_ref):
+def turn_body(pos_ref, p_ref, token_ref, po_ref, x_ref):
     r0, c0 = pos_ref[0], pos_ref[1]
 
     @pl.loop(0, N // 16)
@@ -349,59 +356,79 @@
             po_ref[q, pl.ds(u, 64), :] = jnp.concatenate(rows, axis=0).astype(BF16)
 
 
-def turn(pos, pupil):
+def turn(pos, pupil, token):
     vm = pl.BlockSpec(memory_space=pltpu.VMEM)
     return pl.pallas_call(
         turn_body,
         out_shape=jax.ShapeDtypeStruct((2, N, N), BF16),
-        in_specs=[pl.BlockSpec(memory_space=pltpu.SMEM), vm],
+        in_specs=[pl.BlockSpec(memory_space=pltpu.SMEM), vm, pl.BlockSpec(memory_space=pl.ANY)],
         out_specs=vm,
         scratch_shapes=[pltpu.VMEM((2, N + 264, N), F32)],
         compiler_params=pltpu.CompilerParams(vmem_limit_bytes=40 * 2**20),
         cost_estimate=pl.CostEstimate(flops=N**3, bytes_accessed=24 * 2**20, transcendentals=0),
         name="turn",
-    )(pos, pupil)
-
-
-def order_body(pos_ref, amp_ref, perm_ref, spec_ref, ao_ref, v_ref, vl_ref, vr_ref, i_ref, sem):
+    )(pos, pupil, token)
+
+
+def order_body(pos_ref, amp_ref, perm_ref, spec_ref, ao_ref, v_ref, vl_ref, vr_ref):
     core = pos_ref[2]
     gap = TILE - RIM
     outer = pl.multiple_of(core * gap, 128)
-    inner = pl.multiple_of((1 - core) * gap, 128)
-    ends = ((v_ref, outer, 0, TILE), (vl_ref, outer, gap, RIM), (vr_ref, outer, 0, RIM), (i_ref, inner, 0, TILE))
-    copies = [
-        pltpu.make_async_copy(spec_ref.at[:, pl.ds(row, RIM), pl.ds(col, wide)], out, sem.at[k])
-        for k, (out, row, col, wide) in enumerate(ends)
-    ]
-    for copy in copies:
-        copy.start()
+    ends = ((v_ref, outer, 0, TILE), (vl_ref, outer, gap, RIM), (vr_ref, outer, 0, RIM))
+    for out, row, col, wide in ends:
+        @pl.loop(0, RIM // 32)
+        def _(i):
+            src = pl.ds(pl.multiple_of(row + i * 32, 32), 32)
+            for q in range(2):
+                out[q, pl.ds(pl.multiple_of(i * 32, 32), 32), :] = spec_ref[q, src, col:col + wide]
+
     for i in range(4):
         part = dot(perm_ref[i * 256:(i + 1) * 256, :], amp_ref[...]).astype(BF16)
         part = lax.dot_general(part, perm_ref[...], (((1,), (1,)), ((), ())), preferred_element_type=F32)
         ao_ref[i * 256:(i + 1) * 256, :] = part.astype(BF16)
-    for copy in copies:
-        copy.wait()
 
 
 def order(pos, amplitude, perm, spectrum):
     vm = pl.BlockSpec(memory_space=pltpu.VMEM)
-    hbm = pl.BlockSpec(memory_space=pl.ANY)
-    ends = [jax.ShapeDtypeStruct((2, RIM, wide), BF16) for wide in (TILE, RIM, RIM, TILE)]
+    ends = [jax.ShapeDtypeStruct((2, RIM, wide), BF16) for wide in (TILE, RIM, RIM)]
     return pl.pallas_call(
         order_body,
         out_shape=[jax.ShapeDtypeStruct((N, N), BF16)] + ends,
-        in_specs=[pl.BlockSpec(memory_space=pltpu.SMEM), vm, vm, hbm],
-        out_specs=[vm] + [hbm] * 4,
-        scratch_shapes=[pltpu.SemaphoreType.DMA((4,))],
+        in_specs=[pl.BlockSpec(memory_space=pltpu.SMEM), vm, vm, vm],
+        out_specs=[vm] * 4,
         compiler_params=pltpu.CompilerParams(vmem_limit_bytes=40 * 2**20),
         cost_estimate=pl.CostEstimate(flops=4 * N**3, bytes_accessed=12 * 2**20, transcendentals=0),
         name="order",
     )(pos, amplitude, perm, spectrum)
 
 
-def sides_body(pos_ref, l_ref, r_ref, il_ref, ir_ref, ol_ref, or_ref):
+def cut_body(pos_ref, l_ref, r_ref, token_ref, out_ref):
+    row = (1 - pos_ref[2]) * (TILE - RIM)
+
+    @pl.loop(0, RIM // 32)
+    def _(i):
+        dst = pl.ds(pl.multiple_of(i * 32, 32), 32)
+        src = pl.ds(pl.multiple_of(row + i * 32, 32), 32)
+        for q in range(2):
+            out_ref[q, dst, 0:RIM] = l_ref[q, src, :]
+            out_ref[q, dst, RIM:2 * RIM] = r_ref[q, src, :]
+
+
+def cut(pos, l, r, token):
+    vm = pl.BlockSpec(memory_space=pltpu.VMEM)
+    return pl.pallas_call(
+        cut_body,
+        out_shape=jax.ShapeDtypeStruct((2, RIM, 2 * RIM), BF16),
+        in_specs=[pl.BlockSpec(memory_space=pltpu.SMEM), vm, vm, pl.BlockSpec(memory_space=pl.ANY)],
+        out_specs=vm,
+        cost_estimate=pl.CostEstimate(flops=0, bytes_accessed=4 * 2**20, transcendentals=0),
+        name="cut",
+    )(pos, l, r, token)
+
+
+def sides_body(pos_ref, l_ref, r_ref, i_ref, first_ref, second_ref, ol_ref, or_ref):
     at = (1 - pos_ref[2]) * (TILE - RIM)
-    for mid_ref, add_ref, out_ref in ((l_ref, il_ref, ol_ref), (r_ref, ir_ref, or_ref)):
+    for mid_ref, col, out_ref in ((l_ref, 0, ol_ref), (r_ref, RIM + TILE, or_ref)):
         out_ref[...] = mid_ref[...]
 
         @pl.loop(0, RIM // 32)
@@ -409,20 +436,21 @@
             src = pl.ds(pl.multiple_of(i * 32, 32), 32)
             dst = pl.ds(pl.multiple_of(at + i * 32, 32), 32)
             for q in range(2):
-                out_ref[q, dst, :] = (mid_ref[q, dst, :].astype(F32) + add_ref[q, src, :].astype(F32)).astype(BF16)
-
-
-def sides(pos, l, r, il, ir):
+                add = i_ref[q, src, col:col + RIM].astype(F32)
+                out_ref[q, dst, :] = (mid_ref[q, dst, :].astype(F32) + add).astype(BF16)
+
+
+def sides(pos, l, r, i, first, second):
     vm = pl.BlockSpec(memory_space=pltpu.VMEM)
     return pl.pallas_call(
         sides_body,
         out_shape=[jax.ShapeDtypeStruct(l.shape, BF16)] * 2,
-        in_specs=[pl.BlockSpec(memory_space=pltpu.SMEM)] + [vm] * 4,
+        in_specs=[pl.BlockSpec(memory_space=pltpu.SMEM)] + [vm] * 3 + [pl.BlockSpec(memory_space=pl.ANY)] * 2,
         out_specs=[vm] * 2,
         compiler_params=pltpu.CompilerParams(vmem_limit_bytes=32 * 2**20),
         cost_estimate=pl.CostEstimate(flops=2**20, bytes_accessed=6 * 2**20, transcendentals=0),
         name="sides",
-    )(pos, l, r, il, ir)
+    )(pos, l, r, i, first, second)
 
 
 def tile_body(pos_ref, c_ref, i_ref, v_ref, l_ref, r_ref, vl_ref, vr_ref, out_ref):
@@ -437,7 +465,7 @@
     @pl.loop(0, RIM // 32)
     def _(i):
         src = pl.ds(pl.multiple_of(i * 32, 32), 32)
-        out_ref[0, pl.ds(pl.multiple_of(at_i + i * 32, 32), 32), :] += i_ref[0, src, :].astype(F32)
+        out_ref[0, pl.ds(pl.multiple_of(at_i + i * 32, 32), 32), :] += i_ref[0, src, RIM:RIM + TILE].astype(F32)
         dst = pl.ds(pl.multiple_of(at_v + i * 32, 32), 32)
         out_ref[0, dst, :] += v_ref[0, src, :].astype(F32)
         out_ref[0, dst, gap:] += vl_ref[0, src, :].astype(F32)
@@ -460,27 +488,39 @@
     )(pos, *parts)
 
 
-CUT = 640
-
-
-def pair_body(mine_ref, other_ref, token_ref, a_ref, b_ref):
-    total = mine_ref[...] + other_ref[...]
-    a_ref[...] = total[:, :CUT].astype(BF16)
+def pair_body(mine_ref, other_ref, out_ref):
     for z in range(8):
-        b_ref[z, 0] = total[z * 16:(z + 1) * 16, CUT:].astype(BF16)
-
-
-def pair_sum(mine, other, token):
+        rows = pl.ds(z * 16, 16)
+        out_ref[z, 0] = mine_ref[rows, :] + other_ref[rows, :].astype(F32)
+
+
+def pair_sum(mine, other):
     rows = pl.BlockSpec((128, N), lambda i: (i, 0))
     return pl.pallas_call(
         pair_body,
         grid=(8,),
-        out_shape=[jax.ShapeDtypeStruct((N, CUT), BF16), jax.ShapeDtypeStruct((8, 8, 16, N - CUT), BF16)],
-        in_specs=[rows, rows, pl.BlockSpec(memory_space=pl.ANY)],
-        out_specs=[pl.BlockSpec((128, CUT), lambda i: (i, 0)), pl.BlockSpec((8, 1, 16, N - CUT), lambda i: (0, i, 0, 0))],
-        cost_estimate=pl.CostEstimate(flops=N * N, bytes_accessed=10 * 2**20, transcendentals=0),
+        out_shape=jax.ShapeDtypeStruct((8, 8, 16, N), F32),
+        in_specs=[rows, rows],
+        out_specs=pl.BlockSpec((8, 1, 16, N), lambda i: (0, i, 0, 0)),
+        cost_estimate=pl.CostEstimate(flops=N * N, bytes_accessed=12 * 2**20, transcendentals=0),
         name="pair_sum",
-    )(mine, other, token)
+    )(mine, other)
+
+
+def after_body(x_ref, token_ref, out_ref):
+    out_ref[...] = x_ref[...]
+
+
+def after(x, token):
+    vm = pl.BlockSpec(memory_space=pltpu.VMEM)
+    return pl.pallas_call(
+        after_body,
+        out_shape=jax.ShapeDtypeStruct(x.shape, x.dtype),
+        in_specs=[vm, pl.BlockSpec(memory_space=pl.ANY)],
+        out_specs=vm,
+        cost_estimate=pl.CostEstimate(flops=0, bytes_accessed=2**20, transcendentals=0),
+        name="after",
+    )(x, token)
 
 
 KY, KX = ("x", "yh", "core"), ("z", "yl")
@@ -515,38 +555,28 @@
 
     in_l = lax.ppermute(spectrum[:, :, TILE - RIM:], KX, right)
     in_r = lax.ppermute(spectrum[:, :, :RIM], KX, left)
-    amp, out_v, out_vl, out_vr, out_i = order(pos, amplitude, tb["perm"], spectrum)
+    amp, out_v, out_vl, out_vr = order(pos, amplitude, tb["perm"], spectrum)
     in_v = lax.ppermute(out_v, KY, vert)
     in_vl = lax.ppermute(out_vl, ALL, vert_r)
     in_vr = lax.ppermute(out_vr, ALL, vert_l)
-    in_i = lax.ppermute(out_i, "core", swap)
-    pupil = turn(pos, pupil)
-    in_il = lax.ppermute(jnp.where(first, in_l[:, TILE - RIM:], in_l[:, :RIM]), "core", swap)
-    in_ir = lax.ppermute(jnp.where(first, in_r[:, TILE - RIM:], in_r[:, :RIM]), "core", swap)
-    pieces = (spectrum, in_l, in_r, in_v, in_vl, in_vr, in_i, in_il, in_ir)
-    c, l, r, v, vl, vr, i, il, ir, mine, other = led(pos, pieces, pupil, amp, tb)
-
-    il = lax.ppermute(il, "core", swap)
-    ir = lax.ppermute(ir, "core", swap)
+    in_i = lax.ppermute(spectrum, "core", swap)
+    pupil = turn(pos, pupil, out_v)
+    in_c = lax.ppermute(cut(pos, in_l, in_r, pupil), "core", swap)
+    pieces = (spectrum, in_l, in_r, in_v, in_vl, in_vr, in_i, in_c)
+    c, l, r, v, vl, vr, i, mine, other = led(pos, pieces, pupil, amp, tb)
+
+    i = lax.ppermute(i, "core", swap)
     v = lax.ppermute(v, KY, vert)
     vl = lax.ppermute(vl, ALL, vert_l)
     vr = lax.ppermute(vr, ALL, vert_r)
-    i = lax.ppermute(i, "core", swap)
-    other = lax.ppermute(other, "core", swap)
-    l, r = sides(pos, l, r, il, ir)
-    part_a, part_b = pair_sum(mine, other, l)
+    total = pair_sum(mine, lax.ppermute(other, "core", swap))
+    l, r = sides(pos, l, r, i, total, v)
     l = lax.ppermute(l, KX, left)
     r = lax.ppermute(r, KX, right)
-
-    part_a = lax.all_to_all(part_a.reshape(4, N // 4, CUT), "x", 0, 0)
-    part_b = lax.all_to_all(part_b.reshape(8, N // 8, N - CUT), "z", 0, 0)
-    part_a = jnp.sum(part_a.astype(F32), axis=0).reshape(2, 8, 16, CUT).transpose(1, 0, 2, 3).reshape(8, 32, CUT)
-    part_b = jnp.sum(part_b.astype(F32), axis=0).reshape(4, 32, N - CUT)
-    part_a = jnp.sum(lax.all_to_all(part_a, "z", 0, 0), axis=0)
-    part_b = jnp.sum(lax.all_to_all(part_b, "x", 0, 0), axis=0)
-    rest = jnp.concatenate([part_a, part_b], axis=1).reshape(4, 8, N)
-    pupil_grad = jnp.sum(lax.all_to_all(rest, ("yh", "yl"), 0, 0), axis=0).reshape(-1)
-    return tile_sum(pos, (c, i, v, l, r, vl, vr)), pupil_grad
+    tile = tile_sum(pos, (c, i, v, l, r, vl, vr))
+    total = lax.psum_scatter(total.reshape(8, 128, N), "z", scatter_dimension=0, tiled=True).reshape(16, 8, N)
+    total = lax.all_to_all(after(total, tile), ("x", "yh", "yl"), 0, 0)
+    return tile, jnp.sum(total, axis=0).reshape(-1)
 
 
 def solution(mesh):

time: 296 us -> 284 us (0.959); the launches traced: 291 us -> 282 us
  starting transfers between devices: 64.2 us -> 36.6 us
  between operations: 2.22 us -> 15.6 us
  waiting for transfers between devices: 87 us -> 98.6 us
  other arithmetic: 6.47 us -> 0.11 us
  local copies, waits for them, and re-layouts: 20.9 us -> 17.2 us
  Pallas kernels: 78.2 us -> 81.6 us
    ppermute x1, waiting for transfers between devices: 0.01 us -> 32.9 us  [body(): v = lax.ppermute(v, KY, vert)]
    all_to_all x4 -> x0, waiting for transfers between devices: 20.4 us -> none  [the longest x1 16.4 us: body(): part_a = lax.all_to_all(part_a.reshape(4, N // 4, CUT), 'x', 0, 0)]
    all_to_all x4 -> x0, starting transfers between devices: 16.2 us -> none  [the longest x1 4.6 us: body(): lax.all_to_all(rest, ('yh', 'yl'), 0, 0)]
    ppermute x1, waiting for transfers between devices: 25.5 us -> 38.8 us  [body(): in_vl = lax.ppermute(out_vl, ALL, vert_r)]
    ppermute x1, waiting for transfers between devices: 7.65 us -> 0.01 us  [body(): r = lax.ppermute(r, KX, right)]
    ppermute x1, waiting for transfers between devices: 8.05 us -> 2.27 us  [body(): vr = lax.ppermute(vr, ALL, vert_r)]
    ppermute x1, starting transfers between devices: 16 us -> 10.5 us  [body(): vr = lax.ppermute(vr, ALL, vert_r)]
    pallas_call x2 -> x4, Pallas kernels: 61 us -> 64.8 us  [the longest x1 53.3 us: led(): pl.pallas_call(led_body, out_shape=rims(TILE) + rims(RIM) + [jax.ShapeDty...]
  transfers between devices with their start and end apart: 21 -> 15, of which waited for: 9 -> 7; matrix products, arithmetic and copies ran while one was open for 3% -> 0% of each run, Pallas kernels for 6% -> 6%
where the time goes in v2:
time: 284 us; the launch traced here: 282 us
  waiting for transfers between devices  98.6 us (35%)
  Pallas kernels  81.6 us (29%)
  starting transfers between devices  36.6 us (13%)
  blocking collectives  32.4 us (11%)
  local copies, waits for them, and re-layouts  17.2 us (6%)
  between operations  15.6 us (5%)
    pallas_call x1, Pallas kernels, led(): pl.pallas_call(led_body, out_shape=rims(TILE) + rims(RIM) + [jax.ShapeDty...  53.3 us
    ppermute x1, waiting for transfers between devices, body(): in_vl = lax.ppermute(out_vl, ALL, vert_r)  38.8 us
    ppermute x1, waiting for transfers between devices, body(): v = lax.ppermute(v, KY, vert)  32.9 us
    all_to_all x1, blocking collectives, body(): total = lax.all_to_all(after(total, tile), ('x', 'yh', 'yl'), 0, 0)  32.4 us
    unnamed x43, local copies, waits for them, and re-layouts  13.8 us
    ppermute x1, waiting for transfers between devices, body(): in_l = lax.ppermute(spectrum[:, :, TILE - RIM:], KX, right)  10.8 us
    ppermute x1, starting transfers between devices, body(): vr = lax.ppermute(vr, ALL, vert_r)  10.5 us
    pallas_call x1, Pallas kernels, turn(): pl.pallas_call(turn_body, out_shape=jax.ShapeDtypeStruct((2, N, N), BF16)...  7.75 us
  transfers between devices with their start and end apart: 15, of which 7 were waited for; matrix products, arithmetic and copies ran while one was open for 0% of the time, Pallas kernels for 6%

profile of v2, /device:TPU:1, one launch (start us, length us, event | category | flops | bytes accessed | tf_op | source)
XLA Modules:
  0.0 282.2 jit_solution(13138654513218968155)
XLA Ops:
  7.2 0.0 copy-start.3
  7.2 0.0 reduce-scatter.2.cloned.1.call-start
  7.2 2.8 fusion
  10.0 1.3 collective-permute-start.1
  11.3 5.6 %collective-permute-start = (bf16[2,512,384]{2,1,0:T(8,128)(2,1)}, bf16[2,512,384]{2,1,0:T(8,128)(2,1)}, u32[]{:S(2)}, u32[]{:S(2)}) collective-permute-start(bf16[2,512,384]{2,1,0:T(8,128)(2,1)} %get-tuple-element.33), channel_id=1, source_target_pairs={{0,1},{1,2},{2,3},{3,4},{4,5},{5,6},{6,7},{7,8},{8,9},{9,10},{10,1... | collective-permute-start | bytes 2359304 | tf_op jit(solution)/shard_map/ppermute | solution.py:556
  16.8 0.0 copy-done.13
  16.8 0.6 fusion.1
  18.8 0.1 pad_add_fusion.pos_ref
  18.9 1.6 copy-done.9
  20.5 1.6 copy-done.10
  22.1 5.4 %order.1 = (bf16[1024,1024]{1,0:T(8,128)(2,1)S(1)}, bf16[2,384,512]{2,1,0:T(8,128)(2,1)S(1)}, bf16[2,384,384]{2,1,0:T(8,128)(2,1)S(1)}, bf16[2,384,384]{2,1,0:T(8,128)(2,1)S(1)}) custom-call(s32[3]{0:T(128)S(1)} %pad_add_fusion.pos_ref, bf16[1024,1024]{1,0:T(8,128)(2,1)S(1)} %copy-done.9, bf16[1024,1024]{1,0:T(8,128)(2,1)S(1)} %copy-done.10, ...), custom_call_target="tpu_custom_call" | custom-call | flops 4294967296 | bytes 12582912 | tf_op jit(solution)/shard_map/order/pallas_call | solution.py:394
  27.5 0.0 copy-start.11
  27.5 1.3 copy-done.11
  28.8 0.0 copy-done.2
  28.8 7.7 %turn.1.token_ref.pup_ref = bf16[2,1024,1024]{2,1,0:T(8,128)(2,1)S(1)} custom-call(s32[3]{0:T(128)S(1)} %pad_add_fusion.pos_ref, bf16[2,1024,1024]{2,1,0:T(8,128)(2,1)S(1)} %copy-done.2, bf16[2,384,512]{2,1,0:T(8,128)(2,1)S(1)} %get-tuple-element.17.token_ref), custom_call_target="tpu_custom_call" | custom-call | flops 1073741824 | bytes 25165824 | tf_op jit(solution)/shard_map/turn/pallas_call | solution.py:361
  36.6 0.0 copy-start.1
  36.6 2.0 copy-done.1
  38.6 0.0 collective-permute-done.1.r_ref
  38.6 10.8 %collective-permute-done.l_ref = bf16[2,512,384]{2,1,0:T(8,128)(2,1)} collective-permute-done((bf16[2,512,384]{2,1,0:T(8,128)(2,1)}, bf16[2,512,384]{2,1,0:T(8,128)(2,1)}, u32[]{:S(2)}, u32[]{:S(2)}) %collective-permute-start) | collective-permute-done | bytes 786464 | tf_op jit(solution)/shard_map/ppermute | solution.py:556
  49.3 2.6 cut.1
  52.0 0.5 collective-permute-start.6
  52.5 0.0 collective-permute-start.5
  52.5 4.9 %collective-permute-start.2 = (bf16[2,384,512]{2,1,0:T(8,128)(2,1)S(1)}, bf16[2,384,512]{2,1,0:T(8,128)(2,1)S(1)}, u32[]{:S(2)}, u32[]{:S(2)}) collective-permute-start(bf16[2,384,512]{2,1,0:T(8,128)(2,1)S(1)} %get-tuple-element.17.token_ref), channel_id=1, source_target_pairs={{16,32},{48,64},{80,96},{112,128},{144,160},{176,192},{208,224},{3... | collective-permute-start | bytes 2359304 | tf_op jit(solution)/shard_map/ppermute | solution.py:559
  57.4 3.8 %collective-permute-start.3 = (bf16[2,384,384]{2,1,0:T(8,128)(2,1)S(1)}, bf16[2,384,384]{2,1,0:T(8,128)(2,1)S(1)}, u32[]{:S(2)}, u32[]{:S(2)}) collective-permute-start(bf16[2,384,384]{2,1,0:T(8,128)(2,1)S(1)} %get-tuple-element.18), channel_id=1, source_target_pairs={{16,33},{17,34},{18,35},{19,36},{20,37},{21,38},{22,39},{23,40},{2... | collective-permute-start | bytes 1769480 | tf_op jit(solution)/shard_map/ppermute | solution.py:560
  61.2 1.3 collective-permute-start.4
  62.5 38.8 %collective-permute-done.3.vl_ref = bf16[2,384,384]{2,1,0:T(8,128)(2,1)S(1)} collective-permute-done((bf16[2,384,384]{2,1,0:T(8,128)(2,1)S(1)}, bf16[2,384,384]{2,1,0:T(8,128)(2,1)S(1)}, u32[]{:S(2)}, u32[]{:S(2)}) %collective-permute-start.3) | collective-permute-done | bytes 589856 | tf_op jit(solution)/shard_map/ppermute | solution.py:560
  101.3 0.0 collective-permute-done.4.vr_ref
  101.3 0.0 collective-permute-done.2.v_ref
  101.3 0.0 copy-start.16
  101.3 0.0 collective-permute-done.5.i_ref
  101.4 1.0 copy-done.15
  102.4 0.0 collective-permute-done.6.c_ref
  102.4 0.1 copy-done.19
  102.5 0.2 copy-done.20
  102.7 0.2 copy-done.16
  103.0 53.3 %led.1 = (bf16[2,512,512]{2,1,0:T(8,128)(2,1)}, bf16[2,512,384]{2,1,0:T(8,128)(2,1)}, bf16[2,512,384]{2,1,0:T(8,128)(2,1)}, bf16[2,384,512]{2,1,0:T(8,128)(2,1)}...) custom-call(s32[3]{0:T(128)} %copy-done.7, ...), custom_call_target="tpu_custom_call" | custom-call | flops 12999999488 | bytes 31457280 | tf_op jit(solution)/shard_map/led/pallas_call | solution.py:307
  156.3 0.1 collective-permute-start.9
  156.4 4.4 %collective-permute-done.9.other_ref = bf16[1024,1024]{1,0:T(8,128)(2,1)S(1)} collective-permute-done((bf16[1024,1024]{1,0:T(8,128)(2,1)}, bf16[1024,1024]{1,0:T(8,128)(2,1)S(1)}, u32[]{:S(2)}, u32[]{:S(2)}) %collective-permute-start.9) | collective-permute-done | bytes 2097184 | tf_op jit(solution)/shard_map/ppermute | solution.py:572
  160.8 1.3 copy-done.12
  162.1 7.0 %pair_sum.1.first_ref = f32[8,8,16,1024]{3,2,1,0:T(8,128)} custom-call(f32[1024,1024]{1,0:T(8,128)} %get-tuple-element.26.mine_ref, bf16[1024,1024]{1,0:T(8,128)(2,1)} %copy-done.12), custom_call_target="tpu_custom_call" | custom-call | flops 1048576 | bytes 12582912 | tf_op jit(solution)/shard_map/pair_sum/pallas_call | solution.py:499
  169.1 0.0 copy-start.8
  169.1 0.0 reduce-scatter.2.cloned.1.call-update
  169.1 1.5 copy-done.14
  170.6 0.1 collective-permute-start.7
  170.8 1.9 collective-permute-start.8
  172.7 32.9 %collective-permute-done.8.second_ref.v_ref = bf16[2,384,512]{2,1,0:T(8,128)(2,1)S(1)} collective-permute-done((bf16[2,384,512]{2,1,0:T(8,128)(2,1)}, bf16[2,384,512]{2,1,0:T(8,128)(2,1)S(1)}, u32[]{:S(2)}, u32[]{:S(2)}) %collective-permute-start.8) | collective-permute-done | bytes 786464 | tf_op jit(solution)/shard_map/ppermute | solution.py:569
  205.5 0.0 collective-permute-done.7.i_ref
  205.5 0.0 copy-done.6
  205.6 0.0 copy-start
  205.6 2.2 copy-done
  207.8 1.1 sides.1
  208.9 1.3 collective-permute-start.10
  210.2 4.0 %collective-permute-start.11 = (bf16[2,512,384]{2,1,0:T(8,128)(2,1)S(1)}, bf16[2,512,384]{2,1,0:T(8,128)(2,1)S(1)}, u32[]{:S(2)}, u32[]{:S(2)}) collective-permute-start(bf16[2,512,384]{2,1,0:T(8,128)(2,1)S(1)} %get-tuple-element.29), channel_id=1, source_target_pairs={{0,1},{1,2},{2,3},{3,4},{4,5},{5,6},{6,7},{7,8},{8,9},{9,10},{10,1... | collective-permute-start | bytes 2359304 | tf_op jit(solution)/shard_map/ppermute | solution.py:575
  214.2 1.3 collective-permute-start.12
  215.6 10.5 %collective-permute-start.13 = (bf16[2,384,384]{2,1,0:T(8,128)(2,1)S(1)}, bf16[2,384,384]{2,1,0:T(8,128)(2,1)S(1)}, u32[]{:S(2)}, u32[]{:S(2)}) collective-permute-start(bf16[2,384,384]{2,1,0:T(8,128)(2,1)S(1)} %copy-done.17), channel_id=1, source_target_pairs={{16,33},{17,34},{18,35},{19,36},{20,37},{21,38},{22,39},{23,40},{2... | collective-permute-start | bytes 1769480 | tf_op jit(solution)/shard_map/ppermute | solution.py:571
  226.1 5.9 %collective-permute-done.12.vl_ref = bf16[2,384,384]{2,1,0:T(8,128)(2,1)S(1)} collective-permute-done((bf16[2,384,384]{2,1,0:T(8,128)(2,1)S(1)}, bf16[2,384,384]{2,1,0:T(8,128)(2,1)S(1)}, u32[]{:S(2)}, u32[]{:S(2)}) %collective-permute-start.12) | collective-permute-done | bytes 589856 | tf_op jit(solution)/shard_map/ppermute | solution.py:570
  232.0 2.3 collective-permute-done.13.vr_ref
  234.2 0.0 collective-permute-done.10.l_ref
  234.3 0.0 collective-permute-done.11.r_ref
  234.3 2.6 tile_sum.1.token_ref
  236.8 3.6 %reduce-scatter.2.cloned.1.call-done = f32[1,128,1024]{2,1,0:T(8,128)} async-done(((f32[8,128,1024]{2,1,0:T(8,128)}), f32[1,128,1024]{2,1,0:T(8,128)}) %reduce-scatter.2.cloned.1.call-update) | async-done | bytes 524304 | tf_op jit(solution)/shard_map/reduce_scatter | solution.py:577
  240.4 1.9 after.1
  242.3 32.4 %all_to_all.5 = f32[16,8,1024]{2,1,0:T(8,128)S(1)} all-to-all(f32[16,8,1024]{2,1,0:T(8,128)} %after.1), channel_id=1, replica_groups=mesh['x'=4,'yh'=2,'core'=2,'z'=8,'yl'=2] {'x','yh','yl'}, dimensions={0} | all-to-all | bytes 1048576 | tf_op jit(solution)/shard_map/all_to_all | solution.py:578
  274.7 0.6 copy.15
  (23 shorter events, 0.1 us)
Async XLA Ops:
  7.2 11.7 %copy-start.3 = (bf16[2,512,512]{2,1,0:T(8,128)(2,1)S(1)}, bf16[2,512,512]{2,1,0:T(8,128)(2,1)}, u32[]{:S(2)}) copy-start(bf16[2,512,512]{2,1,0:T(8,128)(2,1)} %own_ref.1) | copy-start | bytes 3145732
  7.2 9.7 %copy-start.13 = (s32[1,1,2]{2,1,0:T(1,128)S(1)}, s32[1,1,2]{2,1,0:T(1,128)}, u32[]{:S(2)}) copy-start(s32[1,1,2]{2,1,0:T(1,128)} %param.14) | copy-start | bytes 28
  7.2 233.2 %reduce-scatter.2.cloned.1.call-start = ((), (), s32[]{:S(2)}) async-start(), calls=%async_computation.2 | async-start | bytes 4718592 | tf_op jit(solution)/shard_map/reduce_scatter | solution.py:577
  10.0 28.6 %collective-permute-start.1 = (bf16[2,512,384]{2,1,0:T(8,128)(2,1)}, bf16[2,512,384]{2,1,0:T(8,128)(2,1)}, u32[]{:S(2)}, u32[]{:S(2)}) collective-permute-start(bf16[2,512,384]{2,1,0:T(8,128)(2,1)} %get-tuple-element.32), channel_id=1, source_target_pairs={{1,0},{2,1},{3,2},{4,3},{5,4},{6,5},{7,6},{8,7},{9,8},{10,9},{11,1... | collective-permute-start | bytes 2359304 | tf_op jit(solution)/shard_map/ppermute | solution.py:557
  11.3 38.1 %collective-permute-start = (bf16[2,512,384]{2,1,0:T(8,128)(2,1)}, bf16[2,512,384]{2,1,0:T(8,128)(2,1)}, u32[]{:S(2)}, u32[]{:S(2)}) collective-permute-start(bf16[2,512,384]{2,1,0:T(8,128)(2,1)} %get-tuple-element.33), channel_id=1, source_target_pairs={{0,1},{1,2},{2,3},{3,4},{4,5},{5,6},{6,7},{7,8},{8,9},{9,10},{10,1... | collective-permute-start | bytes 2359304 | tf_op jit(solution)/shard_map/ppermute | solution.py:556
  18.9 1.6 copy-start.9
  20.5 1.6 copy-start.10
  22.1 6.8 %copy-start.7 = (s32[3]{0:T(128)}, s32[3]{0:T(128)S(1)}, u32[]{:S(2)}) copy-start(s32[3]{0:T(128)S(1)} %pad_add_fusion.pos_ref) | copy-start | bytes 40
  22.1 6.8 %copy-start.2 = (bf16[2,1024,1024]{2,1,0:T(8,128)(2,1)S(1)}, bf16[2,1024,1024]{2,1,0:T(8,128)(2,1)}, u32[]{:S(2)}) copy-start(bf16[2,1024,1024]{2,1,0:T(8,128)(2,1)} %p_ref.1) | copy-start | bytes 12582916
  27.5 1.3 copy-start.11
  36.6 2.0 copy-start.1
  52.0 50.4 %collective-permute-start.6 = (bf16[2,384,768]{2,1,0:T(8,128)(2,1)}, bf16[2,384,768]{2,1,0:T(8,128)(2,1)}, u32[]{:S(2)}, u32[]{:S(2)}) collective-permute-start(bf16[2,384,768]{2,1,0:T(8,128)(2,1)} %cut.1), channel_id=1, source_target_pairs={{0,16},{16,0},{1,17},{17,1},{2,18},{18,2},{3,19},{19,3},{4,20},{20... | collective-permute-start | bytes 3538952 | tf_op jit(solution)/shard_map/ppermute | solution.py:564
  52.5 48.9 %collective-permute-start.5 = (bf16[2,512,512]{2,1,0:T(8,128)(2,1)S(1)}, bf16[2,512,512]{2,1,0:T(8,128)(2,1)S(1)}, u32[]{:S(2)}, u32[]{:S(2)}) collective-permute-start(bf16[2,512,512]{2,1,0:T(8,128)(2,1)S(1)} %copy-done.3), channel_id=1, source_target_pairs={{0,16},{16,0},{1,17},{17,1},{2,18},{18,2},{3,19},{19,3},{4,20},{20... | collective-permute-start | bytes 3145736 | tf_op jit(solution)/shard_map/ppermute | solution.py:562
  52.5 48.8 %collective-permute-start.2 = (bf16[2,384,512]{2,1,0:T(8,128)(2,1)S(1)}, bf16[2,384,512]{2,1,0:T(8,128)(2,1)S(1)}, u32[]{:S(2)}, u32[]{:S(2)}) collective-permute-start(bf16[2,384,512]{2,1,0:T(8,128)(2,1)S(1)} %get-tuple-element.17.token_ref), channel_id=1, source_target_pairs={{16,32},{48,64},{80,96},{112,128},{144,160},{176,192},{208,224},{3... | collective-permute-start | bytes 2359304 | tf_op jit(solution)/shard_map/ppermute | solution.py:559
  57.4 43.9 %collective-permute-start.3 = (bf16[2,384,384]{2,1,0:T(8,128)(2,1)S(1)}, bf16[2,384,384]{2,1,0:T(8,128)(2,1)S(1)}, u32[]{:S(2)}, u32[]{:S(2)}) collective-permute-start(bf16[2,384,384]{2,1,0:T(8,128)(2,1)S(1)} %get-tuple-element.18), channel_id=1, source_target_pairs={{16,33},{17,34},{18,35},{19,36},{20,37},{21,38},{22,39},{23,40},{2... | collective-permute-start | bytes 1769480 | tf_op jit(solution)/shard_map/ppermute | solution.py:560
  61.2 40.1 %collective-permute-start.4 = (bf16[2,384,384]{2,1,0:T(8,128)(2,1)S(1)}, bf16[2,384,384]{2,1,0:T(8,128)(2,1)S(1)}, u32[]{:S(2)}, u32[]{:S(2)}) collective-permute-start(bf16[2,384,384]{2,1,0:T(8,128)(2,1)S(1)} %get-tuple-element.19), channel_id=1, source_target_pairs={{17,32},{18,33},{19,34},{20,35},{21,36},{22,37},{23,38},{24,39},{2... | collective-permute-start | bytes 1769480 | tf_op jit(solution)/shard_map/ppermute | solution.py:561
  101.3 1.2 copy-start.19
  101.3 1.4 copy-start.20
  101.3 1.6 copy-start.16
  101.3 1.1 copy-start.15
  156.3 4.5 %collective-permute-start.9 = (bf16[1024,1024]{1,0:T(8,128)(2,1)}, bf16[1024,1024]{1,0:T(8,128)(2,1)S(1)}, u32[]{:S(2)}, u32[]{:S(2)}) collective-permute-start(bf16[1024,1024]{1,0:T(8,128)(2,1)} %get-tuple-element.27), channel_id=1, source_target_pairs={{0,16},{16,0},{1,17},{17,1},{2,18},{18,2},{3,19},{19,3},{4,20},{20... | collective-permute-start | bytes 6291464 | tf_op jit(solution)/shard_map/ppermute | solution.py:572
  160.8 1.3 copy-start.12
  169.1 1.5 copy-start.14
  169.1 36.5 %copy-start.5 = (bf16[2,512,384]{2,1,0:T(8,128)(2,1)S(1)}, bf16[2,512,384]{2,1,0:T(8,128)(2,1)}, u32[]{:S(2)}) copy-start(bf16[2,512,384]{2,1,0:T(8,128)(2,1)} %get-tuple-element.24.l_ref) | copy-start | bytes 2359300
  169.1 36.5 %copy-start.6 = (bf16[2,512,384]{2,1,0:T(8,128)(2,1)S(1)}, bf16[2,512,384]{2,1,0:T(8,128)(2,1)}, u32[]{:S(2)}) copy-start(bf16[2,512,384]{2,1,0:T(8,128)(2,1)} %get-tuple-element.25.r_ref) | copy-start | bytes 2359300
  169.1 36.5 %copy-start.8 = (s32[3]{0:T(128)S(1)}, s32[3]{0:T(128)}, u32[]{:S(2)}) copy-start(s32[3]{0:T(128)} %copy-done.7) | copy-start | bytes 40
  170.6 34.9 %collective-permute-start.7 = (bf16[2,384,1280]{2,1,0:T(8,128)(2,1)S(1)}, bf16[2,384,1280]{2,1,0:T(8,128)(2,1)S(1)}, u32[]{:S(2)}, u32[]{:S(2)}) collective-permute-start(bf16[2,384,1280]{2,1,0:T(8,128)(2,1)S(1)} %copy-done.14), channel_id=1, source_target_pairs={{0,16},{16,0},{1,17},{17,1},{2,18},{18,2},{3,19},{19,3},{4,20},{20... | collective-permute-start | bytes 5898248 | tf_op jit(solution)/shard_map/ppermute | solution.py:568
  170.8 34.8 %collective-permute-start.8 = (bf16[2,384,512]{2,1,0:T(8,128)(2,1)}, bf16[2,384,512]{2,1,0:T(8,128)(2,1)S(1)}, u32[]{:S(2)}, u32[]{:S(2)}) collective-permute-start(bf16[2,384,512]{2,1,0:T(8,128)(2,1)} %get-tuple-element.23), channel_id=1, source_target_pairs={{16,32},{48,64},{80,96},{112,128},{144,160},{176,192},{208,224},{3... | collective-permute-start | bytes 2359304 | tf_op jit(solution)/shard_map/ppermute | solution.py:569
  205.6 2.2 copy-start
  207.8 6.5 %copy-start.18 = (bf16[2,384,384]{2,1,0:T(8,128)(2,1)S(1)}, bf16[2,384,384]{2,1,0:T(8,128)(2,1)}, u32[]{:S(2)}) copy-start(bf16[2,384,384]{2,1,0:T(8,128)(2,1)} %get-tuple-element.30) | copy-start | bytes 1769476
  207.8 7.8 %copy-start.17 = (bf16[2,384,384]{2,1,0:T(8,128)(2,1)S(1)}, bf16[2,384,384]{2,1,0:T(8,128)(2,1)}, u32[]{:S(2)}) copy-start(bf16[2,384,384]{2,1,0:T(8,128)(2,1)} %get-tuple-element.31) | copy-start | bytes 1769476
  207.8 26.5 %copy-start.4 = (bf16[2,512,512]{2,1,0:T(8,128)(2,1)S(1)}, bf16[2,512,512]{2,1,0:T(8,128)(2,1)}, u32[]{:S(2)}) copy-start(bf16[2,512,512]{2,1,0:T(8,128)(2,1)} %get-tuple-element.21.c_ref) | copy-start | bytes 3145732
  208.9 25.4 %collective-permute-start.10 = (bf16[2,512,384]{2,1,0:T(8,128)(2,1)S(1)}, bf16[2,512,384]{2,1,0:T(8,128)(2,1)S(1)}, u32[]{:S(2)}, u32[]{:S(2)}) collective-permute-start(bf16[2,512,384]{2,1,0:T(8,128)(2,1)S(1)} %get-tuple-element.28), channel_id=1, source_target_pairs={{1,0},{2,1},{3,2},{4,3},{5,4},{6,5},{7,6},{8,7},{9,8},{10,9},{11,1... | collective-permute-start | bytes 2359304 | tf_op jit(solution)/shard_map/ppermute | solution.py:574
  210.2 24.1 %collective-permute-start.11 = (bf16[2,512,384]{2,1,0:T(8,128)(2,1)S(1)}, bf16[2,512,384]{2,1,0:T(8,128)(2,1)S(1)}, u32[]{:S(2)}, u32[]{:S(2)}) collective-permute-start(bf16[2,512,384]{2,1,0:T(8,128)(2,1)S(1)} %get-tuple-element.29), channel_id=1, source_target_pairs={{0,1},{1,2},{2,3},{3,4},{4,5},{5,6},{6,7},{7,8},{8,9},{9,10},{10,1... | collective-permute-start | bytes 2359304 | tf_op jit(solution)/shard_map/ppermute | solution.py:575
  214.2 17.7 %collective-permute-start.12 = (bf16[2,384,384]{2,1,0:T(8,128)(2,1)S(1)}, bf16[2,384,384]{2,1,0:T(8,128)(2,1)S(1)}, u32[]{:S(2)}, u32[]{:S(2)}) collective-permute-start(bf16[2,384,384]{2,1,0:T(8,128)(2,1)S(1)} %copy-done.18), channel_id=1, source_target_pairs={{17,32},{18,33},{19,34},{20,35},{21,36},{22,37},{23,38},{24,39},{2... | collective-permute-start | bytes 1769480 | tf_op jit(solution)/shard_map/ppermute | solution.py:570
  215.6 18.7 %collective-permute-start.13 = (bf16[2,384,384]{2,1,0:T(8,128)(2,1)S(1)}, bf16[2,384,384]{2,1,0:T(8,128)(2,1)S(1)}, u32[]{:S(2)}, u32[]{:S(2)}) collective-permute-start(bf16[2,384,384]{2,1,0:T(8,128)(2,1)S(1)} %copy-done.17), channel_id=1, source_target_pairs={{16,33},{17,34},{18,35},{19,36},{20,37},{21,38},{22,39},{23,40},{2... | collective-permute-start | bytes 1769480 | tf_op jit(solution)/shard_map/ppermute | solution.py:571
Sparse Core Ops, SparseCore 0:
  169.2 71.1 reduce-scatter.1

commit v3 on v2

--- a/solution.py
+++ b/solution.py
@@ -17,6 +17,7 @@
 RIM = 384
 REGION = TILE + 2 * RIM
 FLOOR2 = 0.0625
+FREE = pl.CostEstimate(flops=1, bytes_accessed=1, transcendentals=0)
 
 
 def split_np(t):
@@ -299,7 +300,7 @@
 
 def led(pos, pieces, p, amp, tb):
     vm = pl.BlockSpec(memory_space=pltpu.VMEM)
-    hbm = pl.BlockSpec(memory_space=pl.ANY)
+    hbm = pl.BlockSpec(memory_space=pltpu.HBM)
 
     def rims(rows):
         return [jax.ShapeDtypeStruct((2, rows, cols), BF16) for cols in (TILE, RIM, RIM)]
@@ -330,7 +331,7 @@
     )(pos, *pieces, p, amp, tb["lane_inv"], tb["lane_fwd"], tb["row_inv"], tb["row_fwd"], tb["tw_lane"], tb["tw_row"])
 
 
-def turn_body(pos_ref, p_ref, token_ref, po_ref, x_ref):
+def turn_body(pos_ref, p_ref, po_ref, x_ref):
     r0, c0 = pos_ref[0], pos_ref[1]
 
     @pl.loop(0, N // 16)
@@ -356,53 +357,71 @@
             po_ref[q, pl.ds(u, 64), :] = jnp.concatenate(rows, axis=0).astype(BF16)
 
 
-def turn(pos, pupil, token):
+def turn(pos, pupil):
     vm = pl.BlockSpec(memory_space=pltpu.VMEM)
     return pl.pallas_call(
         turn_body,
         out_shape=jax.ShapeDtypeStruct((2, N, N), BF16),
-        in_specs=[pl.BlockSpec(memory_space=pltpu.SMEM), vm, pl.BlockSpec(memory_space=pl.ANY)],
+        in_specs=[pl.BlockSpec(memory_space=pltpu.SMEM), vm],
         out_specs=vm,
         scratch_shapes=[pltpu.VMEM((2, N + 264, N), F32)],
         compiler_params=pltpu.CompilerParams(vmem_limit_bytes=40 * 2**20),
-        cost_estimate=pl.CostEstimate(flops=N**3, bytes_accessed=24 * 2**20, transcendentals=0),
+        cost_estimate=FREE,
         name="turn",
-    )(pos, pupil, token)
-
-
-def order_body(pos_ref, amp_ref, perm_ref, spec_ref, ao_ref, v_ref, vl_ref, vr_ref):
-    core = pos_ref[2]
-    gap = TILE - RIM
-    outer = pl.multiple_of(core * gap, 128)
-    ends = ((v_ref, outer, 0, TILE), (vl_ref, outer, gap, RIM), (vr_ref, outer, 0, RIM))
-    for out, row, col, wide in ends:
-        @pl.loop(0, RIM // 32)
-        def _(i):
-            src = pl.ds(pl.multiple_of(row + i * 32, 32), 32)
-            for q in range(2):
-                out[q, pl.ds(pl.multiple_of(i * 32, 32), 32), :] = spec_ref[q, src, col:col + wide]
-
+    )(pos, pupil)
+
+
+def order_body(amp_ref, perm_ref, ao_ref):
     for i in range(4):
         part = dot(perm_ref[i * 256:(i + 1) * 256, :], amp_ref[...]).astype(BF16)
         part = lax.dot_general(part, perm_ref[...], (((1,), (1,)), ((), ())), preferred_element_type=F32)
         ao_ref[i * 256:(i + 1) * 256, :] = part.astype(BF16)
 
 
-def order(pos, amplitude, perm, spectrum):
+def order(amplitude, perm):
     vm = pl.BlockSpec(memory_space=pltpu.VMEM)
-    ends = [jax.ShapeDtypeStruct((2, RIM, wide), BF16) for wide in (TILE, RIM, RIM)]
     return pl.pallas_call(
         order_body,
-        out_shape=[jax.ShapeDtypeStruct((N, N), BF16)] + ends,
-        in_specs=[pl.BlockSpec(memory_space=pltpu.SMEM), vm, vm, vm],
-        out_specs=[vm] * 4,
+        out_shape=jax.ShapeDtypeStruct((N, N), BF16),
+        in_specs=[vm, vm],
+        out_specs=vm,
         compiler_params=pltpu.CompilerParams(vmem_limit_bytes=40 * 2**20),
-        cost_estimate=pl.CostEstimate(flops=4 * N**3, bytes_accessed=12 * 2**20, transcendentals=0),
+        cost_estimate=FREE,
         name="order",
-    )(pos, amplitude, perm, spectrum)
-
-
-def cut_body(pos_ref, l_ref, r_ref, token_ref, out_ref):
+    )(amplitude, perm)
+
+
+def ends_body(pos_ref, spec_ref, l_ref, r_ref, v_ref, vl_ref, vr_ref):
+    gap = TILE - RIM
+    l_ref[...] = spec_ref[:, :, gap:]
+    r_ref[...] = spec_ref[:, :, :RIM]
+    outer = pos_ref[2] * gap
+
+    @pl.loop(0, RIM // 32)
+    def _(i):
+        src = pl.ds(pl.multiple_of(outer + i * 32, 32), 32)
+        dst = pl.ds(pl.multiple_of(i * 32, 32), 32)
+        for q in range(2):
+            v_ref[q, dst, :] = spec_ref[q, src, :]
+            vl_ref[q, dst, :] = spec_ref[q, src, gap:]
+            vr_ref[q, dst, :] = spec_ref[q, src, :RIM]
+
+
+def ends(pos, spectrum):
+    vm = pl.BlockSpec(memory_space=pltpu.VMEM)
+    sizes = ((TILE, RIM), (TILE, RIM), (RIM, TILE), (RIM, RIM), (RIM, RIM))
+    return pl.pallas_call(
+        ends_body,
+        out_shape=[jax.ShapeDtypeStruct((2,) + size, BF16) for size in sizes],
+        in_specs=[pl.BlockSpec(memory_space=pltpu.SMEM), vm],
+        out_specs=[vm] * 5,
+        cost_estimate=FREE,
+        name="ends",
+    )(pos, spectrum)
+
+
+def cut_body(pos_ref, l_ref, r_ref, *refs):
+    out_ref = refs[-1]
     row = (1 - pos_ref[2]) * (TILE - RIM)
 
     @pl.loop(0, RIM // 32)
@@ -414,19 +433,20 @@
             out_ref[q, dst, RIM:2 * RIM] = r_ref[q, src, :]
 
 
-def cut(pos, l, r, token):
+def cut(pos, l, r, *tokens):
     vm = pl.BlockSpec(memory_space=pltpu.VMEM)
     return pl.pallas_call(
         cut_body,
         out_shape=jax.ShapeDtypeStruct((2, RIM, 2 * RIM), BF16),
-        in_specs=[pl.BlockSpec(memory_space=pltpu.SMEM), vm, vm, pl.BlockSpec(memory_space=pl.ANY)],
+        in_specs=[pl.BlockSpec(memory_space=pltpu.SMEM), vm, vm] + [pl.BlockSpec(memory_space=pl.ANY)] * len(tokens),
         out_specs=vm,
-        cost_estimate=pl.CostEstimate(flops=0, bytes_accessed=4 * 2**20, transcendentals=0),
+        cost_estimate=FREE,
         name="cut",
-    )(pos, l, r, token)
-
-
-def sides_body(pos_ref, l_ref, r_ref, i_ref, first_ref, second_ref, ol_ref, or_ref):
+    )(pos, l, r, *tokens)
+
+
+def sides_body(pos_ref, l_ref, r_ref, i_ref, *refs):
+    ol_ref, or_ref = refs[-2:]
     at = (1 - pos_ref[2]) * (TILE - RIM)
     for mid_ref, col, out_ref in ((l_ref, 0, ol_ref), (r_ref, RIM + TILE, or_ref)):
         out_ref[...] = mid_ref[...]
@@ -440,17 +460,17 @@
                 out_ref[q, dst, :] = (mid_ref[q, dst, :].astype(F32) + add).astype(BF16)
 
 
-def sides(pos, l, r, i, first, second):
+def sides(pos, l, r, i, *tokens):
     vm = pl.BlockSpec(memory_space=pltpu.VMEM)
     return pl.pallas_call(
         sides_body,
         out_shape=[jax.ShapeDtypeStruct(l.shape, BF16)] * 2,
-        in_specs=[pl.BlockSpec(memory_space=pltpu.SMEM)] + [vm] * 3 + [pl.BlockSpec(memory_space=pl.ANY)] * 2,
+        in_specs=[pl.BlockSpec(memory_space=pltpu.SMEM)] + [vm] * 3 + [pl.BlockSpec(memory_space=pl.ANY)] * len(tokens),
         out_specs=[vm] * 2,
         compiler_params=pltpu.CompilerParams(vmem_limit_bytes=32 * 2**20),
-        cost_estimate=pl.CostEstimate(flops=2**20, bytes_accessed=6 * 2**20, transcendentals=0),
+        cost_estimate=FREE,
         name="sides",
-    )(pos, l, r, i, first, second)
+    )(pos, l, r, i, *tokens)
 
 
 def tile_body(pos_ref, c_ref, i_ref, v_ref, l_ref, r_ref, vl_ref, vr_ref, out_ref):
@@ -483,7 +503,7 @@
         in_specs=[pl.BlockSpec(memory_space=pltpu.SMEM)] + [block(x) for x in parts],
         out_specs=pl.BlockSpec((1, TILE, TILE), lambda q: (q, 0, 0)),
         compiler_params=pltpu.CompilerParams(vmem_limit_bytes=32 * 2**20),
-        cost_estimate=pl.CostEstimate(flops=2**21, bytes_accessed=8 * 2**20, transcendentals=0),
+        cost_estimate=FREE,
         name="tile_sum",
     )(pos, *parts)
 
@@ -502,7 +522,7 @@
         out_shape=jax.ShapeDtypeStruct((8, 8, 16, N), F32),
         in_specs=[rows, rows],
         out_specs=pl.BlockSpec((8, 1, 16, N), lambda i: (0, i, 0, 0)),
-        cost_estimate=pl.CostEstimate(flops=N * N, bytes_accessed=12 * 2**20, transcendentals=0),
+        cost_estimate=FREE,
         name="pair_sum",
     )(mine, other)
 
@@ -518,7 +538,7 @@
         out_shape=jax.ShapeDtypeStruct(x.shape, x.dtype),
         in_specs=[vm, pl.BlockSpec(memory_space=pl.ANY)],
         out_specs=vm,
-        cost_estimate=pl.CostEstimate(flops=0, bytes_accessed=2**20, transcendentals=0),
+        cost_estimate=FREE,
         name="after",
     )(x, token)
 
@@ -553,15 +573,16 @@
     vert_l, vert_r = both(vert, left, n_kx), both(vert, right, n_kx)
     swap = [(0, 1), (1, 0)]
 
-    in_l = lax.ppermute(spectrum[:, :, TILE - RIM:], KX, right)
-    in_r = lax.ppermute(spectrum[:, :, :RIM], KX, left)
-    amp, out_v, out_vl, out_vr = order(pos, amplitude, tb["perm"], spectrum)
+    out_l, out_r, out_v, out_vl, out_vr = ends(pos, spectrum)
+    in_l = lax.ppermute(out_l, KX, right)
+    in_r = lax.ppermute(out_r, KX, left)
     in_v = lax.ppermute(out_v, KY, vert)
     in_vl = lax.ppermute(out_vl, ALL, vert_r)
     in_vr = lax.ppermute(out_vr, ALL, vert_l)
     in_i = lax.ppermute(spectrum, "core", swap)
-    pupil = turn(pos, pupil, out_v)
-    in_c = lax.ppermute(cut(pos, in_l, in_r, pupil), "core", swap)
+    amp = order(amplitude, tb["perm"])
+    pupil = turn(pos, pupil)
+    in_c = lax.ppermute(cut(pos, in_l, in_r, pupil, amp, in_v, in_vl, in_vr), "core", swap)
     pieces = (spectrum, in_l, in_r, in_v, in_vl, in_vr, in_i, in_c)
     c, l, r, v, vl, vr, i, mine, other = led(pos, pieces, pupil, amp, tb)
 
@@ -570,7 +591,7 @@
     vl = lax.ppermute(vl, ALL, vert_l)
     vr = lax.ppermute(vr, ALL, vert_r)
     total = pair_sum(mine, lax.ppermute(other, "core", swap))
-    l, r = sides(pos, l, r, i, total, v)
+    l, r = sides(pos, l, r, i, v, total)
     l = lax.ppermute(l, KX, left)
     r = lax.ppermute(r, KX, right)
     tile = tile_sum(pos, (c, i, v, l, r, vl, vr))

time: 284 us -> 265 us (0.933)
  waiting for transfers between devices: 98.6 us -> 72.8 us
    ppermute x1, waiting for transfers between devices: 38.8 us -> 22.3 us  [body(): in_vl = lax.ppermute(out_vl, ALL, vert_r)]
    ppermute x3, waiting for transfers between devices: 10.8 us -> 0.34 us  [the longest x1 0.33 us: body(): lax.ppermute(cut(pos, in_l, in_r, pupil, amp, in_v, in_vl, in_vr), 'core'...]
    ppermute x1, waiting for transfers between devices: 0.01 us -> 3.71 us  [body(): in_i = lax.ppermute(spectrum, 'core', swap)]
    unnamed x43 -> x47, local copies, waits for them, and re-layouts: 13.8 us -> 16.2 us
    pallas_call x1 -> x2, Pallas kernels: 5.41 us -> 7.86 us  [the longest x1 4.52 us: order(): pl.pallas_call(order_body, out_shape=jax.ShapeDtypeStruct((N, N), BF16),...]
  transfers between devices with their start and end apart: 15 -> 15, of which waited for: 7 -> 8; matrix products, arithmetic and copies ran while one was open for 0% -> 0% of each run, Pallas kernels for 6% -> 6%
where the time goes in v3:
time: 265 us; the launch traced here: 263 us
  Pallas kernels  84.1 us (32%)
  waiting for transfers between devices  72.8 us (27%)
  starting transfers between devices  38.3 us (14%)
  blocking collectives  34.4 us (13%)
  local copies, waits for them, and re-layouts  17.6 us (7%)
  between operations  15.5 us (6%)
    pallas_call x1, Pallas kernels, led(): pl.pallas_call(led_body, out_shape=rims(TILE) + rims(RIM) + [jax.ShapeDty...  53.3 us
    all_to_all x1, blocking collectives, body(): total = lax.all_to_all(after(total, tile), ('x', 'yh', 'yl'), 0, 0)  34.4 us
    ppermute x1, waiting for transfers between devices, body(): v = lax.ppermute(v, KY, vert)  32.9 us
    ppermute x1, waiting for transfers between devices, body(): in_vl = lax.ppermute(out_vl, ALL, vert_r)  22.3 us
    unnamed x47, local copies, waits for them, and re-layouts  16.2 us
    ppermute x1, starting transfers between devices, body(): vr = lax.ppermute(vr, ALL, vert_r)  12.2 us
    pallas_call x1, Pallas kernels, turn(): pl.pallas_call(turn_body, out_shape=jax.ShapeDtypeStruct((2, N, N), BF16)...  7.75 us
    pallas_call x1, Pallas kernels, pair_sum(): pl.pallas_call(pair_body, grid=(8,), out_shape=jax.ShapeDtypeStruct((8, 8...  7.01 us
  transfers between devices with their start and end apart: 15, of which 8 were waited for; matrix products, arithmetic and copies ran while one was open for 0% of the time, Pallas kernels for 6%

profile of v3, /device:TPU:1, one launch (start us, length us, event | category | flops | bytes accessed | tf_op | source)
XLA Modules:
  0.0 263.3 jit_solution(4667081007477302975)
XLA Ops:
  7.2 0.0 reduce-scatter.2.cloned.1.call-start
  7.2 1.3 fusion
  9.8 0.6 pad_add_fusion.pos_ref
  10.4 3.3 %ends.1 = (bf16[2,512,384]{2,1,0:T(8,128)(2,1)}, bf16[2,512,384]{2,1,0:T(8,128)(2,1)}, bf16[2,384,512]{2,1,0:T(8,128)(2,1)}, bf16[2,384,384]{2,1,0:T(8,128)(2,1)}, bf16[2,384,384]{2,1,0:T(8,128)(2,1)}) custom-call(s32[3]{0:T(128)} %pad_add_fusion.pos_ref, bf16[2,512,512]{2,1,0:T(8,128)(2,1)} %own_ref.1), custom_call_target="tpu_custom_call" | custom-call | flops 1 | bytes 1 | tf_op jit(solution)/shard_map/ends/pallas_call | solution.py:413
  13.7 4.1 %collective-permute-start = (bf16[2,512,384]{2,1,0:T(8,128)(2,1)}, bf16[2,512,384]{2,1,0:T(8,128)(2,1)S(1)}, u32[]{:S(2)}, u32[]{:S(2)}) collective-permute-start(bf16[2,512,384]{2,1,0:T(8,128)(2,1)} %get-tuple-element.18), channel_id=1, source_target_pairs={{0,1},{1,2},{2,3},{3,4},{4,5},{5,6},{6,7},{7,8},{8,9},{9,10},{10,1... | collective-permute-start | bytes 2359304 | tf_op jit(solution)/shard_map/ppermute | solution.py:577
  17.8 1.3 collective-permute-start.1
  19.1 5.4 %collective-permute-start.2 = (bf16[2,384,512]{2,1,0:T(8,128)(2,1)}, bf16[2,384,512]{2,1,0:T(8,128)(2,1)S(1)}, u32[]{:S(2)}, u32[]{:S(2)}) collective-permute-start(bf16[2,384,512]{2,1,0:T(8,128)(2,1)} %get-tuple-element.20), channel_id=1, source_target_pairs={{16,32},{48,64},{80,96},{112,128},{144,160},{176,192},{208,224},{3... | collective-permute-start | bytes 2359304 | tf_op jit(solution)/shard_map/ppermute | solution.py:579
  24.5 3.3 %collective-permute-start.3 = (bf16[2,384,384]{2,1,0:T(8,128)(2,1)}, bf16[2,384,384]{2,1,0:T(8,128)(2,1)S(1)}, u32[]{:S(2)}, u32[]{:S(2)}) collective-permute-start(bf16[2,384,384]{2,1,0:T(8,128)(2,1)} %get-tuple-element.21), channel_id=1, source_target_pairs={{16,33},{17,34},{18,35},{19,36},{20,37},{21,38},{22,39},{23,40},{2... | collective-permute-start | bytes 1769480 | tf_op jit(solution)/shard_map/ppermute | solution.py:580
  27.8 1.3 collective-permute-start.4
  29.1 0.0 copy-start.3
  29.1 2.2 copy-done.3
  31.3 0.6 copy-done.9
  31.9 7.7 %turn.1.refs_0_.pup_ref = bf16[2,1024,1024]{2,1,0:T(8,128)(2,1)S(1)} custom-call(s32[3]{0:T(128)S(1)} %copy-done.9, bf16[2,1024,1024]{2,1,0:T(8,128)(2,1)S(1)} %copy-done.3), custom_call_target="tpu_custom_call" | custom-call | flops 1 | bytes 1 | tf_op jit(solution)/shard_map/turn/pallas_call | solution.py:362
  39.6 0.0 copy-start.1
  39.6 2.0 copy-done.1
  41.6 0.0 copy-done.5
  41.6 4.5 %order.1.refs_1_.ampl_ref = bf16[1024,1024]{1,0:T(8,128)(2,1)S(1)} custom-call(bf16[1024,1024]{1,0:T(8,128)(2,1)S(1)} %copy-done.4, bf16[1024,1024]{1,0:T(8,128)(2,1)S(1)} %copy-done.5), custom_call_target="tpu_custom_call" | custom-call | flops 1 | bytes 1 | tf_op jit(solution)/shard_map/order/pallas_call | solution.py:383
  46.1 0.0 copy-start.2
  46.1 1.3 copy-done.2
  47.4 22.3 %collective-permute-done.3.refs_3_.vl_ref = bf16[2,384,384]{2,1,0:T(8,128)(2,1)S(1)} collective-permute-done((bf16[2,384,384]{2,1,0:T(8,128)(2,1)}, bf16[2,384,384]{2,1,0:T(8,128)(2,1)S(1)}, u32[]{:S(2)}, u32[]{:S(2)}) %collective-permute-start.3) | collective-permute-done | bytes 589856 | tf_op jit(solution)/shard_map/ppermute | solution.py:580
  69.7 0.0 collective-permute-done.4.refs_4_.vr_ref
  69.7 0.0 collective-permute-done.l_ref
  69.7 0.0 collective-permute-done.1.r_ref
  69.7 0.8 copy-done.16
  70.5 0.2 copy-done.17
  70.7 0.0 collective-permute-done.2.refs_2_.v_ref
  70.7 0.3 copy-done.13
  71.0 0.6 copy-done.14
  71.6 0.9 copy-done.15
  72.5 2.6 %cut.1 = bf16[2,384,768]{2,1,0:T(8,128)(2,1)} custom-call(s32[3]{0:T(128)} %pad_add_fusion.pos_ref, bf16[2,512,384]{2,1,0:T(8,128)(2,1)} %copy-done.13, bf16[2,512,384]{2,1,0:T(8,128)(2,1)} %copy-done.14, bf16[2,1024,1024]{2,1,0:T(8,128)(2,1)} %copy-done.1, bf16[1024,1024]{1,0:T(8,128)(2,1)} %copy-done.2, bf16[2,384,512]{2,1,0:T(8,128)(2,1)} %copy-done.15, ...), custom_call_target="tpu_custom_call" | custom-call | flops 1 | bytes 1 | tf_op jit(solution)/shard_map/cut/pallas_call | solution.py:438
  75.2 0.0 collective-permute-start.6
  75.2 0.5 collective-permute-start.5
  75.7 3.7 %collective-permute-done.5.i_ref = bf16[2,512,512]{2,1,0:T(8,128)(2,1)S(1)} collective-permute-done((bf16[2,512,512]{2,1,0:T(8,128)(2,1)S(1)}, bf16[2,512,512]{2,1,0:T(8,128)(2,1)S(1)}, u32[]{:S(2)}, u32[]{:S(2)}) %collective-permute-start.5) | collective-permute-done | bytes 1048608 | tf_op jit(solution)/shard_map/ppermute | solution.py:582
  79.4 0.3 collective-permute-done.6.c_ref
  79.7 0.6 copy-done.20
  80.4 1.0 copy-done.19
  81.4 53.3 %led.1 = (bf16[2,512,512]{2,1,0:T(8,128)(2,1)}, bf16[2,512,384]{2,1,0:T(8,128)(2,1)}, bf16[2,512,384]{2,1,0:T(8,128)(2,1)}, bf16[2,384,512]{2,1,0:T(8,128)(2,1)}...) custom-call(s32[3]{0:T(128)} %pad_add_fusion.pos_ref, ...), custom_call_target="tpu_custom_call" | custom-call | flops 12999999488 | bytes 31457280 | tf_op jit(solution)/shard_map/led/pallas_call | solution.py:308
  134.8 0.2 collective-permute-start.9
  135.0 4.2 %collective-permute-done.9.other_ref = bf16[1024,1024]{1,0:T(8,128)(2,1)S(1)} collective-permute-done((bf16[1024,1024]{1,0:T(8,128)(2,1)}, bf16[1024,1024]{1,0:T(8,128)(2,1)S(1)}, u32[]{:S(2)}, u32[]{:S(2)}) %collective-permute-start.9) | collective-permute-done | bytes 2097184 | tf_op jit(solution)/shard_map/ppermute | solution.py:593
  139.2 1.3 copy-done.11
  140.5 7.0 %pair_sum.1.refs_1_ = f32[8,8,16,1024]{3,2,1,0:T(8,128)} custom-call(f32[1024,1024]{1,0:T(8,128)} %get-tuple-element.28.mine_ref, bf16[1024,1024]{1,0:T(8,128)(2,1)} %copy-done.11), custom_call_target="tpu_custom_call" | custom-call | flops 1 | bytes 1 | tf_op jit(solution)/shard_map/pair_sum/pallas_call | solution.py:519
  147.6 0.0 reduce-scatter.2.cloned.1.call-update
  147.6 1.5 copy-done.18
  149.1 0.1 collective-permute-start.7
  149.2 3.3 %collective-permute-start.8 = (bf16[2,384,512]{2,1,0:T(8,128)(2,1)}, bf16[2,384,512]{2,1,0:T(8,128)(2,1)S(1)}, u32[]{:S(2)}, u32[]{:S(2)}) collective-permute-start(bf16[2,384,512]{2,1,0:T(8,128)(2,1)} %get-tuple-element.25), channel_id=1, source_target_pairs={{16,32},{48,64},{80,96},{112,128},{144,160},{176,192},{208,224},{3... | collective-permute-start | bytes 2359304 | tf_op jit(solution)/shard_map/ppermute | solution.py:590
  152.5 32.9 %collective-permute-done.8.refs_0_.v_ref = bf16[2,384,512]{2,1,0:T(8,128)(2,1)S(1)} collective-permute-done((bf16[2,384,512]{2,1,0:T(8,128)(2,1)}, bf16[2,384,512]{2,1,0:T(8,128)(2,1)S(1)}, u32[]{:S(2)}, u32[]{:S(2)}) %collective-permute-start.8) | collective-permute-done | bytes 786464 | tf_op jit(solution)/shard_map/ppermute | solution.py:590
  185.4 0.0 collective-permute-done.7.i_ref
  185.4 0.0 copy-done.10
  185.5 2.2 copy-done
  187.7 1.1 sides.1
  188.8 1.3 collective-permute-start.10
  190.1 4.0 %collective-permute-start.11 = (bf16[2,512,384]{2,1,0:T(8,128)(2,1)S(1)}, bf16[2,512,384]{2,1,0:T(8,128)(2,1)S(1)}, u32[]{:S(2)}, u32[]{:S(2)}) collective-permute-start(bf16[2,512,384]{2,1,0:T(8,128)(2,1)S(1)} %get-tuple-element.31), channel_id=1, source_target_pairs={{0,1},{1,2},{2,3},{3,4},{4,5},{5,6},{6,7},{7,8},{8,9},{9,10},{10,1... | collective-permute-start | bytes 2359304 | tf_op jit(solution)/shard_map/ppermute | solution.py:596
  194.1 1.3 collective-permute-start.12
  195.5 12.2 %collective-permute-start.13 = (bf16[2,384,384]{2,1,0:T(8,128)(2,1)S(1)}, bf16[2,384,384]{2,1,0:T(8,128)(2,1)S(1)}, u32[]{:S(2)}, u32[]{:S(2)}) collective-permute-start(bf16[2,384,384]{2,1,0:T(8,128)(2,1)S(1)} %copy-done.21), channel_id=1, source_target_pairs={{16,33},{17,34},{18,35},{19,36},{20,37},{21,38},{22,39},{23,40},{2... | collective-permute-start | bytes 1769480 | tf_op jit(solution)/shard_map/ppermute | solution.py:592
  207.6 6.0 %collective-permute-done.12.vl_ref = bf16[2,384,384]{2,1,0:T(8,128)(2,1)S(1)} collective-permute-done((bf16[2,384,384]{2,1,0:T(8,128)(2,1)S(1)}, bf16[2,384,384]{2,1,0:T(8,128)(2,1)S(1)}, u32[]{:S(2)}, u32[]{:S(2)}) %collective-permute-start.12) | collective-permute-done | bytes 589856 | tf_op jit(solution)/shard_map/ppermute | solution.py:591
  213.6 2.1 collective-permute-done.13.vr_ref
  215.7 0.0 collective-permute-done.10.l_ref
  215.7 0.0 collective-permute-done.11.r_ref
  215.8 0.0 copy-done.6
  215.8 2.6 tile_sum.1.token_ref
  218.3 1.2 reduce-scatter.2.cloned.1.call-done
  219.5 1.9 after.1
  221.4 34.4 %all_to_all.5 = f32[16,8,1024]{2,1,0:T(8,128)S(1)} all-to-all(f32[16,8,1024]{2,1,0:T(8,128)} %after.1), channel_id=1, replica_groups=mesh['x'=4,'yh'=2,'core'=2,'z'=8,'yl'=2] {'x','yh','yl'}, dimensions={0} | all-to-all | bytes 1048576 | tf_op jit(solution)/shard_map/all_to_all | solution.py:599
  255.9 0.6 copy.15
  (27 shorter events, 0.1 us)
Async XLA Ops:
  7.2 212.4 %reduce-scatter.2.cloned.1.call-start = ((), (), s32[]{:S(2)}) async-start(), calls=%async_computation.2 | async-start | bytes 4718592 | tf_op jit(solution)/shard_map/reduce_scatter | solution.py:598
  13.7 56.0 %collective-permute-start = (bf16[2,512,384]{2,1,0:T(8,128)(2,1)}, bf16[2,512,384]{2,1,0:T(8,128)(2,1)S(1)}, u32[]{:S(2)}, u32[]{:S(2)}) collective-permute-start(bf16[2,512,384]{2,1,0:T(8,128)(2,1)} %get-tuple-element.18), channel_id=1, source_target_pairs={{0,1},{1,2},{2,3},{3,4},{4,5},{5,6},{6,7},{7,8},{8,9},{9,10},{10,1... | collective-permute-start | bytes 2359304 | tf_op jit(solution)/shard_map/ppermute | solution.py:577
  17.8 51.9 %collective-permute-start.1 = (bf16[2,512,384]{2,1,0:T(8,128)(2,1)}, bf16[2,512,384]{2,1,0:T(8,128)(2,1)S(1)}, u32[]{:S(2)}, u32[]{:S(2)}) collective-permute-start(bf16[2,512,384]{2,1,0:T(8,128)(2,1)} %get-tuple-element.19), channel_id=1, source_target_pairs={{1,0},{2,1},{3,2},{4,3},{5,4},{6,5},{7,6},{8,7},{9,8},{10,9},{11,1... | collective-permute-start | bytes 2359304 | tf_op jit(solution)/shard_map/ppermute | solution.py:578
  19.1 51.6 %collective-permute-start.2 = (bf16[2,384,512]{2,1,0:T(8,128)(2,1)}, bf16[2,384,512]{2,1,0:T(8,128)(2,1)S(1)}, u32[]{:S(2)}, u32[]{:S(2)}) collective-permute-start(bf16[2,384,512]{2,1,0:T(8,128)(2,1)} %get-tuple-element.20), channel_id=1, source_target_pairs={{16,32},{48,64},{80,96},{112,128},{144,160},{176,192},{208,224},{3... | collective-permute-start | bytes 2359304 | tf_op jit(solution)/shard_map/ppermute | solution.py:579
  24.5 45.2 %collective-permute-start.3 = (bf16[2,384,384]{2,1,0:T(8,128)(2,1)}, bf16[2,384,384]{2,1,0:T(8,128)(2,1)S(1)}, u32[]{:S(2)}, u32[]{:S(2)}) collective-permute-start(bf16[2,384,384]{2,1,0:T(8,128)(2,1)} %get-tuple-element.21), channel_id=1, source_target_pairs={{16,33},{17,34},{18,35},{19,36},{20,37},{21,38},{22,39},{23,40},{2... | collective-permute-start | bytes 1769480 | tf_op jit(solution)/shard_map/ppermute | solution.py:580
  27.8 42.0 %collective-permute-start.4 = (bf16[2,384,384]{2,1,0:T(8,128)(2,1)}, bf16[2,384,384]{2,1,0:T(8,128)(2,1)S(1)}, u32[]{:S(2)}, u32[]{:S(2)}) collective-permute-start(bf16[2,384,384]{2,1,0:T(8,128)(2,1)} %get-tuple-element.22), channel_id=1, source_target_pairs={{17,32},{18,33},{19,34},{20,35},{21,36},{22,37},{23,38},{24,39},{2... | collective-permute-start | bytes 1769480 | tf_op jit(solution)/shard_map/ppermute | solution.py:581
  29.1 2.2 copy-start.3
  31.3 0.6 copy-start.9
  31.9 9.7 %copy-start.4 = (bf16[1024,1024]{1,0:T(8,128)(2,1)S(1)}, bf16[1024,1024]{1,0:T(8,128)(2,1)}, u32[]{:S(2)}) copy-start(bf16[1024,1024]{1,0:T(8,128)(2,1)} %amp_ref.1) | copy-start | bytes 6291460
  31.9 9.7 %copy-start.5 = (bf16[1024,1024]{1,0:T(8,128)(2,1)S(1)}, bf16[1024,1024]{1,0:T(8,128)(2,1)}, u32[]{:S(2)}) copy-start(bf16[1024,1024]{1,0:T(8,128)(2,1)} %constant.54.clone.perm_ref) | copy-start | bytes 6291460
  39.6 2.0 copy-start.1
  46.1 1.3 copy-start.2
  47.4 27.7 %copy-start.12 = (bf16[2,512,512]{2,1,0:T(8,128)(2,1)S(1)}, bf16[2,512,512]{2,1,0:T(8,128)(2,1)}, u32[]{:S(2)}) copy-start(bf16[2,512,512]{2,1,0:T(8,128)(2,1)} %own_ref.1) | copy-start | bytes 3145732
  69.7 0.8 copy-start.16
  69.7 1.0 copy-start.17
  69.7 1.3 copy-start.13
  70.7 0.9 copy-start.14
  71.6 0.9 copy-start.15
  75.2 4.6 %collective-permute-start.6 = (bf16[2,384,768]{2,1,0:T(8,128)(2,1)}, bf16[2,384,768]{2,1,0:T(8,128)(2,1)S(1)}, u32[]{:S(2)}, u32[]{:S(2)}) collective-permute-start(bf16[2,384,768]{2,1,0:T(8,128)(2,1)} %cut.1), channel_id=1, source_target_pairs={{0,16},{16,0},{1,17},{17,1},{2,18},{18,2},{3,19},{19,3},{4,20},{20... | collective-permute-start | bytes 3538952 | tf_op jit(solution)/shard_map/ppermute | solution.py:585
  75.2 4.2 %collective-permute-start.5 = (bf16[2,512,512]{2,1,0:T(8,128)(2,1)S(1)}, bf16[2,512,512]{2,1,0:T(8,128)(2,1)S(1)}, u32[]{:S(2)}, u32[]{:S(2)}) collective-permute-start(bf16[2,512,512]{2,1,0:T(8,128)(2,1)S(1)} %copy-done.12), channel_id=1, source_target_pairs={{0,16},{16,0},{1,17},{17,1},{2,18},{18,2},{3,19},{19,3},{4,20},{20... | collective-permute-start | bytes 3145736 | tf_op jit(solution)/shard_map/ppermute | solution.py:582
  79.4 1.0 copy-start.20
  80.4 1.0 copy-start.19
  134.8 4.5 %collective-permute-start.9 = (bf16[1024,1024]{1,0:T(8,128)(2,1)}, bf16[1024,1024]{1,0:T(8,128)(2,1)S(1)}, u32[]{:S(2)}, u32[]{:S(2)}) collective-permute-start(bf16[1024,1024]{1,0:T(8,128)(2,1)} %get-tuple-element.29), channel_id=1, source_target_pairs={{0,16},{16,0},{1,17},{17,1},{2,18},{18,2},{3,19},{19,3},{4,20},{20... | collective-permute-start | bytes 6291464 | tf_op jit(solution)/shard_map/ppermute | solution.py:593
  139.2 1.3 copy-start.11
  147.5 1.5 copy-start.18
  147.5 37.9 %copy-start.7 = (bf16[2,512,384]{2,1,0:T(8,128)(2,1)S(1)}, bf16[2,512,384]{2,1,0:T(8,128)(2,1)}, u32[]{:S(2)}) copy-start(bf16[2,512,384]{2,1,0:T(8,128)(2,1)} %get-tuple-element.26.l_ref) | copy-start | bytes 2359300
  147.6 37.9 %copy-start.8 = (bf16[2,512,384]{2,1,0:T(8,128)(2,1)S(1)}, bf16[2,512,384]{2,1,0:T(8,128)(2,1)}, u32[]{:S(2)}) copy-start(bf16[2,512,384]{2,1,0:T(8,128)(2,1)} %get-tuple-element.27.r_ref) | copy-start | bytes 2359300
  147.6 37.9 %copy-start.10 = (s32[3]{0:T(128)S(1)}, s32[3]{0:T(128)}, u32[]{:S(2)}) copy-start(s32[3]{0:T(128)} %pad_add_fusion.pos_ref) | copy-start | bytes 40
  149.1 36.3 %collective-permute-start.7 = (bf16[2,384,1280]{2,1,0:T(8,128)(2,1)S(1)}, bf16[2,384,1280]{2,1,0:T(8,128)(2,1)S(1)}, u32[]{:S(2)}, u32[]{:S(2)}) collective-permute-start(bf16[2,384,1280]{2,1,0:T(8,128)(2,1)S(1)} %copy-done.18), channel_id=1, source_target_pairs={{0,16},{16,0},{1,17},{17,1},{2,18},{18,2},{3,19},{19,3},{4,20},{20... | collective-permute-start | bytes 5898248 | tf_op jit(solution)/shard_map/ppermute | solution.py:589
  149.2 36.2 %collective-permute-start.8 = (bf16[2,384,512]{2,1,0:T(8,128)(2,1)}, bf16[2,384,512]{2,1,0:T(8,128)(2,1)S(1)}, u32[]{:S(2)}, u32[]{:S(2)}) collective-permute-start(bf16[2,384,512]{2,1,0:T(8,128)(2,1)} %get-tuple-element.25), channel_id=1, source_target_pairs={{16,32},{48,64},{80,96},{112,128},{144,160},{176,192},{208,224},{3... | collective-permute-start | bytes 2359304 | tf_op jit(solution)/shard_map/ppermute | solution.py:590
  185.4 2.2 copy-start
  187.7 6.5 %copy-start.22 = (bf16[2,384,384]{2,1,0:T(8,128)(2,1)S(1)}, bf16[2,384,384]{2,1,0:T(8,128)(2,1)}, u32[]{:S(2)}) copy-start(bf16[2,384,384]{2,1,0:T(8,128)(2,1)} %get-tuple-element.32) | copy-start | bytes 1769476
  187.7 7.8 %copy-start.21 = (bf16[2,384,384]{2,1,0:T(8,128)(2,1)S(1)}, bf16[2,384,384]{2,1,0:T(8,128)(2,1)}, u32[]{:S(2)}) copy-start(bf16[2,384,384]{2,1,0:T(8,128)(2,1)} %get-tuple-element.33) | copy-start | bytes 1769476
  187.7 28.1 %copy-start.6 = (bf16[2,512,512]{2,1,0:T(8,128)(2,1)S(1)}, bf16[2,512,512]{2,1,0:T(8,128)(2,1)}, u32[]{:S(2)}) copy-start(bf16[2,512,512]{2,1,0:T(8,128)(2,1)} %get-tuple-element.23.c_ref) | copy-start | bytes 3145732
  188.8 27.0 %collective-permute-start.10 = (bf16[2,512,384]{2,1,0:T(8,128)(2,1)S(1)}, bf16[2,512,384]{2,1,0:T(8,128)(2,1)S(1)}, u32[]{:S(2)}, u32[]{:S(2)}) collective-permute-start(bf16[2,512,384]{2,1,0:T(8,128)(2,1)S(1)} %get-tuple-element.30), channel_id=1, source_target_pairs={{1,0},{2,1},{3,2},{4,3},{5,4},{6,5},{7,6},{8,7},{9,8},{10,9},{11,1... | collective-permute-start | bytes 2359304 | tf_op jit(solution)/shard_map/ppermute | solution.py:595
  190.1 25.7 %collective-permute-start.11 = (bf16[2,512,384]{2,1,0:T(8,128)(2,1)S(1)}, bf16[2,512,384]{2,1,0:T(8,128)(2,1)S(1)}, u32[]{:S(2)}, u32[]{:S(2)}) collective-permute-start(bf16[2,512,384]{2,1,0:T(8,128)(2,1)S(1)} %get-tuple-element.31), channel_id=1, source_target_pairs={{0,1},{1,2},{2,3},{3,4},{4,5},{5,6},{6,7},{7,8},{8,9},{9,10},{10,1... | collective-permute-start | bytes 2359304 | tf_op jit(solution)/shard_map/ppermute | solution.py:596
  194.1 19.5 %collective-permute-start.12 = (bf16[2,384,384]{2,1,0:T(8,128)(2,1)S(1)}, bf16[2,384,384]{2,1,0:T(8,128)(2,1)S(1)}, u32[]{:S(2)}, u32[]{:S(2)}) collective-permute-start(bf16[2,384,384]{2,1,0:T(8,128)(2,1)S(1)} %copy-done.22), channel_id=1, source_target_pairs={{17,32},{18,33},{19,34},{20,35},{21,36},{22,37},{23,38},{24,39},{2... | collective-permute-start | bytes 1769480 | tf_op jit(solution)/shard_map/ppermute | solution.py:591
  195.5 20.3 %collective-permute-start.13 = (bf16[2,384,384]{2,1,0:T(8,128)(2,1)S(1)}, bf16[2,384,384]{2,1,0:T(8,128)(2,1)S(1)}, u32[]{:S(2)}, u32[]{:S(2)}) collective-permute-start(bf16[2,384,384]{2,1,0:T(8,128)(2,1)S(1)} %copy-done.21), channel_id=1, source_target_pairs={{16,33},{17,34},{18,35},{19,36},{20,37},{21,38},{22,39},{23,40},{2... | collective-permute-start | bytes 1769480 | tf_op jit(solution)/shard_map/ppermute | solution.py:592
Sparse Core Ops, SparseCore 0:
  147.7 71.7 reduce-scatter.1

commit v4 on v3

--- a/solution.py
+++ b/solution.py
@@ -86,15 +86,15 @@
     return jnp.dot(a, b, preferred_element_type=F32)
 
 
-RB = 256
+RB = 64
 CB = 256
 
 
 def led_body(
-    pos_ref, own_ref, l_ref, r_ref, v_ref, vl_ref, vr_ref, i_ref, c_ref, pup_ref, ampl_ref,
+    pos_ref, own_ref, l_ref, r_ref, v_ref, vl_ref, vr_ref, i_ref, c_ref, p_ref, amp_ref,
     li_ref, lf_ref, ri_ref, rf_ref, twl_ref, twr_ref,
     oc_ref, ol_ref, or_ref, ov_ref, ovl_ref, ovr_ref, oi_ref, mine_ref, other_ref,
-    w_ref, p_ref, amp_ref, a_ref, s_ref, s2_ref, z_ref, z2_ref, to_ref, tm_ref, in_sem, out_sem,
+    w_ref, a_ref, s_refs, z_refs, s2_refs, z2_refs, to_ref, tm_ref, in_sem, out_sem,
 ):
     r0, c0, core = pos_ref[0], pos_ref[1], pos_ref[2]
     outer = pl.multiple_of((RIM + TILE) * core, 128)
@@ -109,11 +109,8 @@
     sides = [w_ref.at[:, pl.ds(inner, RIM), pl.ds(col, wide)] for col, wide in ((RIM, TILE), (0, RIM), (RIM + TILE, RIM))]
     loads = [pltpu.make_async_copy(x, y, in_sem.at[k]) for k, (x, y) in enumerate(zip(arrivals, places + sides))]
     places.append(w_ref.at[:, pl.ds(inner, RIM), :])
-    loads.append(pltpu.make_async_copy(pup_ref, p_ref, in_sem.at[9]))
-    amp_load = pltpu.make_async_copy(ampl_ref, amp_ref, in_sem.at[10])
     for load in loads:
         load.start()
-    amp_load.start()
 
     def lane_tile(k):
         return pl.ds(k * 128, 128)
@@ -123,7 +120,7 @@
     for load in loads:
         load.wait()
 
-    @pl.loop(0, REGION // 16)
+    @pl.loop(0, REGION // 16, unroll=4)
     def _(i):
         rows = pl.ds(pl.multiple_of(i * 16, 16), 16)
         for q in range(2):
@@ -131,7 +128,7 @@
                 here, there = w_ref[q, rows, lane_tile(a)].astype(F32), w_ref[q, rows, lane_tile(a + 8)].astype(F32)
                 w_ref[q, rows, lane_tile(a)] = jnp.where(lane + 128 * a >= c0, here, there).astype(BF16)
 
-    @pl.loop(0, 16)
+    @pl.loop(0, 16, unroll=2)
     def _(i):
         k = pl.multiple_of(i * 16, 16)
         for q in range(2):
@@ -140,12 +137,17 @@
                 there = w_ref[q, pl.ds(k + N, 16), lane_tile(a)].astype(F32)
                 w_ref[q, pl.ds(k, 16), lane_tile(a)] = jnp.where(line + k >= r0, here, there).astype(BF16)
 
-    @pl.loop(0, N // RB)
-    def _(rb):
-        @pl.loop(0, RB // 16)
-        def _(i):
-            rows = pl.ds(pl.multiple_of(rb * RB + i * 16, 16), 16)
-            sub = pl.ds(pl.multiple_of(i * 16, 16), 16)
+    def put(ref, at, hs, yr, yi, step):
+        (hr, lr), (hi, li) = split(yr), split(yi)
+        for k, part in enumerate((hr, hi, lr, li)):
+            if step is None:
+                ref[at, k * 128:(k + 1) * 128] = part
+            else:
+                ref[at[0], pl.ds(at[1] + k * step, 16), hs] = part
+
+    def first_vpu(n, s_ref):
+        for i in range(RB // 16):
+            rows = pl.ds(pl.multiple_of(n * RB + i * 16, 16), 16)
             x = []
             for a in range(8):
                 pr, pi = p_ref[0, rows, lane_tile(a)].astype(F32), p_ref[1, rows, lane_tile(a)].astype(F32)
@@ -155,55 +157,51 @@
                 if c > 0:
                     tr, ti = twl_ref[0, c], twl_ref[1, c]
                     yr, yi = yr * tr - yi * ti, yr * ti + yi * tr
-                (hr, lr), (hi, li) = split(yr), split(yi)
-                s_ref[c, sub, 0:128] = hr
-                s_ref[c, sub, 128:256] = hi
-                s_ref[c, sub, 256:384] = lr
-                s_ref[c, sub, 384:512] = li
-
-        rows = pl.ds(pl.multiple_of(rb * RB, RB), RB)
+                put(s_ref, pl.ds(c * RB + i * 16, 16), None, yr, yi, None)
+
+    def first_mxu(n, s_ref):
+        rows = pl.ds(pl.multiple_of(n * RB, RB), RB)
+        acc = dot(s_ref[...], li_ref[0:512]) + dot(s_ref[:, 0:256], li_ref[512:768])
         for c in range(8):
-            acc = dot(s_ref[c], li_ref[0:512]) + dot(s_ref[c, :, 0:256], li_ref[512:768])
-            a_ref[0, rows, lane_tile(c)] = acc[:, 0:128]
-            a_ref[1, rows, lane_tile(c)] = acc[:, 128:256]
-
-    amp_load.wait()
-
-    @pl.loop(0, N // CB)
-    def _(cb):
-        def lanes(h):
-            return pl.ds(pl.multiple_of(cb * CB + h * 128, 128), 128)
-
-        @pl.loop(0, 8)
-        def _(i):
-            b = pl.multiple_of(i * 16, 16)
-            for h in range(CB // 128):
-                hs = pl.ds(h * 128, 128)
-                x = [tuple(a_ref[q, pl.ds(a * 128 + b, 16), lanes(h)] for q in range(2)) for a in range(8)]
-                for c, (yr, yi) in enumerate(fft8(x, 1)):
-                    if c > 0:
-                        tr, ti = twr_ref[0, c, pl.ds(b, 16)], twr_ref[1, c, pl.ds(b, 16)]
-                        yr, yi = yr * tr - yi * ti, yr * ti + yi * tr
-                    (hr, lr), (hi, li) = split(yr), split(yi)
-                    s2_ref[c, pl.ds(b, 16), hs] = hr
-                    s2_ref[c, pl.ds(128 + b, 16), hs] = hi
-                    s2_ref[c, pl.ds(256 + b, 16), hs] = lr
-                    s2_ref[c, pl.ds(384 + b, 16), hs] = li
-
+            a_ref[0, rows, lane_tile(c)] = acc[c * RB:(c + 1) * RB, 0:128]
+            a_ref[1, rows, lane_tile(c)] = acc[c * RB:(c + 1) * RB, 128:256]
+
+    last = N // RB - 1
+    first_vpu(0, s_refs[0])
+
+    @pl.loop(0, N // RB // 2)
+    def _(j):
+        first_mxu(2 * j, s_refs[0])
+        first_vpu(2 * j + 1, s_refs[1])
+        first_mxu(2 * j + 1, s_refs[1])
+        first_vpu(jnp.minimum(2 * j + 2, last), s_refs[0])
+
+    def lanes(cb, h):
+        return pl.ds(pl.multiple_of(cb * CB + h * 128, 128), 128)
+
+    def second_in(cb, part, s2_ref):
+        b = pl.multiple_of(part * 16, 16)
+        for h in range(CB // 128):
+            x = [tuple(a_ref[q, pl.ds(a * 128 + b, 16), lanes(cb, h)] for q in range(2)) for a in range(8)]
+            for c, (yr, yi) in enumerate(fft8(x, 1)):
+                if c > 0:
+                    tr, ti = twr_ref[0, c, pl.ds(b, 16)], twr_ref[1, c, pl.ds(b, 16)]
+                    yr, yi = yr * tr - yi * ti, yr * ti + yi * tr
+                put(s2_ref, (c, b), pl.ds(h * 128, 128), yr, yi, 128)
+
+    def second_mxu(cb, c, s2_ref, z2_ref):
         wide = pl.ds(pl.multiple_of(cb * CB, CB), CB)
-        for c in range(8):
-            acc = dot(ri_ref[:, 0:512], s2_ref[c]) + dot(ri_ref[:, 512:768], s2_ref[c, 0:256])
-            ir, ii = acc[0:128], acc[128:256]
-            amp = amp_ref[pl.ds(c * 128, 128), wide].astype(F32)
-            keep = 1.0 - amp * lax.rsqrt(jnp.maximum(ir * ir + ii * ii, FLOOR2))
-            (hr, lr), (hi, li) = split(ir * keep), split(ii * keep)
-            s3 = jnp.concatenate([hr, hi, lr, li], axis=0)
-            acc = dot(rf_ref[:, 0:512], s3) + dot(rf_ref[:, 512:768], s3[0:256])
-            z2_ref[c] = acc
-
-        @pl.loop(0, 16)
-        def _(i):
-            b = pl.multiple_of(i * 8, 8)
+        acc = dot(ri_ref[:, 0:512], s2_ref[c]) + dot(ri_ref[:, 512:768], s2_ref[c, 0:256])
+        ir, ii = acc[0:128], acc[128:256]
+        amp = amp_ref[pl.ds(pl.multiple_of(c * 128, 128), 128), wide].astype(F32)
+        keep = 1.0 - amp * lax.rsqrt(jnp.maximum(ir * ir + ii * ii, FLOOR2))
+        (hr, lr), (hi, li) = split(ir * keep), split(ii * keep)
+        s3 = jnp.concatenate([hr, hi, lr, li], axis=0)
+        z2_ref[c] = dot(rf_ref[:, 0:512], s3) + dot(rf_ref[:, 512:768], s3[0:256])
+
+    def second_out(cb, part, z2_ref):
+        for half in range(2):
+            b = pl.multiple_of(part * 16 + half * 8, 8)
             for h in range(CB // 128):
                 hs = pl.ds(h * 128, 128)
                 x = []
@@ -214,27 +212,41 @@
                         zr, zi = zr * tr + zi * ti, zi * tr - zr * ti
                     x.append((zr, zi))
                 for a, (yr, yi) in enumerate(fft8(x, -1)):
-                    a_ref[0, pl.ds(a * 128 + b, 8), lanes(h)] = yr
-                    a_ref[1, pl.ds(a * 128 + b, 8), lanes(h)] = yi
+                    a_ref[0, pl.ds(a * 128 + b, 8), lanes(cb, h)] = yr
+                    a_ref[1, pl.ds(a * 128 + b, 8), lanes(cb, h)] = yi
+
+    @pl.loop(0, 8)
+    def _(c):
+        second_in(0, c, s2_refs[0])
+
+    for cb in range(N // CB):
+        @pl.loop(0, 8, unroll=8)
+        def _(c):
+            if cb + 1 < N // CB:
+                second_in(cb + 1, c, s2_refs[(cb + 1) % 2])
+            second_mxu(cb, c, s2_refs[cb % 2], z2_refs[cb % 2])
+            if cb > 0:
+                second_out(cb - 1, c, z2_refs[(cb - 1) % 2])
+
+    @pl.loop(0, 8)
+    def _(c):
+        second_out(N // CB - 1, c, z2_refs[(N // CB - 1) % 2])
 
     back = jnp.bitwise_and(N - c0, N - 1)
 
-    @pl.loop(0, N // RB)
-    def _(rb):
-        rows = pl.ds(pl.multiple_of(rb * RB, RB), RB)
+    def third_mxu(n, s_ref, z_ref):
+        rows = pl.ds(pl.multiple_of(n * RB, RB), RB)
         for c in range(8):
-            (hr, lr), (hi, li) = split(a_ref[0, rows, lane_tile(c)]), split(a_ref[1, rows, lane_tile(c)])
-            h = jnp.concatenate([hr, hi], axis=1)
-            acc = dot(h, lf_ref[0:256]) + dot(jnp.concatenate([lr, li], axis=1), lf_ref[256:512])
-            z_ref[c] = acc + dot(h, lf_ref[512:768])
-
-        @pl.loop(0, RB // 16)
-        def _(i):
-            rows = pl.ds(pl.multiple_of(rb * RB + i * 16, 16), 16)
-            sub = pl.ds(pl.multiple_of(i * 16, 16), 16)
+            put(s_ref, pl.ds(c * RB, RB), None, a_ref[0, rows, lane_tile(c)], a_ref[1, rows, lane_tile(c)], None)
+        z_ref[...] = dot(s_ref[...], lf_ref[0:512]) + dot(s_ref[:, 0:256], lf_ref[512:768])
+
+    def third_vpu(n, z_ref):
+        for i in range(RB // 16):
+            rows = pl.ds(pl.multiple_of(n * RB + i * 16, 16), 16)
             x = []
             for c in range(8):
-                zr, zi = z_ref[c, sub, 0:128], z_ref[c, sub, 128:256]
+                sub = pl.ds(c * RB + i * 16, 16)
+                zr, zi = z_ref[sub, 0:128], z_ref[sub, 128:256]
                 if c > 0:
                     tr, ti = twl_ref[0, c], twl_ref[1, c]
                     zr, zi = zr * tr + zi * ti, zi * tr - zr * ti
@@ -249,7 +261,20 @@
             for q in range(2):
                 a_ref[q, rows, :] = pltpu.roll(a_ref[q, rows, :], back, 1)
 
-    @pl.loop(0, N // 16)
+    third_mxu(0, s_refs[0], z_refs[0])
+
+    @pl.loop(0, N // RB // 2 - 1)
+    def _(j):
+        third_mxu(2 * j + 1, s_refs[1], z_refs[1])
+        third_vpu(2 * j, z_refs[0])
+        third_mxu(2 * j + 2, s_refs[0], z_refs[0])
+        third_vpu(2 * j + 1, z_refs[1])
+
+    third_mxu(last, s_refs[1], z_refs[1])
+    third_vpu(last - 1, z_refs[0])
+    third_vpu(last, z_refs[1])
+
+    @pl.loop(0, N // 16, unroll=4)
     def _(i):
         rows = pl.ds(pl.multiple_of(i * 16, 16), 16)
         for q in range(2):
@@ -259,7 +284,7 @@
                 w_ref[q, rows, lane_tile(a)] = jnp.where(ahead, x, 0.0).astype(BF16)
                 w_ref[q, rows, lane_tile(a + 8)] = jnp.where(ahead, 0.0, x).astype(BF16)
 
-    @pl.loop(0, 16)
+    @pl.loop(0, 16, unroll=2)
     def _(i):
         k = pl.multiple_of(i * 16, 16)
         for q in range(2):
@@ -309,23 +334,21 @@
         led_body,
         out_shape=rims(TILE) + rims(RIM) + [jax.ShapeDtypeStruct((2, RIM, REGION), BF16)]
         + [jax.ShapeDtypeStruct((N, N), F32), jax.ShapeDtypeStruct((N, N), BF16)],
-        in_specs=[pl.BlockSpec(memory_space=pltpu.SMEM)] + [hbm] * 10 + [vm] * 6,
+        in_specs=[pl.BlockSpec(memory_space=pltpu.SMEM)] + [hbm] * 8 + [vm] * 8,
         out_specs=[hbm] * 9,
         scratch_shapes=[
             pltpu.VMEM((2, REGION, REGION), BF16),
-            pltpu.VMEM((2, N, N), BF16),
-            pltpu.VMEM((N, N), BF16),
             pltpu.VMEM((2, N + 264, N), F32),
-            pltpu.VMEM((8, RB, 512), BF16),
-            pltpu.VMEM((8, 512, CB), BF16),
-            pltpu.VMEM((8, RB, 256), F32),
-            pltpu.VMEM((8, 256, CB), F32),
+            [pltpu.VMEM((8 * RB, 512), BF16)] * 2,
+            [pltpu.VMEM((8 * RB, 256), F32)] * 2,
+            [pltpu.VMEM((8, 512, CB), BF16)] * 2,
+            [pltpu.VMEM((8, 256, CB), F32)] * 2,
             pltpu.VMEM((N, N), BF16),
             pltpu.VMEM((N, N), F32),
-            pltpu.SemaphoreType.DMA((11,)),
+            pltpu.SemaphoreType.DMA((9,)),
             pltpu.SemaphoreType.DMA((9,)),
         ],
-        compiler_params=pltpu.CompilerParams(vmem_limit_bytes=60 * 2**20),
+        compiler_params=pltpu.CompilerParams(vmem_limit_bytes=52 * 2**20),
         cost_estimate=pl.CostEstimate(flops=13 * 10**9, bytes_accessed=30 * 2**20, transcendentals=N * N),
         name="led",
     )(pos, *pieces, p, amp, tb["lane_inv"], tb["lane_fwd"], tb["row_inv"], tb["row_fwd"], tb["tw_lane"], tb["tw_row"])
@@ -511,35 +534,40 @@
 def pair_body(mine_ref, other_ref, out_ref):
     for z in range(8):
         rows = pl.ds(z * 16, 16)
-        out_ref[z, 0] = mine_ref[rows, :] + other_ref[rows, :].astype(F32)
+        out_ref[0, z, 0] = (mine_ref[rows, :] + other_ref[rows, :].astype(F32)).astype(BF16)
 
 
 def pair_sum(mine, other):
-    rows = pl.BlockSpec((128, N), lambda i: (i, 0))
+    rows = pl.BlockSpec((128, N), lambda x, y: (2 * x + y, 0))
     return pl.pallas_call(
         pair_body,
-        grid=(8,),
-        out_shape=jax.ShapeDtypeStruct((8, 8, 16, N), F32),
+        grid=(4, 2),
+        out_shape=jax.ShapeDtypeStruct((4, 8, 2, 16, N), BF16),
         in_specs=[rows, rows],
-        out_specs=pl.BlockSpec((8, 1, 16, N), lambda i: (0, i, 0, 0)),
+        out_specs=pl.BlockSpec((1, 8, 1, 16, N), lambda x, y: (x, 0, y, 0, 0)),
         cost_estimate=FREE,
         name="pair_sum",
     )(mine, other)
 
 
-def after_body(x_ref, token_ref, out_ref):
-    out_ref[...] = x_ref[...]
-
-
-def after(x, token):
+def gather_body(x_ref, token_ref, out_ref):
+    for i in range(2):
+        rows = pl.ds(i * 16, 16)
+        total = x_ref[0, rows, :].astype(F32)
+        for k in range(1, 32):
+            total += x_ref[k, rows, :].astype(F32)
+        out_ref[rows, :] = total
+
+
+def gather_sum(x, token):
     vm = pl.BlockSpec(memory_space=pltpu.VMEM)
     return pl.pallas_call(
-        after_body,
-        out_shape=jax.ShapeDtypeStruct(x.shape, x.dtype),
+        gather_body,
+        out_shape=jax.ShapeDtypeStruct((32, N), F32),
         in_specs=[vm, pl.BlockSpec(memory_space=pl.ANY)],
         out_specs=vm,
         cost_estimate=FREE,
-        name="after",
+        name="gather_sum",
     )(x, token)
 
 
@@ -595,8 +623,9 @@
     l = lax.ppermute(l, KX, left)
     r = lax.ppermute(r, KX, right)
     tile = tile_sum(pos, (c, i, v, l, r, vl, vr))
-    total = lax.psum_scatter(total.reshape(8, 128, N), "z", scatter_dimension=0, tiled=True).reshape(16, 8, N)
-    total = lax.all_to_all(after(total, tile), ("x", "yh", "yl"), 0, 0)
+    total = lax.all_to_all(total.reshape(32, 32, N), ("x", "z"), 0, 0)
+    total = gather_sum(total, tile).reshape(4, 8, N)
+    total = lax.all_to_all(total, ("yh", "yl"), 0, 0)
     return tile, jnp.sum(total, axis=0).reshape(-1)
 
 

time: 265 us -> 239 us (0.902)
  between operations: 15.5 us -> 2.17 us
  starting transfers between devices: 38.3 us -> 50.4 us
  Pallas kernels: 84.1 us -> 74.8 us
  waiting for transfers between devices: 72.8 us -> 63.9 us
  local copies, waits for them, and re-layouts: 17.6 us -> 14.1 us
    all_to_all x0 -> x1, starting transfers between devices: none -> 16.3 us  [body(): total = lax.all_to_all(total.reshape(32, 32, N), ('x', 'z'), 0, 0)]
    ppermute x1, waiting for transfers between devices: 32.9 us -> 20.9 us  [body(): v = lax.ppermute(v, KY, vert)]
    pallas_call x1, Pallas kernels: 53.3 us -> 43.8 us  [led(): pl.pallas_call(led_body, out_shape=rims(TILE) + rims(RIM) + [jax.ShapeDty...]
    ppermute x1, waiting for transfers between devices: 2.14 us -> 6.54 us  [body(): vr = lax.ppermute(vr, ALL, vert_r)]
    ppermute x1, starting transfers between devices: 12.2 us -> 8.15 us  [body(): vr = lax.ppermute(vr, ALL, vert_r)]
    unnamed x47 -> x51, local copies, waits for them, and re-layouts: 16.2 us -> 12.7 us
  transfers between devices with their start and end apart: 15 -> 15, of which waited for: 8 -> 7; matrix products, arithmetic and copies ran while one was open for 0% -> 0% of each run, Pallas kernels for 6% -> 7%
where the time goes in v4:
time: 239 us; the launch traced here: 238 us
  Pallas kernels  74.8 us (31%)
  waiting for transfers between devices  63.9 us (27%)
  starting transfers between devices  50.4 us (21%)
  blocking collectives  32.2 us (13%)
  local copies, waits for them, and re-layouts  14.1 us (6%)
    pallas_call x1, Pallas kernels, led(): pl.pallas_call(led_body, out_shape=rims(TILE) + rims(RIM) + [jax.ShapeDty...  43.8 us
    all_to_all x1, blocking collectives, body(): total = lax.all_to_all(total, ('yh', 'yl'), 0, 0)  32.2 us
    ppermute x1, waiting for transfers between devices, body(): in_vl = lax.ppermute(out_vl, ALL, vert_r)  22.1 us
    ppermute x1, waiting for transfers between devices, body(): v = lax.ppermute(v, KY, vert)  20.9 us
    all_to_all x1, starting transfers between devices, body(): total = lax.all_to_all(total.reshape(32, 32, N), ('x', 'z'), 0, 0)  16.3 us
    unnamed x51, local copies, waits for them, and re-layouts  12.7 us
    ppermute x1, starting transfers between devices, body(): vr = lax.ppermute(vr, ALL, vert_r)  8.15 us
    pallas_call x1, Pallas kernels, turn(): pl.pallas_call(turn_body, out_shape=jax.ShapeDtypeStruct((2, N, N), BF16)...  7.75 us
  transfers between devices with their start and end apart: 15, of which 7 were waited for; matrix products, arithmetic and copies ran while one was open for 0% of the time, Pallas kernels for 7%

profile of v4, /device:TPU:1, one launch (start us, length us, event | category | flops | bytes accessed | tf_op | source)
XLA Modules:
  0.0 238.1 jit_solution(11997445949231563912)
XLA Ops:
  0.6 1.3 fusion
  3.3 0.7 pad_add_fusion.pos_ref
  3.9 3.3 %ends.1 = (bf16[2,512,384]{2,1,0:T(8,128)(2,1)}, bf16[2,512,384]{2,1,0:T(8,128)(2,1)}, bf16[2,384,512]{2,1,0:T(8,128)(2,1)}, bf16[2,384,384]{2,1,0:T(8,128)(2,1)}, bf16[2,384,384]{2,1,0:T(8,128)(2,1)}) custom-call(s32[3]{0:T(128)} %pad_add_fusion.pos_ref, bf16[2,512,512]{2,1,0:T(8,128)(2,1)} %own_ref.1), custom_call_target="tpu_custom_call" | custom-call | flops 1 | bytes 1 | tf_op jit(solution)/shard_map/ends/pallas_call | solution.py:436
  7.3 4.1 %collective-permute-start = (bf16[2,512,384]{2,1,0:T(8,128)(2,1)}, bf16[2,512,384]{2,1,0:T(8,128)(2,1)S(1)}, u32[]{:S(2)}, u32[]{:S(2)}) collective-permute-start(bf16[2,512,384]{2,1,0:T(8,128)(2,1)} %get-tuple-element.18), channel_id=1, source_target_pairs={{0,1},{1,2},{2,3},{3,4},{4,5},{5,6},{6,7},{7,8},{8,9},{9,10},{10,1... | collective-permute-start | bytes 2359304 | tf_op jit(solution)/shard_map/ppermute | solution.py:605
  11.4 1.3 collective-permute-start.1
  12.7 5.4 %collective-permute-start.2 = (bf16[2,384,512]{2,1,0:T(8,128)(2,1)}, bf16[2,384,512]{2,1,0:T(8,128)(2,1)}, u32[]{:S(2)}, u32[]{:S(2)}) collective-permute-start(bf16[2,384,512]{2,1,0:T(8,128)(2,1)} %get-tuple-element.20), channel_id=1, source_target_pairs={{16,32},{48,64},{80,96},{112,128},{144,160},{176,192},{208,224},{3... | collective-permute-start | bytes 2359304 | tf_op jit(solution)/shard_map/ppermute | solution.py:607
  18.0 3.3 %collective-permute-start.3 = (bf16[2,384,384]{2,1,0:T(8,128)(2,1)}, bf16[2,384,384]{2,1,0:T(8,128)(2,1)S(1)}, u32[]{:S(2)}, u32[]{:S(2)}) collective-permute-start(bf16[2,384,384]{2,1,0:T(8,128)(2,1)} %get-tuple-element.21), channel_id=1, source_target_pairs={{16,33},{17,34},{18,35},{19,36},{20,37},{21,38},{22,39},{23,40},{2... | collective-permute-start | bytes 1769480 | tf_op jit(solution)/shard_map/ppermute | solution.py:608
  21.3 1.3 collective-permute-start.4
  22.6 0.0 copy-start.3
  22.6 2.2 copy-done.3
  24.8 0.7 copy-done.9
  25.5 7.7 %turn.1.refs_0_.p_ref = bf16[2,1024,1024]{2,1,0:T(8,128)(2,1)S(1)} custom-call(s32[3]{0:T(128)S(1)} %copy-done.9, bf16[2,1024,1024]{2,1,0:T(8,128)(2,1)S(1)} %copy-done.3), custom_call_target="tpu_custom_call" | custom-call | flops 1 | bytes 1 | tf_op jit(solution)/shard_map/turn/pallas_call | solution.py:385
  33.2 0.0 copy-start.1
  33.3 2.0 copy-done.1
  35.2 0.0 copy-done.4
  35.2 0.0 copy-done.5
  35.2 4.5 %order.1.refs_1_.amp_ref = bf16[1024,1024]{1,0:T(8,128)(2,1)S(1)} custom-call(bf16[1024,1024]{1,0:T(8,128)(2,1)S(1)} %copy-done.4, bf16[1024,1024]{1,0:T(8,128)(2,1)S(1)} %copy-done.5), custom_call_target="tpu_custom_call" | custom-call | flops 1 | bytes 1 | tf_op jit(solution)/shard_map/order/pallas_call | solution.py:406
  39.8 0.0 copy-start.2
  39.8 1.3 copy-done.2
  41.1 0.0 copy-start.13
  41.1 0.0 copy-start.14
  41.1 0.0 copy-start.15
  41.1 22.1 %collective-permute-done.3.refs_3_.vl_ref = bf16[2,384,384]{2,1,0:T(8,128)(2,1)S(1)} collective-permute-done((bf16[2,384,384]{2,1,0:T(8,128)(2,1)}, bf16[2,384,384]{2,1,0:T(8,128)(2,1)S(1)}, u32[]{:S(2)}, u32[]{:S(2)}) %collective-permute-start.3) | collective-permute-done | bytes 589856 | tf_op jit(solution)/shard_map/ppermute | solution.py:608
  63.3 0.0 collective-permute-done.4.refs_4_.vr_ref
  63.3 0.0 collective-permute-done.l_ref
  63.3 0.8 copy-done.19
  64.1 0.0 collective-permute-done.1.r_ref
  64.1 0.2 copy-done.20
  64.3 0.0 collective-permute-done.2.refs_2_.v_ref
  64.3 0.8 copy-done.18
  65.0 2.6 %cut.1 = bf16[2,384,768]{2,1,0:T(8,128)(2,1)} custom-call(s32[3]{0:T(128)} %pad_add_fusion.pos_ref, bf16[2,512,384]{2,1,0:T(8,128)(2,1)} %copy-done.18, bf16[2,512,384]{2,1,0:T(8,128)(2,1)} %collective-permute-done.1.r_ref, bf16[2,1024,1024]{2,1,0:T(8,128)(2,1)} %copy-done.1, bf16[1024,1024]{1,0:T(8,128)(2,1)} %copy-done.2, ...), custom_call_target="tpu_custom_call" | custom-call | flops 1 | bytes 1 | tf_op jit(solution)/shard_map/cut/pallas_call | solution.py:461
  67.7 0.0 collective-permute-start.6
  67.7 0.5 collective-permute-start.5
  68.2 3.7 %collective-permute-done.5.i_ref = bf16[2,512,512]{2,1,0:T(8,128)(2,1)S(1)} collective-permute-done((bf16[2,512,512]{2,1,0:T(8,128)(2,1)S(1)}, bf16[2,512,512]{2,1,0:T(8,128)(2,1)S(1)}, u32[]{:S(2)}, u32[]{:S(2)}) %collective-permute-start.5) | collective-permute-done | bytes 1048608 | tf_op jit(solution)/shard_map/ppermute | solution.py:610
  71.9 0.3 collective-permute-done.6.c_ref
  72.2 0.7 copy-done.22
  72.9 1.0 copy-done.21
  73.9 0.0 copy-done.12
  73.9 43.8 %led.1 = (bf16[2,512,512]{2,1,0:T(8,128)(2,1)}, bf16[2,512,384]{2,1,0:T(8,128)(2,1)}, bf16[2,512,384]{2,1,0:T(8,128)(2,1)}, bf16[2,384,512]{2,1,0:T(8,128)(2,1)}...) custom-call(s32[3]{0:T(128)S(1)} %copy-done.10, ...), custom_call_target="tpu_custom_call" | custom-call | flops 12999999488 | bytes 31457280 | tf_op jit(solution)/shard_map/led/pallas_call | solution.py:333
  117.7 0.2 collective-permute-start.9
  117.9 4.2 %collective-permute-done.9.other_ref = bf16[1024,1024]{1,0:T(8,128)(2,1)S(1)} collective-permute-done((bf16[1024,1024]{1,0:T(8,128)(2,1)}, bf16[1024,1024]{1,0:T(8,128)(2,1)S(1)}, u32[]{:S(2)}, u32[]{:S(2)}) %collective-permute-start.9) | collective-permute-done | bytes 2097184 | tf_op jit(solution)/shard_map/ppermute | solution.py:621
  122.2 1.3 copy-done.16
  123.5 6.6 %pair_sum.1.refs_1_ = bf16[4,8,2,16,1024]{4,3,2,1,0:T(8,128)(2,1)} custom-call(f32[1024,1024]{1,0:T(8,128)} %get-tuple-element.28.mine_ref, bf16[1024,1024]{1,0:T(8,128)(2,1)} %copy-done.16), custom_call_target="tpu_custom_call" | custom-call | flops 1 | bytes 1 | tf_op jit(solution)/shard_map/pair_sum/pallas_call | solution.py:542
  130.1 16.3 %all-to-all-start = ((bf16[32,32,1024]{2,1,0:T(8,128)(2,1)}), bf16[32,32,1024]{2,1,0:T(8,128)(2,1)}, u32[]{:S(2)}, u32[]{:S(2)}) async-start(bf16[32,32,1024]{2,1,0:T(8,128)(2,1)} %bitcast.11), calls=%async_computation | async-start | bytes 4194304 | tf_op jit(solution)/shard_map/all_to_all | solution.py:626
  146.4 0.5 collective-permute-start.7
  146.9 2.8 %collective-permute-start.8 = (bf16[2,384,512]{2,1,0:T(8,128)(2,1)}, bf16[2,384,512]{2,1,0:T(8,128)(2,1)S(1)}, u32[]{:S(2)}, u32[]{:S(2)}) collective-permute-start(bf16[2,384,512]{2,1,0:T(8,128)(2,1)} %get-tuple-element.25), channel_id=1, source_target_pairs={{16,32},{48,64},{80,96},{112,128},{144,160},{176,192},{208,224},{3... | collective-permute-start | bytes 2359304 | tf_op jit(solution)/shard_map/ppermute | solution.py:618
  149.7 20.9 %collective-permute-done.8.refs_0_.v_ref = bf16[2,384,512]{2,1,0:T(8,128)(2,1)S(1)} collective-permute-done((bf16[2,384,512]{2,1,0:T(8,128)(2,1)}, bf16[2,384,512]{2,1,0:T(8,128)(2,1)S(1)}, u32[]{:S(2)}, u32[]{:S(2)}) %collective-permute-start.8) | collective-permute-done | bytes 786464 | tf_op jit(solution)/shard_map/ppermute | solution.py:618
  170.6 0.0 collective-permute-done.7.i_ref
  170.6 0.0 copy-done
  170.6 1.1 copy-done.8
  171.7 1.1 sides.1
  172.8 1.3 collective-permute-start.10
  174.1 4.0 %collective-permute-start.11 = (bf16[2,512,384]{2,1,0:T(8,128)(2,1)S(1)}, bf16[2,512,384]{2,1,0:T(8,128)(2,1)S(1)}, u32[]{:S(2)}, u32[]{:S(2)}) collective-permute-start(bf16[2,512,384]{2,1,0:T(8,128)(2,1)S(1)} %get-tuple-element.31), channel_id=1, source_target_pairs={{0,1},{1,2},{2,3},{3,4},{4,5},{5,6},{6,7},{7,8},{8,9},{9,10},{10,1... | collective-permute-start | bytes 2359304 | tf_op jit(solution)/shard_map/ppermute | solution.py:624
  178.2 1.3 collective-permute-start.12
  179.5 8.2 %collective-permute-start.13 = (bf16[2,384,384]{2,1,0:T(8,128)(2,1)S(1)}, bf16[2,384,384]{2,1,0:T(8,128)(2,1)S(1)}, u32[]{:S(2)}, u32[]{:S(2)}) collective-permute-start(bf16[2,384,384]{2,1,0:T(8,128)(2,1)S(1)} %copy-done.23), channel_id=1, source_target_pairs={{16,33},{17,34},{18,35},{19,36},{20,37},{21,38},{22,39},{23,40},{2... | collective-permute-start | bytes 1769480 | tf_op jit(solution)/shard_map/ppermute | solution.py:620
  187.7 6.0 %collective-permute-done.12.vl_ref = bf16[2,384,384]{2,1,0:T(8,128)(2,1)S(1)} collective-permute-done((bf16[2,384,384]{2,1,0:T(8,128)(2,1)S(1)}, bf16[2,384,384]{2,1,0:T(8,128)(2,1)S(1)}, u32[]{:S(2)}, u32[]{:S(2)}) %collective-permute-start.12) | collective-permute-done | bytes 589856 | tf_op jit(solution)/shard_map/ppermute | solution.py:619
  193.6 6.5 %collective-permute-done.13.vr_ref = bf16[2,384,384]{2,1,0:T(8,128)(2,1)S(1)} collective-permute-done((bf16[2,384,384]{2,1,0:T(8,128)(2,1)S(1)}, bf16[2,384,384]{2,1,0:T(8,128)(2,1)S(1)}, u32[]{:S(2)}, u32[]{:S(2)}) %collective-permute-start.13) | collective-permute-done | bytes 589856 | tf_op jit(solution)/shard_map/ppermute | solution.py:620
  200.2 0.0 collective-permute-done.10.l_ref
  200.2 0.0 collective-permute-done.11.r_ref
  200.2 2.6 %tile_sum.1.token_ref = f32[2,512,512]{2,1,0:T(8,128)} custom-call(s32[3]{0:T(128)S(1)} %copy-done.10, bf16[2,512,512]{2,1,0:T(8,128)(2,1)S(1)} %copy-done.6, bf16[2,384,1280]{2,1,0:T(8,128)(2,1)S(1)} %collective-permute-done.7.i_ref, bf16[2,384,512]{2,1,0:T(8,128)(2,1)S(1)} %collective-permute-done.8.refs_0_.v_ref, ...), custom_call_target="tpu_custom_call" | custom-call | flops 1 | bytes 1 | tf_op jit(solution)/shard_map/tile_sum/pallas_call | solution.py:522
  202.8 0.0 all-to-all-done.x_ref
  202.8 2.5 %gather_sum.1 = f32[32,1024]{1,0:T(8,128)} custom-call(bf16[32,32,1024]{2,1,0:T(8,128)(2,1)} %all-to-all-done.x_ref, f32[2,512,512]{2,1,0:T(8,128)} %tile_sum.1.token_ref), custom_call_target="tpu_custom_call" | custom-call | flops 1 | bytes 1 | tf_op jit(solution)/shard_map/gather_sum/pallas_call | solution.py:564
  205.3 32.2 %all_to_all.10 = f32[4,8,1024]{2,1,0:T(8,128)S(1)} all-to-all(f32[4,8,1024]{2,1,0:T(8,128)} %bitcast.12), channel_id=1, replica_groups=mesh['x'=4,'yh'=2,'core'=2,'z'=8,'yl'=2] {'yh','yl'}, dimensions={0} | all-to-all | bytes 262144 | tf_op jit(solution)/shard_map/all_to_all | solution.py:628
  237.5 0.6 copy.15
  (30 shorter events, 0.1 us)
Async XLA Ops:
  7.3 56.0 %collective-permute-start = (bf16[2,512,384]{2,1,0:T(8,128)(2,1)}, bf16[2,512,384]{2,1,0:T(8,128)(2,1)S(1)}, u32[]{:S(2)}, u32[]{:S(2)}) collective-permute-start(bf16[2,512,384]{2,1,0:T(8,128)(2,1)} %get-tuple-element.18), channel_id=1, source_target_pairs={{0,1},{1,2},{2,3},{3,4},{4,5},{5,6},{6,7},{7,8},{8,9},{9,10},{10,1... | collective-permute-start | bytes 2359304 | tf_op jit(solution)/shard_map/ppermute | solution.py:605
  11.4 52.7 %collective-permute-start.1 = (bf16[2,512,384]{2,1,0:T(8,128)(2,1)}, bf16[2,512,384]{2,1,0:T(8,128)(2,1)}, u32[]{:S(2)}, u32[]{:S(2)}) collective-permute-start(bf16[2,512,384]{2,1,0:T(8,128)(2,1)} %get-tuple-element.19), channel_id=1, source_target_pairs={{1,0},{2,1},{3,2},{4,3},{5,4},{6,5},{7,6},{8,7},{9,8},{10,9},{11,1... | collective-permute-start | bytes 2359304 | tf_op jit(solution)/shard_map/ppermute | solution.py:606
  12.7 51.6 %collective-permute-start.2 = (bf16[2,384,512]{2,1,0:T(8,128)(2,1)}, bf16[2,384,512]{2,1,0:T(8,128)(2,1)}, u32[]{:S(2)}, u32[]{:S(2)}) collective-permute-start(bf16[2,384,512]{2,1,0:T(8,128)(2,1)} %get-tuple-element.20), channel_id=1, source_target_pairs={{16,32},{48,64},{80,96},{112,128},{144,160},{176,192},{208,224},{3... | collective-permute-start | bytes 2359304 | tf_op jit(solution)/shard_map/ppermute | solution.py:607
  18.0 45.2 %collective-permute-start.3 = (bf16[2,384,384]{2,1,0:T(8,128)(2,1)}, bf16[2,384,384]{2,1,0:T(8,128)(2,1)S(1)}, u32[]{:S(2)}, u32[]{:S(2)}) collective-permute-start(bf16[2,384,384]{2,1,0:T(8,128)(2,1)} %get-tuple-element.21), channel_id=1, source_target_pairs={{16,33},{17,34},{18,35},{19,36},{20,37},{21,38},{22,39},{23,40},{2... | collective-permute-start | bytes 1769480 | tf_op jit(solution)/shard_map/ppermute | solution.py:608
  21.3 42.0 %collective-permute-start.4 = (bf16[2,384,384]{2,1,0:T(8,128)(2,1)}, bf16[2,384,384]{2,1,0:T(8,128)(2,1)S(1)}, u32[]{:S(2)}, u32[]{:S(2)}) collective-permute-start(bf16[2,384,384]{2,1,0:T(8,128)(2,1)} %get-tuple-element.22), channel_id=1, source_target_pairs={{17,32},{18,33},{19,34},{20,35},{21,36},{22,37},{23,38},{24,39},{2... | collective-permute-start | bytes 1769480 | tf_op jit(solution)/shard_map/ppermute | solution.py:609
  22.6 2.2 copy-start.3
  24.8 0.7 copy-start.9
  25.5 9.8 %copy-start.4 = (bf16[1024,1024]{1,0:T(8,128)(2,1)S(1)}, bf16[1024,1024]{1,0:T(8,128)(2,1)}, u32[]{:S(2)}) copy-start(bf16[1024,1024]{1,0:T(8,128)(2,1)} %amp_ref.1) | copy-start | bytes 6291460
  25.5 9.8 %copy-start.5 = (bf16[1024,1024]{1,0:T(8,128)(2,1)S(1)}, bf16[1024,1024]{1,0:T(8,128)(2,1)}, u32[]{:S(2)}) copy-start(bf16[1024,1024]{1,0:T(8,128)(2,1)} %constant.54.clone.perm_ref) | copy-start | bytes 6291460
  33.2 2.0 copy-start.1
  39.8 1.3 copy-start.2
  41.1 26.6 %copy-start.17 = (bf16[2,512,512]{2,1,0:T(8,128)(2,1)S(1)}, bf16[2,512,512]{2,1,0:T(8,128)(2,1)}, u32[]{:S(2)}) copy-start(bf16[2,512,512]{2,1,0:T(8,128)(2,1)} %own_ref.1) | copy-start | bytes 3145732
  41.1 32.8 %copy-start.10 = (s32[3]{0:T(128)S(1)}, s32[3]{0:T(128)}, u32[]{:S(2)}) copy-start(s32[3]{0:T(128)} %pad_add_fusion.pos_ref) | copy-start | bytes 40
  41.1 32.8 %copy-start.11 = (bf16[256,768]{1,0:T(8,128)(2,1)S(1)}, bf16[256,768]{1,0:T(8,128)(2,1)}, u32[]{:S(2)}) copy-start(bf16[256,768]{1,0:T(8,128)(2,1)} %constant.51.clone.rf_ref) | copy-start | bytes 1179652
  41.1 32.8 %copy-start.12 = (bf16[768,256]{1,0:T(8,128)(2,1)S(1)}, bf16[768,256]{1,0:T(8,128)(2,1)}, u32[]{:S(2)}) copy-start(bf16[768,256]{1,0:T(8,128)(2,1)} %constant.50.clone.lf_ref) | copy-start | bytes 1179652
  41.1 32.8 %copy-start.13 = (bf16[256,768]{1,0:T(8,128)(2,1)S(1)}, bf16[256,768]{1,0:T(8,128)(2,1)}, u32[]{:S(2)}) copy-start(bf16[256,768]{1,0:T(8,128)(2,1)} %constant.49.clone.ri_ref) | copy-start | bytes 1179652
  41.1 32.8 %copy-start.14 = (bf16[768,256]{1,0:T(8,128)(2,1)S(1)}, bf16[768,256]{1,0:T(8,128)(2,1)}, u32[]{:S(2)}) copy-start(bf16[768,256]{1,0:T(8,128)(2,1)} %constant.48.clone.li_ref) | copy-start | bytes 1179652
  41.1 32.8 %copy-start.15 = (f32[2,8,1,128]{3,2,1,0:T(1,128)S(1)}, f32[2,8,1,128]{3,2,1,0:T(1,128)}, u32[]{:S(2)}) copy-start(f32[2,8,1,128]{3,2,1,0:T(1,128)} %constant.52.clone.twl_ref) | copy-start | bytes 24580
  63.3 0.8 copy-start.19
  63.3 1.0 copy-start.20
  64.1 0.9 copy-start.18
  67.7 4.6 %collective-permute-start.6 = (bf16[2,384,768]{2,1,0:T(8,128)(2,1)}, bf16[2,384,768]{2,1,0:T(8,128)(2,1)S(1)}, u32[]{:S(2)}, u32[]{:S(2)}) collective-permute-start(bf16[2,384,768]{2,1,0:T(8,128)(2,1)} %cut.1), channel_id=1, source_target_pairs={{0,16},{16,0},{1,17},{17,1},{2,18},{18,2},{3,19},{19,3},{4,20},{20... | collective-permute-start | bytes 3538952 | tf_op jit(solution)/shard_map/ppermute | solution.py:613
  67.7 4.2 %collective-permute-start.5 = (bf16[2,512,512]{2,1,0:T(8,128)(2,1)S(1)}, bf16[2,512,512]{2,1,0:T(8,128)(2,1)S(1)}, u32[]{:S(2)}, u32[]{:S(2)}) collective-permute-start(bf16[2,512,512]{2,1,0:T(8,128)(2,1)S(1)} %copy-done.17), channel_id=1, source_target_pairs={{0,16},{16,0},{1,17},{17,1},{2,18},{18,2},{3,19},{19,3},{4,20},{20... | collective-permute-start | bytes 3145736 | tf_op jit(solution)/shard_map/ppermute | solution.py:610
  71.9 1.0 copy-start.22
  72.9 1.0 copy-start.21
  117.7 4.5 %collective-permute-start.9 = (bf16[1024,1024]{1,0:T(8,128)(2,1)}, bf16[1024,1024]{1,0:T(8,128)(2,1)S(1)}, u32[]{:S(2)}, u32[]{:S(2)}) collective-permute-start(bf16[1024,1024]{1,0:T(8,128)(2,1)} %get-tuple-element.29), channel_id=1, source_target_pairs={{0,16},{16,0},{1,17},{17,1},{2,18},{18,2},{3,19},{19,3},{4,20},{20... | collective-permute-start | bytes 6291464 | tf_op jit(solution)/shard_map/ppermute | solution.py:621
  122.2 1.3 copy-start.16
  130.0 40.5 %copy-start = (bf16[4,8,2,16,1024]{4,3,2,1,0:T(8,128)(2,1)S(1)}, bf16[4,8,2,16,1024]{4,3,2,1,0:T(8,128)(2,1)}, u32[]{:S(2)}) copy-start(bf16[4,8,2,16,1024]{4,3,2,1,0:T(8,128)(2,1)} %pair_sum.1.refs_1_) | copy-start | bytes 6291460
  130.0 40.5 %copy-start.7 = (bf16[2,512,384]{2,1,0:T(8,128)(2,1)S(1)}, bf16[2,512,384]{2,1,0:T(8,128)(2,1)}, u32[]{:S(2)}) copy-start(bf16[2,512,384]{2,1,0:T(8,128)(2,1)} %get-tuple-element.26.l_ref) | copy-start | bytes 2359300
  130.1 72.7 %all-to-all-start = ((bf16[32,32,1024]{2,1,0:T(8,128)(2,1)}), bf16[32,32,1024]{2,1,0:T(8,128)(2,1)}, u32[]{:S(2)}, u32[]{:S(2)}) async-start(bf16[32,32,1024]{2,1,0:T(8,128)(2,1)} %bitcast.11), calls=%async_computation | async-start | bytes 4194304 | tf_op jit(solution)/shard_map/all_to_all | solution.py:626
  146.4 24.2 %collective-permute-start.7 = (bf16[2,384,1280]{2,1,0:T(8,128)(2,1)}, bf16[2,384,1280]{2,1,0:T(8,128)(2,1)S(1)}, u32[]{:S(2)}, u32[]{:S(2)}) collective-permute-start(bf16[2,384,1280]{2,1,0:T(8,128)(2,1)} %get-tuple-element.24), channel_id=1, source_target_pairs={{0,16},{16,0},{1,17},{17,1},{2,18},{18,2},{3,19},{19,3},{4,20},{20... | collective-permute-start | bytes 5898248 | tf_op jit(solution)/shard_map/ppermute | solution.py:617
  146.9 23.7 %collective-permute-start.8 = (bf16[2,384,512]{2,1,0:T(8,128)(2,1)}, bf16[2,384,512]{2,1,0:T(8,128)(2,1)S(1)}, u32[]{:S(2)}, u32[]{:S(2)}) collective-permute-start(bf16[2,384,512]{2,1,0:T(8,128)(2,1)} %get-tuple-element.25), channel_id=1, source_target_pairs={{16,32},{48,64},{80,96},{112,128},{144,160},{176,192},{208,224},{3... | collective-permute-start | bytes 2359304 | tf_op jit(solution)/shard_map/ppermute | solution.py:618
  170.6 1.1 copy-start.8
  171.7 6.5 %copy-start.24 = (bf16[2,384,384]{2,1,0:T(8,128)(2,1)S(1)}, bf16[2,384,384]{2,1,0:T(8,128)(2,1)}, u32[]{:S(2)}) copy-start(bf16[2,384,384]{2,1,0:T(8,128)(2,1)} %get-tuple-element.32) | copy-start | bytes 1769476
  171.7 7.8 %copy-start.23 = (bf16[2,384,384]{2,1,0:T(8,128)(2,1)S(1)}, bf16[2,384,384]{2,1,0:T(8,128)(2,1)}, u32[]{:S(2)}) copy-start(bf16[2,384,384]{2,1,0:T(8,128)(2,1)} %get-tuple-element.33) | copy-start | bytes 1769476
  171.7 28.5 %copy-start.6 = (bf16[2,512,512]{2,1,0:T(8,128)(2,1)S(1)}, bf16[2,512,512]{2,1,0:T(8,128)(2,1)}, u32[]{:S(2)}) copy-start(bf16[2,512,512]{2,1,0:T(8,128)(2,1)} %get-tuple-element.23.c_ref) | copy-start | bytes 3145732
  172.8 27.4 %collective-permute-start.10 = (bf16[2,512,384]{2,1,0:T(8,128)(2,1)S(1)}, bf16[2,512,384]{2,1,0:T(8,128)(2,1)S(1)}, u32[]{:S(2)}, u32[]{:S(2)}) collective-permute-start(bf16[2,512,384]{2,1,0:T(8,128)(2,1)S(1)} %get-tuple-element.30), channel_id=1, source_target_pairs={{1,0},{2,1},{3,2},{4,3},{5,4},{6,5},{7,6},{8,7},{9,8},{10,9},{11,1... | collective-permute-start | bytes 2359304 | tf_op jit(solution)/shard_map/ppermute | solution.py:623
  174.1 26.1 %collective-permute-start.11 = (bf16[2,512,384]{2,1,0:T(8,128)(2,1)S(1)}, bf16[2,512,384]{2,1,0:T(8,128)(2,1)S(1)}, u32[]{:S(2)}, u32[]{:S(2)}) collective-permute-start(bf16[2,512,384]{2,1,0:T(8,128)(2,1)S(1)} %get-tuple-element.31), channel_id=1, source_target_pairs={{0,1},{1,2},{2,3},{3,4},{4,5},{5,6},{6,7},{7,8},{8,9},{9,10},{10,1... | collective-permute-start | bytes 2359304 | tf_op jit(solution)/shard_map/ppermute | solution.py:624
  178.2 15.5 %collective-permute-start.12 = (bf16[2,384,384]{2,1,0:T(8,128)(2,1)S(1)}, bf16[2,384,384]{2,1,0:T(8,128)(2,1)S(1)}, u32[]{:S(2)}, u32[]{:S(2)}) collective-permute-start(bf16[2,384,384]{2,1,0:T(8,128)(2,1)S(1)} %copy-done.24), channel_id=1, source_target_pairs={{17,32},{18,33},{19,34},{20,35},{21,36},{22,37},{23,38},{24,39},{2... | collective-permute-start | bytes 1769480 | tf_op jit(solution)/shard_map/ppermute | solution.py:619
  179.5 20.7 %collective-permute-start.13 = (bf16[2,384,384]{2,1,0:T(8,128)(2,1)S(1)}, bf16[2,384,384]{2,1,0:T(8,128)(2,1)S(1)}, u32[]{:S(2)}, u32[]{:S(2)}) collective-permute-start(bf16[2,384,384]{2,1,0:T(8,128)(2,1)S(1)} %copy-done.23), channel_id=1, source_target_pairs={{16,33},{17,34},{18,35},{19,36},{20,37},{21,38},{22,39},{23,40},{2... | collective-permute-start | bytes 1769480 | tf_op jit(solution)/shard_map/ppermute | solution.py:620

commit v5 on v4

--- a/solution.py
+++ b/solution.py
@@ -414,10 +414,8 @@
     )(amplitude, perm)
 
 
-def ends_body(pos_ref, spec_ref, l_ref, r_ref, v_ref, vl_ref, vr_ref):
+def ends_body(pos_ref, spec_ref, v_ref, vl_ref, vr_ref):
     gap = TILE - RIM
-    l_ref[...] = spec_ref[:, :, gap:]
-    r_ref[...] = spec_ref[:, :, :RIM]
     outer = pos_ref[2] * gap
 
     @pl.loop(0, RIM // 32)
@@ -432,12 +430,12 @@
 
 def ends(pos, spectrum):
     vm = pl.BlockSpec(memory_space=pltpu.VMEM)
-    sizes = ((TILE, RIM), (TILE, RIM), (RIM, TILE), (RIM, RIM), (RIM, RIM))
+    sizes = ((RIM, TILE), (RIM, RIM), (RIM, RIM))
     return pl.pallas_call(
         ends_body,
         out_shape=[jax.ShapeDtypeStruct((2,) + size, BF16) for size in sizes],
         in_specs=[pl.BlockSpec(memory_space=pltpu.SMEM), vm],
-        out_specs=[vm] * 5,
+        out_specs=[vm] * 3,
         cost_estimate=FREE,
         name="ends",
     )(pos, spectrum)
@@ -531,26 +529,30 @@
     )(pos, *parts)
 
 
-def pair_body(mine_ref, other_ref, out_ref):
-    for z in range(8):
-        rows = pl.ds(z * 16, 16)
-        out_ref[0, z, 0] = (mine_ref[rows, :] + other_ref[rows, :].astype(F32)).astype(BF16)
-
-
-def pair_sum(mine, other):
-    rows = pl.BlockSpec((128, N), lambda x, y: (2 * x + y, 0))
+def pair_body(mine_ref, other_ref, token_ref, out_ref):
+    @pl.loop(0, 4)
+    def _(x):
+        for y in range(2):
+            for z in range(8):
+                rows = pl.ds(pl.multiple_of(x * 256 + y * 128 + z * 16, 16), 16)
+                out_ref[x, z, y] = (mine_ref[rows, :] + other_ref[rows, :].astype(F32)).astype(BF16)
+
+
+def pair_sum(mine, other, token):
+    vm = pl.BlockSpec(memory_space=pltpu.VMEM)
     return pl.pallas_call(
         pair_body,
-        grid=(4, 2),
         out_shape=jax.ShapeDtypeStruct((4, 8, 2, 16, N), BF16),
-        in_specs=[rows, rows],
-        out_specs=pl.BlockSpec((1, 8, 1, 16, N), lambda x, y: (x, 0, y, 0, 0)),
+        in_specs=[vm, vm, pl.BlockSpec(memory_space=pl.ANY)],
+        out_specs=vm,
+        compiler_params=pltpu.CompilerParams(vmem_limit_bytes=24 * 2**20),
         cost_estimate=FREE,
         name="pair_sum",
-    )(mine, other)
-
-
-def gather_body(x_ref, token_ref, out_ref):
+    )(mine, other, token)
+
+
+def gather_body(x_ref, *refs):
+    out_ref = refs[-1]
     for i in range(2):
         rows = pl.ds(i * 16, 16)
         total = x_ref[0, rows, :].astype(F32)
@@ -559,16 +561,16 @@
         out_ref[rows, :] = total
 
 
-def gather_sum(x, token):
+def gather_sum(x, *tokens):
     vm = pl.BlockSpec(memory_space=pltpu.VMEM)
     return pl.pallas_call(
         gather_body,
         out_shape=jax.ShapeDtypeStruct((32, N), F32),
-        in_specs=[vm, pl.BlockSpec(memory_space=pl.ANY)],
+        in_specs=[vm] + [pl.BlockSpec(memory_space=pl.ANY)] * len(tokens),
         out_specs=vm,
         cost_estimate=FREE,
         name="gather_sum",
-    )(x, token)
+    )(x, *tokens)
 
 
 KY, KX = ("x", "yh", "core"), ("z", "yl")
@@ -601,9 +603,9 @@
     vert_l, vert_r = both(vert, left, n_kx), both(vert, right, n_kx)
     swap = [(0, 1), (1, 0)]
 
-    out_l, out_r, out_v, out_vl, out_vr = ends(pos, spectrum)
-    in_l = lax.ppermute(out_l, KX, right)
-    in_r = lax.ppermute(out_r, KX, left)
+    in_l = lax.ppermute(spectrum[:, :, TILE - RIM:], KX, right)
+    in_r = lax.ppermute(spectrum[:, :, :RIM], KX, left)
+    out_v, out_vl, out_vr = ends(pos, spectrum)
     in_v = lax.ppermute(out_v, KY, vert)
     in_vl = lax.ppermute(out_vl, ALL, vert_r)
     in_vr = lax.ppermute(out_vr, ALL, vert_l)
@@ -618,13 +620,13 @@
     v = lax.ppermute(v, KY, vert)
     vl = lax.ppermute(vl, ALL, vert_l)
     vr = lax.ppermute(vr, ALL, vert_r)
-    total = pair_sum(mine, lax.ppermute(other, "core", swap))
-    l, r = sides(pos, l, r, i, v, total)
+    total = pair_sum(mine, lax.ppermute(other, "core", swap), i)
+    l, r = sides(pos, l, r, i)
     l = lax.ppermute(l, KX, left)
     r = lax.ppermute(r, KX, right)
     tile = tile_sum(pos, (c, i, v, l, r, vl, vr))
     total = lax.all_to_all(total.reshape(32, 32, N), ("x", "z"), 0, 0)
-    total = gather_sum(total, tile).reshape(4, 8, N)
+    total = gather_sum(total, l, r, v, vl, vr).reshape(4, 8, N)
     total = lax.all_to_all(total, ("yh", "yl"), 0, 0)
     return tile, jnp.sum(total, axis=0).reshape(-1)
 

time: 239 us -> 240 us (level)
  starting transfers between devices: 50.4 us -> 83.2 us
  blocking collectives: 32.2 us -> 0 us
  local copies, waits for them, and re-layouts: 14.1 us -> 22.9 us
  Pallas kernels: 74.8 us -> 68.3 us
    all_to_all x0 -> x1, starting transfers between devices: none -> 34.1 us  [body(): total = lax.all_to_all(total, ('yh', 'yl'), 0, 0)]
    all_to_all x1 -> x0, blocking collectives: 32.2 us -> none  [body(): total = lax.all_to_all(total, ('yh', 'yl'), 0, 0)]
    ppermute x1, waiting for transfers between devices: 20.9 us -> 0.01 us  [body(): v = lax.ppermute(v, KY, vert)]
    all_to_all x1, waiting for transfers between devices: 0.01 us -> 9.82 us  [body(): total = lax.all_to_all(total.reshape(32, 32, N), ('x', 'z'), 0, 0)]
    unnamed x51 -> x63, local copies, waits for them, and re-layouts: 12.7 us -> 19.8 us
    ppermute x1, waiting for transfers between devices: 0.01 us -> 6.67 us  [body(): i = lax.ppermute(i, 'core', swap)]
    pallas_call x1, Pallas kernels: 6.56 us -> 0.35 us  [pair_sum(): pl.pallas_call(pair_body, out_shape=jax.ShapeDtypeStruct((4, 8, 2, 16, N)...]
    ppermute x1, waiting for transfers between devices: 6.54 us -> 11.3 us  [body(): vr = lax.ppermute(vr, ALL, vert_r)]
  transfers between devices with their start and end apart: 15 -> 16, of which waited for: 7 -> 8; matrix products, arithmetic and copies ran while one was open for 0% -> 1% of each run, Pallas kernels for 7% -> 8%
where the time goes in v5:
time: 240 us; the launch traced here: 239 us
  starting transfers between devices  83.2 us (35%)
  Pallas kernels  68.3 us (28%)
  waiting for transfers between devices  61.7 us (26%)
  local copies, waits for them, and re-layouts  22.9 us (10%)
    pallas_call x1, Pallas kernels, led(): pl.pallas_call(led_body, out_shape=rims(TILE) + rims(RIM) + [jax.ShapeDty...  43.7 us
    all_to_all x1, starting transfers between devices, body(): total = lax.all_to_all(total, ('yh', 'yl'), 0, 0)  34.1 us
    ppermute x1, waiting for transfers between devices, body(): in_vl = lax.ppermute(out_vl, ALL, vert_r)  21.6 us
    unnamed x63, local copies, waits for them, and re-layouts  19.8 us
    all_to_all x1, starting transfers between devices, body(): total = lax.all_to_all(total.reshape(32, 32, N), ('x', 'z'), 0, 0)  14.6 us
    ppermute x1, waiting for transfers between devices, body(): vr = lax.ppermute(vr, ALL, vert_r)  11.3 us
    all_to_all x1, waiting for transfers between devices, body(): total = lax.all_to_all(total.reshape(32, 32, N), ('x', 'z'), 0, 0)  9.82 us
    pallas_call x1, Pallas kernels, turn(): pl.pallas_call(turn_body, out_shape=jax.ShapeDtypeStruct((2, N, N), BF16)...  7.75 us
  transfers between devices with their start and end apart: 16, of which 8 were waited for; matrix products, arithmetic and copies ran while one was open for 1% of the time, Pallas kernels for 8%

profile of v5, /device:TPU:1, one launch (start us, length us, event | category | flops | bytes accessed | tf_op | source)
XLA Modules:
  0.0 239.0 jit_solution(16815123898066777988)
XLA Ops:
  0.6 2.4 %fusion = (bf16[2,512,384]{2,1,0:T(8,128)(2,1)}, bf16[2,512,384]{2,1,0:T(8,128)(2,1)S(1)}) fusion(bf16[2,512,512]{2,1,0:T(8,128)(2,1)} %own_ref.1), kind=kLoop, calls=%fused_computation.2 | loop fusion | bytes 3145728 | tf_op jit(solution)/shard_map/slice | solution.py:607
  3.1 1.3 collective-permute-start.1
  4.4 0.7 fusion.1
  6.3 0.7 pad_add_fusion.pos_ref
  7.0 5.5 %collective-permute-start = (bf16[2,512,384]{2,1,0:T(8,128)(2,1)S(1)}, bf16[2,512,384]{2,1,0:T(8,128)(2,1)}, u32[]{:S(2)}, u32[]{:S(2)}) collective-permute-start(bf16[2,512,384]{2,1,0:T(8,128)(2,1)S(1)} %get-tuple-element.31), channel_id=1, source_target_pairs={{0,1},{1,2},{2,3},{3,4},{4,5},{5,6},{6,7},{7,8},{8,9},{9,10},{10,1... | collective-permute-start | bytes 2359304 | tf_op jit(solution)/shard_map/ppermute | solution.py:606
  12.5 2.7 %ends.1 = (bf16[2,384,512]{2,1,0:T(8,128)(2,1)}, bf16[2,384,384]{2,1,0:T(8,128)(2,1)}, bf16[2,384,384]{2,1,0:T(8,128)(2,1)}) custom-call(s32[3]{0:T(128)} %pad_add_fusion.pos_ref, bf16[2,512,512]{2,1,0:T(8,128)(2,1)} %own_ref.1), custom_call_target="tpu_custom_call" | custom-call | flops 1 | bytes 1 | tf_op jit(solution)/shard_map/ends/pallas_call | solution.py:434
  15.2 6.1 %collective-permute-start.2 = (bf16[2,384,512]{2,1,0:T(8,128)(2,1)}, bf16[2,384,512]{2,1,0:T(8,128)(2,1)}, u32[]{:S(2)}, u32[]{:S(2)}) collective-permute-start(bf16[2,384,512]{2,1,0:T(8,128)(2,1)} %get-tuple-element.16), channel_id=1, source_target_pairs={{16,32},{48,64},{80,96},{112,128},{144,160},{176,192},{208,224},{3... | collective-permute-start | bytes 2359304 | tf_op jit(solution)/shard_map/ppermute | solution.py:609
  21.3 1.9 collective-permute-start.3
  23.2 1.3 collective-permute-start.4
  24.5 0.0 copy-start.3
  24.5 2.2 copy-done.3
  26.7 0.7 copy-done.18
  27.4 7.7 %turn.1.refs_0_.p_ref = bf16[2,1024,1024]{2,1,0:T(8,128)(2,1)S(1)} custom-call(s32[3]{0:T(128)S(1)} %copy-done.18, bf16[2,1024,1024]{2,1,0:T(8,128)(2,1)S(1)} %copy-done.3), custom_call_target="tpu_custom_call" | custom-call | flops 1 | bytes 1 | tf_op jit(solution)/shard_map/turn/pallas_call | solution.py:385
  35.2 2.0 copy-done
  37.1 4.5 %order.1.refs_1_.amp_ref = bf16[1024,1024]{1,0:T(8,128)(2,1)S(1)} custom-call(bf16[1024,1024]{1,0:T(8,128)(2,1)S(1)} %copy-done.13, bf16[1024,1024]{1,0:T(8,128)(2,1)S(1)} %copy-done.14), custom_call_target="tpu_custom_call" | custom-call | flops 1 | bytes 1 | tf_op jit(solution)/shard_map/order/pallas_call | solution.py:406
  41.6 0.0 copy-start.2
  41.7 1.3 copy-done.2
  43.0 0.0 copy-start.22
  43.0 0.0 copy-start.23
  43.0 0.0 copy-start.24
  43.0 21.6 %collective-permute-done.3.refs_3_.vl_ref = bf16[2,384,384]{2,1,0:T(8,128)(2,1)S(1)} collective-permute-done((bf16[2,384,384]{2,1,0:T(8,128)(2,1)}, bf16[2,384,384]{2,1,0:T(8,128)(2,1)S(1)}, u32[]{:S(2)}, u32[]{:S(2)}) %collective-permute-start.3) | collective-permute-done | bytes 589856 | tf_op jit(solution)/shard_map/ppermute | solution.py:610
  64.7 0.0 collective-permute-done.4.refs_4_.vr_ref
  64.7 0.0 collective-permute-done.1.r_ref
  64.7 0.0 collective-permute-done.l_ref
  64.7 0.8 copy-done.26
  65.5 0.2 copy-done.27
  65.7 2.6 %cut.1 = bf16[2,384,768]{2,1,0:T(8,128)(2,1)} custom-call(s32[3]{0:T(128)} %pad_add_fusion.pos_ref, bf16[2,512,384]{2,1,0:T(8,128)(2,1)} %collective-permute-done.l_ref, bf16[2,512,384]{2,1,0:T(8,128)(2,1)} %collective-permute-done.1.r_ref, bf16[2,1024,1024]{2,1,0:T(8,128)(2,1)} %copy-done, bf16[1024,1024]{1,0:T(8,128)(2,1)} %copy-done.2, ...), custom_call_target="tpu_custom_call" | custom-call | flops 1 | bytes 1 | tf_op jit(solution)/shard_map/cut/pallas_call | solution.py:459
  68.3 0.5 collective-permute-start.5
  68.8 3.7 %collective-permute-done.5.i_ref = bf16[2,512,512]{2,1,0:T(8,128)(2,1)S(1)} collective-permute-done((bf16[2,512,512]{2,1,0:T(8,128)(2,1)S(1)}, bf16[2,512,512]{2,1,0:T(8,128)(2,1)S(1)}, u32[]{:S(2)}, u32[]{:S(2)}) %collective-permute-start.5) | collective-permute-done | bytes 1048608 | tf_op jit(solution)/shard_map/ppermute | solution.py:612
  72.5 0.3 collective-permute-done.6.c_ref
  72.9 0.7 copy-done.30
  73.5 1.0 copy-done.29
  74.6 43.7 %led.1 = (bf16[2,512,512]{2,1,0:T(8,128)(2,1)}, bf16[2,512,384]{2,1,0:T(8,128)(2,1)}, bf16[2,512,384]{2,1,0:T(8,128)(2,1)}, bf16[2,384,512]{2,1,0:T(8,128)(2,1)}...) custom-call(s32[3]{0:T(128)S(1)} %copy-done.19, ...), custom_call_target="tpu_custom_call" | custom-call | flops 12999999488 | bytes 31457280 | tf_op jit(solution)/shard_map/led/pallas_call | solution.py:333
  118.3 0.2 collective-permute-start.13
  118.5 0.4 collective-permute-start.7
  118.9 6.7 %collective-permute-done.7.i_ref.token_ref = bf16[2,384,1280]{2,1,0:T(8,128)(2,1)S(1)} collective-permute-done((bf16[2,384,1280]{2,1,0:T(8,128)(2,1)}, bf16[2,384,1280]{2,1,0:T(8,128)(2,1)S(1)}, u32[]{:S(2)}, u32[]{:S(2)}) %collective-permute-start.7) | collective-permute-done | bytes 1966112 | tf_op jit(solution)/shard_map/ppermute | solution.py:619
  125.6 0.0 collective-permute-done.13.other_ref
  125.6 2.2 copy-done.4
  127.8 0.4 pair_sum.1
  128.1 0.0 copy-start.1
  128.2 1.3 copy-done.1
  129.5 14.6 %all-to-all-start = ((bf16[32,32,1024]{2,1,0:T(8,128)(2,1)}), bf16[32,32,1024]{2,1,0:T(8,128)(2,1)}, u32[]{:S(2)}, u32[]{:S(2)}) async-start(bf16[32,32,1024]{2,1,0:T(8,128)(2,1)} %bitcast.11), calls=%async_computation | async-start | bytes 4194304 | tf_op jit(solution)/shard_map/all_to_all | solution.py:628
  144.1 4.3 %collective-permute-start.8 = (bf16[2,384,512]{2,1,0:T(8,128)(2,1)}, bf16[2,384,512]{2,1,0:T(8,128)(2,1)S(1)}, u32[]{:S(2)}, u32[]{:S(2)}) collective-permute-start(bf16[2,384,512]{2,1,0:T(8,128)(2,1)} %get-tuple-element.21), channel_id=1, source_target_pairs={{16,32},{48,64},{80,96},{112,128},{144,160},{176,192},{208,224},{3... | collective-permute-start | bytes 2359304 | tf_op jit(solution)/shard_map/ppermute | solution.py:620
  148.4 1.1 copy-done.17
  149.5 1.1 sides.1
  150.6 1.3 collective-permute-start.9
  151.9 4.9 %collective-permute-start.10 = (bf16[2,512,384]{2,1,0:T(8,128)(2,1)S(1)}, bf16[2,512,384]{2,1,0:T(8,128)(2,1)}, u32[]{:S(2)}, u32[]{:S(2)}) collective-permute-start(bf16[2,512,384]{2,1,0:T(8,128)(2,1)S(1)} %get-tuple-element.25), channel_id=1, source_target_pairs={{0,1},{1,2},{2,3},{3,4},{4,5},{5,6},{6,7},{7,8},{8,9},{9,10},{10,1... | collective-permute-start | bytes 2359304 | tf_op jit(solution)/shard_map/ppermute | solution.py:626
  156.8 1.3 collective-permute-start.11
  158.1 5.5 %collective-permute-start.12 = (bf16[2,384,384]{2,1,0:T(8,128)(2,1)}, bf16[2,384,384]{2,1,0:T(8,128)(2,1)S(1)}, u32[]{:S(2)}, u32[]{:S(2)}) collective-permute-start(bf16[2,384,384]{2,1,0:T(8,128)(2,1)} %get-tuple-element.27), channel_id=1, source_target_pairs={{16,33},{17,34},{18,35},{19,36},{20,37},{21,38},{22,39},{23,40},{2... | collective-permute-start | bytes 1769480 | tf_op jit(solution)/shard_map/ppermute | solution.py:622
  163.6 6.2 %collective-permute-done.11.vl_ref.refs_3_ = bf16[2,384,384]{2,1,0:T(8,128)(2,1)S(1)} collective-permute-done((bf16[2,384,384]{2,1,0:T(8,128)(2,1)}, bf16[2,384,384]{2,1,0:T(8,128)(2,1)S(1)}, u32[]{:S(2)}, u32[]{:S(2)}) %collective-permute-start.11) | collective-permute-done | bytes 589856 | tf_op jit(solution)/shard_map/ppermute | solution.py:621
  169.8 11.3 %collective-permute-done.12.vr_ref.refs_4_ = bf16[2,384,384]{2,1,0:T(8,128)(2,1)S(1)} collective-permute-done((bf16[2,384,384]{2,1,0:T(8,128)(2,1)}, bf16[2,384,384]{2,1,0:T(8,128)(2,1)S(1)}, u32[]{:S(2)}, u32[]{:S(2)}) %collective-permute-start.12) | collective-permute-done | bytes 589856 | tf_op jit(solution)/shard_map/ppermute | solution.py:622
  181.2 0.0 collective-permute-done.8.v_ref.refs_2_
  181.2 2.0 collective-permute-done.9.l_ref.refs_0_
  183.2 9.8 %all-to-all-done.x_ref = bf16[32,32,1024]{2,1,0:T(8,128)(2,1)} async-done(((bf16[32,32,1024]{2,1,0:T(8,128)(2,1)}), bf16[32,32,1024]{2,1,0:T(8,128)(2,1)}, u32[]{:S(2)}, u32[]{:S(2)}) %all-to-all-start) | async-done | bytes 2097184 | tf_op jit(solution)/shard_map/all_to_all | solution.py:628
  193.0 2.5 %gather_sum.1 = f32[32,1024]{1,0:T(8,128)} custom-call(bf16[32,32,1024]{2,1,0:T(8,128)(2,1)} %all-to-all-done.x_ref, bf16[2,512,384]{2,1,0:T(8,128)(2,1)} %copy-done.7, bf16[2,512,384]{2,1,0:T(8,128)(2,1)} %collective-permute-done.10.r_ref.refs_1_, bf16[2,384,512]{2,1,0:T(8,128)(2,1)} %copy-done.5, bf16[2,384,384]{2,1,0:T(8,128)(2,1)} %copy-done.9, ...), custom_call_target="tpu_custom_call" | custom-call | flops 1 | bytes 1 | tf_op jit(solution)/shard_map/gather_sum/pallas_call | solution.py:566
  195.6 34.1 %all-to-all-start.1 = ((f32[4,8,1024]{2,1,0:T(8,128)}), f32[4,8,1024]{2,1,0:T(8,128)S(1)}, u32[]{:S(2)}, u32[]{:S(2)}) async-start(f32[4,8,1024]{2,1,0:T(8,128)} %bitcast.12), calls=%async_computation.1 | async-start | bytes 262144 | tf_op jit(solution)/shard_map/all_to_all | solution.py:630
  229.7 1.1 copy-done.6
  230.8 1.1 copy-done.8
  232.0 1.1 copy-done.10
  233.0 1.1 copy-done.12
  234.1 1.2 copy-done.15
  235.3 3.0 %tile_sum.1 = f32[2,512,512]{2,1,0:T(8,128)} custom-call(s32[3]{0:T(128)S(1)} %copy-done.19, bf16[2,512,512]{2,1,0:T(8,128)(2,1)S(1)} %copy-done.15, bf16[2,384,1280]{2,1,0:T(8,128)(2,1)S(1)} %collective-permute-done.7.i_ref.token_ref, bf16[2,384,512]{2,1,0:T(8,128)(2,1)S(1)} %copy-done.6, bf16[2,512,384]{2,1,0:T(8,128)(2,1)S(1)} %copy-done.8, ...), custom_call_target="tpu_custom_call" | custom-call | flops 1 | bytes 1 | tf_op jit(solution)/shard_map/tile_sum/pallas_call | solution.py:520
  238.3 0.0 all-to-all-done.1
  238.3 0.6 copy.15
  (44 shorter events, 0.1 us)
Async XLA Ops:
  0.6 3.8 %copy-start.28 = (s32[1,1,2]{2,1,0:T(1,128)S(1)}, s32[1,1,2]{2,1,0:T(1,128)}, u32[]{:S(2)}) copy-start(s32[1,1,2]{2,1,0:T(1,128)} %param.14) | copy-start | bytes 28
  3.1 61.6 %collective-permute-start.1 = (bf16[2,512,384]{2,1,0:T(8,128)(2,1)}, bf16[2,512,384]{2,1,0:T(8,128)(2,1)}, u32[]{:S(2)}, u32[]{:S(2)}) collective-permute-start(bf16[2,512,384]{2,1,0:T(8,128)(2,1)} %get-tuple-element.30), channel_id=1, source_target_pairs={{1,0},{2,1},{3,2},{4,3},{5,4},{6,5},{7,6},{8,7},{9,8},{10,9},{11,1... | collective-permute-start | bytes 2359304 | tf_op jit(solution)/shard_map/ppermute | solution.py:607
  7.0 57.7 %collective-permute-start = (bf16[2,512,384]{2,1,0:T(8,128)(2,1)S(1)}, bf16[2,512,384]{2,1,0:T(8,128)(2,1)}, u32[]{:S(2)}, u32[]{:S(2)}) collective-permute-start(bf16[2,512,384]{2,1,0:T(8,128)(2,1)S(1)} %get-tuple-element.31), channel_id=1, source_target_pairs={{0,1},{1,2},{2,3},{3,4},{4,5},{5,6},{6,7},{7,8},{8,9},{9,10},{10,1... | collective-permute-start | bytes 2359304 | tf_op jit(solution)/shard_map/ppermute | solution.py:606
  15.2 50.5 %collective-permute-start.2 = (bf16[2,384,512]{2,1,0:T(8,128)(2,1)}, bf16[2,384,512]{2,1,0:T(8,128)(2,1)}, u32[]{:S(2)}, u32[]{:S(2)}) collective-permute-start(bf16[2,384,512]{2,1,0:T(8,128)(2,1)} %get-tuple-element.16), channel_id=1, source_target_pairs={{16,32},{48,64},{80,96},{112,128},{144,160},{176,192},{208,224},{3... | collective-permute-start | bytes 2359304 | tf_op jit(solution)/shard_map/ppermute | solution.py:609
  21.3 43.3 %collective-permute-start.3 = (bf16[2,384,384]{2,1,0:T(8,128)(2,1)}, bf16[2,384,384]{2,1,0:T(8,128)(2,1)S(1)}, u32[]{:S(2)}, u32[]{:S(2)}) collective-permute-start(bf16[2,384,384]{2,1,0:T(8,128)(2,1)} %get-tuple-element.17), channel_id=1, source_target_pairs={{16,33},{17,34},{18,35},{19,36},{20,37},{21,38},{22,39},{23,40},{2... | collective-permute-start | bytes 1769480 | tf_op jit(solution)/shard_map/ppermute | solution.py:610
  23.2 41.4 %collective-permute-start.4 = (bf16[2,384,384]{2,1,0:T(8,128)(2,1)}, bf16[2,384,384]{2,1,0:T(8,128)(2,1)S(1)}, u32[]{:S(2)}, u32[]{:S(2)}) collective-permute-start(bf16[2,384,384]{2,1,0:T(8,128)(2,1)} %get-tuple-element.18), channel_id=1, source_target_pairs={{17,32},{18,33},{19,34},{20,35},{21,36},{22,37},{23,38},{24,39},{2... | collective-permute-start | bytes 1769480 | tf_op jit(solution)/shard_map/ppermute | solution.py:611
  24.5 2.2 copy-start.3
  26.7 0.7 copy-start.18
  27.4 9.7 %copy-start.13 = (bf16[1024,1024]{1,0:T(8,128)(2,1)S(1)}, bf16[1024,1024]{1,0:T(8,128)(2,1)}, u32[]{:S(2)}) copy-start(bf16[1024,1024]{1,0:T(8,128)(2,1)} %amp_ref.1) | copy-start | bytes 6291460
  27.4 9.7 %copy-start.14 = (bf16[1024,1024]{1,0:T(8,128)(2,1)S(1)}, bf16[1024,1024]{1,0:T(8,128)(2,1)}, u32[]{:S(2)}) copy-start(bf16[1024,1024]{1,0:T(8,128)(2,1)} %constant.54.clone.perm_ref) | copy-start | bytes 6291460
  35.1 2.0 copy-start
  41.6 1.3 copy-start.2
  43.0 25.3 %copy-start.25 = (bf16[2,512,512]{2,1,0:T(8,128)(2,1)S(1)}, bf16[2,512,512]{2,1,0:T(8,128)(2,1)}, u32[]{:S(2)}) copy-start(bf16[2,512,512]{2,1,0:T(8,128)(2,1)} %own_ref.1) | copy-start | bytes 3145732
  43.0 31.6 %copy-start.19 = (s32[3]{0:T(128)S(1)}, s32[3]{0:T(128)}, u32[]{:S(2)}) copy-start(s32[3]{0:T(128)} %pad_add_fusion.pos_ref) | copy-start | bytes 40
  43.0 31.6 %copy-start.20 = (bf16[256,768]{1,0:T(8,128)(2,1)S(1)}, bf16[256,768]{1,0:T(8,128)(2,1)}, u32[]{:S(2)}) copy-start(bf16[256,768]{1,0:T(8,128)(2,1)} %constant.51.clone.rf_ref) | copy-start | bytes 1179652
  43.0 31.6 %copy-start.21 = (bf16[768,256]{1,0:T(8,128)(2,1)S(1)}, bf16[768,256]{1,0:T(8,128)(2,1)}, u32[]{:S(2)}) copy-start(bf16[768,256]{1,0:T(8,128)(2,1)} %constant.50.clone.lf_ref) | copy-start | bytes 1179652
  43.0 31.6 %copy-start.22 = (bf16[256,768]{1,0:T(8,128)(2,1)S(1)}, bf16[256,768]{1,0:T(8,128)(2,1)}, u32[]{:S(2)}) copy-start(bf16[256,768]{1,0:T(8,128)(2,1)} %constant.49.clone.ri_ref) | copy-start | bytes 1179652
  43.0 31.6 %copy-start.23 = (bf16[768,256]{1,0:T(8,128)(2,1)S(1)}, bf16[768,256]{1,0:T(8,128)(2,1)}, u32[]{:S(2)}) copy-start(bf16[768,256]{1,0:T(8,128)(2,1)} %constant.48.clone.li_ref) | copy-start | bytes 1179652
  43.0 31.6 %copy-start.24 = (f32[2,8,1,128]{3,2,1,0:T(1,128)S(1)}, f32[2,8,1,128]{3,2,1,0:T(1,128)}, u32[]{:S(2)}) copy-start(f32[2,8,1,128]{3,2,1,0:T(1,128)} %constant.52.clone.twl_ref) | copy-start | bytes 24580
  64.6 0.8 copy-start.26
  64.7 1.0 copy-start.27
  68.3 4.6 %collective-permute-start.6 = (bf16[2,384,768]{2,1,0:T(8,128)(2,1)}, bf16[2,384,768]{2,1,0:T(8,128)(2,1)S(1)}, u32[]{:S(2)}, u32[]{:S(2)}) collective-permute-start(bf16[2,384,768]{2,1,0:T(8,128)(2,1)} %cut.1), channel_id=1, source_target_pairs={{0,16},{16,0},{1,17},{17,1},{2,18},{18,2},{3,19},{19,3},{4,20},{20... | collective-permute-start | bytes 3538952 | tf_op jit(solution)/shard_map/ppermute | solution.py:615
  68.3 4.2 %collective-permute-start.5 = (bf16[2,512,512]{2,1,0:T(8,128)(2,1)S(1)}, bf16[2,512,512]{2,1,0:T(8,128)(2,1)S(1)}, u32[]{:S(2)}, u32[]{:S(2)}) collective-permute-start(bf16[2,512,512]{2,1,0:T(8,128)(2,1)S(1)} %copy-done.25), channel_id=1, source_target_pairs={{0,16},{16,0},{1,17},{17,1},{2,18},{18,2},{3,19},{19,3},{4,20},{20... | collective-permute-start | bytes 3145736 | tf_op jit(solution)/shard_map/ppermute | solution.py:612
  72.5 1.0 copy-start.30
  73.5 1.0 copy-start.29
  118.3 7.3 %collective-permute-start.13 = (bf16[1024,1024]{1,0:T(8,128)(2,1)}, bf16[1024,1024]{1,0:T(8,128)(2,1)S(1)}, u32[]{:S(2)}, u32[]{:S(2)}) collective-permute-start(bf16[1024,1024]{1,0:T(8,128)(2,1)} %get-tuple-element.29), channel_id=1, source_target_pairs={{0,16},{16,0},{1,17},{17,1},{2,18},{18,2},{3,19},{19,3},{4,20},{20... | collective-permute-start | bytes 6291464 | tf_op jit(solution)/shard_map/ppermute | solution.py:623
  118.5 7.0 %collective-permute-start.7 = (bf16[2,384,1280]{2,1,0:T(8,128)(2,1)}, bf16[2,384,1280]{2,1,0:T(8,128)(2,1)S(1)}, u32[]{:S(2)}, u32[]{:S(2)}) collective-permute-start(bf16[2,384,1280]{2,1,0:T(8,128)(2,1)} %get-tuple-element.20), channel_id=1, source_target_pairs={{0,16},{16,0},{1,17},{17,1},{2,18},{18,2},{3,19},{19,3},{4,20},{20... | collective-permute-start | bytes 5898248 | tf_op jit(solution)/shard_map/ppermute | solution.py:619
  125.6 2.2 copy-start.4
  128.1 1.3 copy-start.1
  129.5 18.9 %copy-start.16 = (bf16[2,512,384]{2,1,0:T(8,128)(2,1)S(1)}, bf16[2,512,384]{2,1,0:T(8,128)(2,1)}, u32[]{:S(2)}) copy-start(bf16[2,512,384]{2,1,0:T(8,128)(2,1)} %get-tuple-element.22.l_ref) | copy-start | bytes 2359300
  129.5 63.5 %all-to-all-start = ((bf16[32,32,1024]{2,1,0:T(8,128)(2,1)}), bf16[32,32,1024]{2,1,0:T(8,128)(2,1)}, u32[]{:S(2)}, u32[]{:S(2)}) async-start(bf16[32,32,1024]{2,1,0:T(8,128)(2,1)} %bitcast.11), calls=%async_computation | async-start | bytes 4194304 | tf_op jit(solution)/shard_map/all_to_all | solution.py:628
  144.1 37.1 %collective-permute-start.8 = (bf16[2,384,512]{2,1,0:T(8,128)(2,1)}, bf16[2,384,512]{2,1,0:T(8,128)(2,1)S(1)}, u32[]{:S(2)}, u32[]{:S(2)}) collective-permute-start(bf16[2,384,512]{2,1,0:T(8,128)(2,1)} %get-tuple-element.21), channel_id=1, source_target_pairs={{16,32},{48,64},{80,96},{112,128},{144,160},{176,192},{208,224},{3... | collective-permute-start | bytes 2359304 | tf_op jit(solution)/shard_map/ppermute | solution.py:620
  148.4 1.1 copy-start.17
  150.6 32.6 %collective-permute-start.9 = (bf16[2,512,384]{2,1,0:T(8,128)(2,1)S(1)}, bf16[2,512,384]{2,1,0:T(8,128)(2,1)S(1)}, u32[]{:S(2)}, u32[]{:S(2)}) collective-permute-start(bf16[2,512,384]{2,1,0:T(8,128)(2,1)S(1)} %get-tuple-element.24), channel_id=1, source_target_pairs={{1,0},{2,1},{3,2},{4,3},{5,4},{6,5},{7,6},{8,7},{9,8},{10,9},{11,1... | collective-permute-start | bytes 2359304 | tf_op jit(solution)/shard_map/ppermute | solution.py:625
  151.9 31.3 %collective-permute-start.10 = (bf16[2,512,384]{2,1,0:T(8,128)(2,1)S(1)}, bf16[2,512,384]{2,1,0:T(8,128)(2,1)}, u32[]{:S(2)}, u32[]{:S(2)}) collective-permute-start(bf16[2,512,384]{2,1,0:T(8,128)(2,1)S(1)} %get-tuple-element.25), channel_id=1, source_target_pairs={{0,1},{1,2},{2,3},{3,4},{4,5},{5,6},{6,7},{7,8},{8,9},{9,10},{10,1... | collective-permute-start | bytes 2359304 | tf_op jit(solution)/shard_map/ppermute | solution.py:626
  156.8 13.0 %collective-permute-start.11 = (bf16[2,384,384]{2,1,0:T(8,128)(2,1)}, bf16[2,384,384]{2,1,0:T(8,128)(2,1)S(1)}, u32[]{:S(2)}, u32[]{:S(2)}) collective-permute-start(bf16[2,384,384]{2,1,0:T(8,128)(2,1)} %get-tuple-element.26), channel_id=1, source_target_pairs={{17,32},{18,33},{19,34},{20,35},{21,36},{22,37},{23,38},{24,39},{2... | collective-permute-start | bytes 1769480 | tf_op jit(solution)/shard_map/ppermute | solution.py:621
  158.1 23.1 %collective-permute-start.12 = (bf16[2,384,384]{2,1,0:T(8,128)(2,1)}, bf16[2,384,384]{2,1,0:T(8,128)(2,1)S(1)}, u32[]{:S(2)}, u32[]{:S(2)}) collective-permute-start(bf16[2,384,384]{2,1,0:T(8,128)(2,1)} %get-tuple-element.27), channel_id=1, source_target_pairs={{16,33},{17,34},{18,35},{19,36},{20,37},{21,38},{22,39},{23,40},{2... | collective-permute-start | bytes 1769480 | tf_op jit(solution)/shard_map/ppermute | solution.py:622
  169.8 13.4 %copy-start.9 = (bf16[2,384,384]{2,1,0:T(8,128)(2,1)}, bf16[2,384,384]{2,1,0:T(8,128)(2,1)S(1)}, u32[]{:S(2)}) copy-start(bf16[2,384,384]{2,1,0:T(8,128)(2,1)S(1)} %collective-permute-done.11.vl_ref.refs_3_) | copy-start | bytes 1769476
  181.2 2.0 copy-start.11
  181.2 11.8 %copy-start.5 = (bf16[2,384,512]{2,1,0:T(8,128)(2,1)}, bf16[2,384,512]{2,1,0:T(8,128)(2,1)S(1)}, u32[]{:S(2)}) copy-start(bf16[2,384,512]{2,1,0:T(8,128)(2,1)S(1)} %collective-permute-done.8.v_ref.refs_2_) | copy-start | bytes 2359300
  183.2 9.8 %copy-start.7 = (bf16[2,512,384]{2,1,0:T(8,128)(2,1)}, bf16[2,512,384]{2,1,0:T(8,128)(2,1)S(1)}, u32[]{:S(2)}) copy-start(bf16[2,512,384]{2,1,0:T(8,128)(2,1)S(1)} %collective-permute-done.9.l_ref.refs_0_) | copy-start | bytes 2359300
  195.6 42.8 %all-to-all-start.1 = ((f32[4,8,1024]{2,1,0:T(8,128)}), f32[4,8,1024]{2,1,0:T(8,128)S(1)}, u32[]{:S(2)}, u32[]{:S(2)}) async-start(f32[4,8,1024]{2,1,0:T(8,128)} %bitcast.12), calls=%async_computation.1 | async-start | bytes 262144 | tf_op jit(solution)/shard_map/all_to_all | solution.py:630
  229.7 1.1 copy-start.6
  230.8 1.1 copy-start.8
  232.0 1.1 copy-start.10
  233.0 1.1 copy-start.12
  234.1 1.2 copy-start.15

commit v6 on v5

--- a/solution.py
+++ b/solution.py
@@ -91,7 +91,7 @@
 
 
 def led_body(
-    pos_ref, own_ref, l_ref, r_ref, v_ref, vl_ref, vr_ref, i_ref, c_ref, p_ref, amp_ref,
+    pos_ref, own_ref, l_ref, r_ref, v_ref, vl_ref, vr_ref, c_ref, p_ref, amp_ref,
     li_ref, lf_ref, ri_ref, rf_ref, twl_ref, twr_ref,
     oc_ref, ol_ref, or_ref, ov_ref, ovl_ref, ovr_ref, oi_ref, mine_ref, other_ref,
     w_ref, a_ref, s_refs, z_refs, s2_refs, z2_refs, to_ref, tm_ref, in_sem, out_sem,
@@ -103,12 +103,9 @@
     for start, count in ((RIM, TILE), (outer, RIM)):
         for col, wide in ((RIM, TILE), (0, RIM), (RIM + TILE, RIM)):
             places.append(w_ref.at[:, pl.ds(start, count), pl.ds(col, wide)])
-    arrivals = [own_ref, l_ref, r_ref, v_ref, vl_ref, vr_ref]
-    arrivals.append(i_ref.at[:, pl.ds(pl.multiple_of(core * (TILE - RIM), 128), RIM), :])
-    arrivals += [c_ref.at[:, :, pl.ds(0, RIM)], c_ref.at[:, :, pl.ds(RIM, RIM)]]
-    sides = [w_ref.at[:, pl.ds(inner, RIM), pl.ds(col, wide)] for col, wide in ((RIM, TILE), (0, RIM), (RIM + TILE, RIM))]
-    loads = [pltpu.make_async_copy(x, y, in_sem.at[k]) for k, (x, y) in enumerate(zip(arrivals, places + sides))]
     places.append(w_ref.at[:, pl.ds(inner, RIM), :])
+    arrivals = (own_ref, l_ref, r_ref, v_ref, vl_ref, vr_ref, c_ref)
+    loads = [pltpu.make_async_copy(x, y, in_sem.at[k]) for k, (x, y) in enumerate(zip(arrivals, places))]
     for load in loads:
         load.start()
 
@@ -334,7 +331,7 @@
         led_body,
         out_shape=rims(TILE) + rims(RIM) + [jax.ShapeDtypeStruct((2, RIM, REGION), BF16)]
         + [jax.ShapeDtypeStruct((N, N), F32), jax.ShapeDtypeStruct((N, N), BF16)],
-        in_specs=[pl.BlockSpec(memory_space=pltpu.SMEM)] + [hbm] * 8 + [vm] * 8,
+        in_specs=[pl.BlockSpec(memory_space=pltpu.SMEM)] + [hbm] * 7 + [vm] * 8,
         out_specs=[hbm] * 9,
         scratch_shapes=[
             pltpu.VMEM((2, REGION, REGION), BF16),
@@ -345,7 +342,7 @@
             [pltpu.VMEM((8, 256, CB), F32)] * 2,
             pltpu.VMEM((N, N), BF16),
             pltpu.VMEM((N, N), F32),
-            pltpu.SemaphoreType.DMA((9,)),
+            pltpu.SemaphoreType.DMA((7,)),
             pltpu.SemaphoreType.DMA((9,)),
         ],
         compiler_params=pltpu.CompilerParams(vmem_limit_bytes=52 * 2**20),
@@ -441,7 +438,7 @@
     )(pos, spectrum)
 
 
-def cut_body(pos_ref, l_ref, r_ref, *refs):
+def cut_body(pos_ref, own_ref, l_ref, r_ref, *refs):
     out_ref = refs[-1]
     row = (1 - pos_ref[2]) * (TILE - RIM)
 
@@ -451,19 +448,21 @@
         src = pl.ds(pl.multiple_of(row + i * 32, 32), 32)
         for q in range(2):
             out_ref[q, dst, 0:RIM] = l_ref[q, src, :]
-            out_ref[q, dst, RIM:2 * RIM] = r_ref[q, src, :]
-
-
-def cut(pos, l, r, *tokens):
+            out_ref[q, dst, RIM:RIM + TILE] = own_ref[q, src, :]
+            out_ref[q, dst, RIM + TILE:] = r_ref[q, src, :]
+
+
+def cut(pos, spectrum, l, r, *tokens):
     vm = pl.BlockSpec(memory_space=pltpu.VMEM)
     return pl.pallas_call(
         cut_body,
-        out_shape=jax.ShapeDtypeStruct((2, RIM, 2 * RIM), BF16),
-        in_specs=[pl.BlockSpec(memory_space=pltpu.SMEM), vm, vm] + [pl.BlockSpec(memory_space=pl.ANY)] * len(tokens),
+        out_shape=jax.ShapeDtypeStruct((2, RIM, REGION), BF16),
+        in_specs=[pl.BlockSpec(memory_space=pltpu.SMEM)] + [vm] * 3 + [pl.BlockSpec(memory_space=pl.ANY)] * len(tokens),
         out_specs=vm,
+        compiler_params=pltpu.CompilerParams(vmem_limit_bytes=24 * 2**20),
         cost_estimate=FREE,
         name="cut",
-    )(pos, l, r, *tokens)
+    )(pos, spectrum, l, r, *tokens)
 
 
 def sides_body(pos_ref, l_ref, r_ref, i_ref, *refs):
@@ -609,11 +608,10 @@
     in_v = lax.ppermute(out_v, KY, vert)
     in_vl = lax.ppermute(out_vl, ALL, vert_r)
     in_vr = lax.ppermute(out_vr, ALL, vert_l)
-    in_i = lax.ppermute(spectrum, "core", swap)
     amp = order(amplitude, tb["perm"])
     pupil = turn(pos, pupil)
-    in_c = lax.ppermute(cut(pos, in_l, in_r, pupil, amp, in_v, in_vl, in_vr), "core", swap)
-    pieces = (spectrum, in_l, in_r, in_v, in_vl, in_vr, in_i, in_c)
+    in_c = lax.ppermute(cut(pos, spectrum, in_l, in_r, pupil, amp, in_v, in_vl, in_vr), "core", swap)
+    pieces = (spectrum, in_l, in_r, in_v, in_vl, in_vr, in_c)
     c, l, r, v, vl, vr, i, mine, other = led(pos, pieces, pupil, amp, tb)
 
     i = lax.ppermute(i, "core", swap)
@@ -626,7 +624,8 @@
     r = lax.ppermute(r, KX, right)
     tile = tile_sum(pos, (c, i, v, l, r, vl, vr))
     total = lax.all_to_all(total.reshape(32, 32, N), ("x", "z"), 0, 0)
-    total = gather_sum(total, l, r, v, vl, vr).reshape(4, 8, N)
+    corner = sum(x[0, :16, :128].astype(F32) for x in (l, r, v, vl, vr))
+    total = gather_sum(total, corner).reshape(4, 8, N)
     total = lax.all_to_all(total, ("yh", "yl"), 0, 0)
     return tile, jnp.sum(total, axis=0).reshape(-1)
 

time: 240 us -> 238 us (level)
  Pallas kernels: 68.3 us -> 65.1 us
    all_to_all x1, waiting for transfers between devices: 9.82 us -> 4.76 us  [body(): total = lax.all_to_all(total.reshape(32, 32, N), ('x', 'z'), 0, 0)]
    ppermute x1, waiting for transfers between devices: 21.6 us -> 24.9 us  [body(): in_vl = lax.ppermute(out_vl, ALL, vert_r)]
    all_to_all x1, starting transfers between devices: 34.1 us -> 37.2 us  [body(): total = lax.all_to_all(total, ('yh', 'yl'), 0, 0)]
    unnamed x63 -> x75, local copies, waits for them, and re-layouts: 19.8 us -> 19.2 us
  transfers between devices with their start and end apart: 16 -> 15, of which waited for: 8 -> 7; matrix products, arithmetic and copies ran while one was open for 1% -> 1% of each run, Pallas kernels for 8% -> 8%
where the time goes in v6:
time: 238 us; the launch traced here: 237 us
  starting transfers between devices  85.3 us (36%)
  Pallas kernels  65.1 us (27%)
  waiting for transfers between devices  61.6 us (26%)
  local copies, waits for them, and re-layouts  21.4 us (9%)
    pallas_call x1, Pallas kernels, led(): pl.pallas_call(led_body, out_shape=rims(TILE) + rims(RIM) + [jax.ShapeDty...  42.8 us
    all_to_all x1, starting transfers between devices, body(): total = lax.all_to_all(total, ('yh', 'yl'), 0, 0)  37.2 us
    ppermute x1, waiting for transfers between devices, body(): in_vl = lax.ppermute(out_vl, ALL, vert_r)  24.9 us
    unnamed x75, local copies, waits for them, and re-layouts  19.2 us
    all_to_all x1, starting transfers between devices, body(): total = lax.all_to_all(total.reshape(32, 32, N), ('x', 'z'), 0, 0)  14.6 us
    ppermute x1, waiting for transfers between devices, body(): vr = lax.ppermute(vr, ALL, vert_r)  12.7 us
    pallas_call x1, Pallas kernels, turn(): pl.pallas_call(turn_body, out_shape=jax.ShapeDtypeStruct((2, N, N), BF16)...  7.75 us
    ppermute x1, waiting for transfers between devices, body(): i = lax.ppermute(i, 'core', swap)  6.67 us
  transfers between devices with their start and end apart: 15, of which 7 were waited for; matrix products, arithmetic and copies ran while one was open for 1% of the time, Pallas kernels for 8%

profile of v6, /device:TPU:1, one launch (start us, length us, event | category | flops | bytes accessed | tf_op | source)
XLA Modules:
  0.0 236.9 jit_solution(2858912751417850337)
XLA Ops:
  0.6 1.5 fusion
  2.2 1.3 collective-permute-start.1
  3.5 0.6 fusion.1
  5.4 0.6 pad_add_fusion.pos_ref
  6.0 4.7 %collective-permute-start = (bf16[2,512,384]{2,1,0:T(8,128)(2,1)S(1)}, bf16[2,512,384]{2,1,0:T(8,128)(2,1)S(1)}, u32[]{:S(2)}, u32[]{:S(2)}) collective-permute-start(bf16[2,512,384]{2,1,0:T(8,128)(2,1)S(1)} %get-tuple-element.31), channel_id=1, source_target_pairs={{0,1},{1,2},{2,3},{3,4},{4,5},{5,6},{6,7},{7,8},{8,9},{9,10},{10,1... | collective-permute-start | bytes 2359304 | tf_op jit(solution)/shard_map/ppermute | solution.py:605
  10.7 2.7 %ends.1 = (bf16[2,384,512]{2,1,0:T(8,128)(2,1)}, bf16[2,384,384]{2,1,0:T(8,128)(2,1)}, bf16[2,384,384]{2,1,0:T(8,128)(2,1)}) custom-call(s32[3]{0:T(128)} %pad_add_fusion.pos_ref, bf16[2,512,512]{2,1,0:T(8,128)(2,1)} %own_ref.3), custom_call_target="tpu_custom_call" | custom-call | flops 1 | bytes 1 | tf_op jit(solution)/shard_map/ends/pallas_call | solution.py:431
  13.5 6.1 %collective-permute-start.2 = (bf16[2,384,512]{2,1,0:T(8,128)(2,1)}, bf16[2,384,512]{2,1,0:T(8,128)(2,1)S(1)}, u32[]{:S(2)}, u32[]{:S(2)}) collective-permute-start(bf16[2,384,512]{2,1,0:T(8,128)(2,1)} %get-tuple-element.16), channel_id=1, source_target_pairs={{16,32},{48,64},{80,96},{112,128},{144,160},{176,192},{208,224},{3... | collective-permute-start | bytes 2359304 | tf_op jit(solution)/shard_map/ppermute | solution.py:608
  19.6 2.7 %collective-permute-start.3 = (bf16[2,384,384]{2,1,0:T(8,128)(2,1)}, bf16[2,384,384]{2,1,0:T(8,128)(2,1)S(1)}, u32[]{:S(2)}, u32[]{:S(2)}) collective-permute-start(bf16[2,384,384]{2,1,0:T(8,128)(2,1)} %get-tuple-element.17), channel_id=1, source_target_pairs={{16,33},{17,34},{18,35},{19,36},{20,37},{21,38},{22,39},{23,40},{2... | collective-permute-start | bytes 1769480 | tf_op jit(solution)/shard_map/ppermute | solution.py:609
  22.3 1.3 collective-permute-start.4
  23.6 0.0 copy-start.4
  23.6 2.2 copy-done.4
  25.8 0.6 copy-done.26
  26.4 7.7 %turn.1.refs_0_.p_ref = bf16[2,1024,1024]{2,1,0:T(8,128)(2,1)S(1)} custom-call(s32[3]{0:T(128)S(1)} %copy-done.26, bf16[2,1024,1024]{2,1,0:T(8,128)(2,1)S(1)} %copy-done.4), custom_call_target="tpu_custom_call" | custom-call | flops 1 | bytes 1 | tf_op jit(solution)/shard_map/turn/pallas_call | solution.py:382
  34.2 0.0 copy-start.1
  34.2 4.5 %order.1.refs_1_.amp_ref = bf16[1024,1024]{1,0:T(8,128)(2,1)S(1)} custom-call(bf16[1024,1024]{1,0:T(8,128)(2,1)S(1)} %copy-done.6, bf16[1024,1024]{1,0:T(8,128)(2,1)S(1)} %copy-done.7), custom_call_target="tpu_custom_call" | custom-call | flops 1 | bytes 1 | tf_op jit(solution)/shard_map/order/pallas_call | solution.py:403
  38.8 0.0 copy-start.2
  38.8 0.0 copy-start.28
  38.8 0.0 copy-start.29
  38.8 0.0 copy-start.30
  38.8 0.0 copy-start.31
  38.8 0.0 copy-start.32
  38.9 24.9 %collective-permute-done.3.refs_3_.vl_ref = bf16[2,384,384]{2,1,0:T(8,128)(2,1)S(1)} collective-permute-done((bf16[2,384,384]{2,1,0:T(8,128)(2,1)}, bf16[2,384,384]{2,1,0:T(8,128)(2,1)S(1)}, u32[]{:S(2)}, u32[]{:S(2)}) %collective-permute-start.3) | collective-permute-done | bytes 589856 | tf_op jit(solution)/shard_map/ppermute | solution.py:609
  63.8 0.7 cut.1
  64.6 0.2 copy-done.25
  64.7 0.2 copy-done.15
  65.0 0.3 copy-done.16
  65.2 0.3 copy-done.17
  65.5 0.0 collective-permute-start.5
  65.5 4.0 %collective-permute-done.5.c_ref = bf16[2,384,1280]{2,1,0:T(8,128)(2,1)S(1)} collective-permute-done((bf16[2,384,1280]{2,1,0:T(8,128)(2,1)S(1)}, bf16[2,384,1280]{2,1,0:T(8,128)(2,1)S(1)}, u32[]{:S(2)}, u32[]{:S(2)}) %collective-permute-start.5) | collective-permute-done | bytes 1966112 | tf_op jit(solution)/shard_map/ppermute | solution.py:613
  69.5 1.4 copy-done.34
  70.9 42.8 %led.1 = (bf16[2,512,512]{2,1,0:T(8,128)(2,1)}, bf16[2,512,384]{2,1,0:T(8,128)(2,1)}, bf16[2,512,384]{2,1,0:T(8,128)(2,1)}, bf16[2,384,512]{2,1,0:T(8,128)(2,1)}...) custom-call(s32[3]{0:T(128)S(1)} %copy-done.27, ...), custom_call_target="tpu_custom_call" | custom-call | flops 12999999488 | bytes 31457280 | tf_op jit(solution)/shard_map/led/pallas_call | solution.py:330
  113.7 0.2 collective-permute-start.12
  113.9 0.4 collective-permute-start.6
  114.3 6.7 %collective-permute-done.6.i_ref.token_ref = bf16[2,384,1280]{2,1,0:T(8,128)(2,1)S(1)} collective-permute-done((bf16[2,384,1280]{2,1,0:T(8,128)(2,1)}, bf16[2,384,1280]{2,1,0:T(8,128)(2,1)S(1)}, u32[]{:S(2)}, u32[]{:S(2)}) %collective-permute-start.6) | collective-permute-done | bytes 1966112 | tf_op jit(solution)/shard_map/ppermute | solution.py:617
  121.0 2.2 copy-done.5
  123.2 0.4 pair_sum.1
  123.5 0.0 copy-start.3
  123.6 1.3 copy-done.3
  124.9 14.6 %all-to-all-start = ((bf16[32,32,1024]{2,1,0:T(8,128)(2,1)}), bf16[32,32,1024]{2,1,0:T(8,128)(2,1)}, u32[]{:S(2)}, u32[]{:S(2)}) async-start(bf16[32,32,1024]{2,1,0:T(8,128)(2,1)} %bitcast.13), calls=%async_computation | async-start | bytes 4194304 | tf_op jit(solution)/shard_map/all_to_all | solution.py:626
  139.5 4.4 %collective-permute-start.7 = (bf16[2,384,512]{2,1,0:T(8,128)(2,1)}, bf16[2,384,512]{2,1,0:T(8,128)(2,1)S(1)}, u32[]{:S(2)}, u32[]{:S(2)}) collective-permute-start(bf16[2,384,512]{2,1,0:T(8,128)(2,1)} %get-tuple-element.21), channel_id=1, source_target_pairs={{16,32},{48,64},{80,96},{112,128},{144,160},{176,192},{208,224},{3... | collective-permute-start | bytes 2359304 | tf_op jit(solution)/shard_map/ppermute | solution.py:618
  144.0 1.1 sides.1
  145.1 1.4 collective-permute-start.8
  146.6 4.0 %collective-permute-start.9 = (bf16[2,512,384]{2,1,0:T(8,128)(2,1)S(1)}, bf16[2,512,384]{2,1,0:T(8,128)(2,1)S(1)}, u32[]{:S(2)}, u32[]{:S(2)}) collective-permute-start(bf16[2,512,384]{2,1,0:T(8,128)(2,1)S(1)} %get-tuple-element.25), channel_id=1, source_target_pairs={{0,1},{1,2},{2,3},{3,4},{4,5},{5,6},{6,7},{7,8},{8,9},{9,10},{10,1... | collective-permute-start | bytes 2359304 | tf_op jit(solution)/shard_map/ppermute | solution.py:624
  150.6 1.3 collective-permute-start.10
  151.9 5.5 %collective-permute-start.11 = (bf16[2,384,384]{2,1,0:T(8,128)(2,1)S(1)}, bf16[2,384,384]{2,1,0:T(8,128)(2,1)S(1)}, u32[]{:S(2)}, u32[]{:S(2)}) collective-permute-start(bf16[2,384,384]{2,1,0:T(8,128)(2,1)S(1)} %copy-done.35), channel_id=1, source_target_pairs={{16,33},{17,34},{18,35},{19,36},{20,37},{21,38},{22,39},{23,40},{2... | collective-permute-start | bytes 1769480 | tf_op jit(solution)/shard_map/ppermute | solution.py:620
  157.5 6.0 %collective-permute-done.10.vl_ref = bf16[2,384,384]{2,1,0:T(8,128)(2,1)S(1)} collective-permute-done((bf16[2,384,384]{2,1,0:T(8,128)(2,1)S(1)}, bf16[2,384,384]{2,1,0:T(8,128)(2,1)S(1)}, u32[]{:S(2)}, u32[]{:S(2)}) %collective-permute-start.10) | collective-permute-done | bytes 589856 | tf_op jit(solution)/shard_map/ppermute | solution.py:619
  163.4 12.7 %collective-permute-done.11.vr_ref = bf16[2,384,384]{2,1,0:T(8,128)(2,1)S(1)} collective-permute-done((bf16[2,384,384]{2,1,0:T(8,128)(2,1)S(1)}, bf16[2,384,384]{2,1,0:T(8,128)(2,1)S(1)}, u32[]{:S(2)}, u32[]{:S(2)}) %collective-permute-start.11) | collective-permute-done | bytes 589856 | tf_op jit(solution)/shard_map/ppermute | solution.py:620
  176.2 2.6 %collective-permute-done.8.l_ref = bf16[2,512,384]{2,1,0:T(8,128)(2,1)S(1)} collective-permute-done((bf16[2,512,384]{2,1,0:T(8,128)(2,1)S(1)}, bf16[2,512,384]{2,1,0:T(8,128)(2,1)S(1)}, u32[]{:S(2)}, u32[]{:S(2)}) %collective-permute-start.8) | collective-permute-done | bytes 786464 | tf_op jit(solution)/shard_map/ppermute | solution.py:623
  178.7 0.6 add_bitcast_fusion.refs_0_
  179.4 0.9 copy-done.9
  180.3 0.9 copy-done.11
  181.1 0.9 copy-done.13
  182.0 0.9 copy-done.20
  182.9 0.8 copy-done.22
  183.7 4.8 %all-to-all-done.x_ref = bf16[32,32,1024]{2,1,0:T(8,128)(2,1)} async-done(((bf16[32,32,1024]{2,1,0:T(8,128)(2,1)}), bf16[32,32,1024]{2,1,0:T(8,128)(2,1)}, u32[]{:S(2)}, u32[]{:S(2)}) %all-to-all-start) | async-done | bytes 2097184 | tf_op jit(solution)/shard_map/all_to_all | solution.py:626
  188.5 2.5 %gather_sum.1 = f32[32,1024]{1,0:T(8,128)} custom-call(bf16[32,32,1024]{2,1,0:T(8,128)(2,1)} %all-to-all-done.x_ref, f32[16,128]{1,0:T(8,128)} %add_bitcast_fusion.refs_0_), custom_call_target="tpu_custom_call" | custom-call | flops 1 | bytes 1 | tf_op jit(solution)/shard_map/gather_sum/pallas_call | solution.py:565
  191.0 37.2 %all-to-all-start.1 = ((f32[4,8,1024]{2,1,0:T(8,128)}), f32[4,8,1024]{2,1,0:T(8,128)S(1)}, u32[]{:S(2)}, u32[]{:S(2)}) async-start(f32[4,8,1024]{2,1,0:T(8,128)} %bitcast.14), calls=%async_computation.1 | async-start | bytes 262144 | tf_op jit(solution)/shard_map/all_to_all | solution.py:629
  228.2 1.1 copy-done.10
  229.4 1.1 copy-done.12
  230.5 1.1 copy-done.14
  231.6 1.1 copy-done.21
  232.7 1.1 copy-done.23
  233.8 2.5 %tile_sum.1 = f32[2,512,512]{2,1,0:T(8,128)} custom-call(s32[3]{0:T(128)S(1)} %copy-done.27, bf16[2,512,512]{2,1,0:T(8,128)(2,1)S(1)} %copy-done.8, bf16[2,384,1280]{2,1,0:T(8,128)(2,1)S(1)} %collective-permute-done.6.i_ref.token_ref, bf16[2,384,512]{2,1,0:T(8,128)(2,1)S(1)} %copy-done.10, bf16[2,512,384]{2,1,0:T(8,128)(2,1)S(1)} %copy-done.12, ...), custom_call_target="tpu_custom_call" | custom-call | flops 1 | bytes 1 | tf_op jit(solution)/shard_map/tile_sum/pallas_call | solution.py:519
  236.3 0.6 copy.15
  (55 shorter events, 0.1 us)
Async XLA Ops:
  0.6 2.9 %copy-start.33 = (s32[1,1,2]{2,1,0:T(1,128)S(1)}, s32[1,1,2]{2,1,0:T(1,128)}, u32[]{:S(2)}) copy-start(s32[1,1,2]{2,1,0:T(1,128)} %param.14) | copy-start | bytes 28
  2.2 61.6 %collective-permute-start.1 = (bf16[2,512,384]{2,1,0:T(8,128)(2,1)S(1)}, bf16[2,512,384]{2,1,0:T(8,128)(2,1)S(1)}, u32[]{:S(2)}, u32[]{:S(2)}) collective-permute-start(bf16[2,512,384]{2,1,0:T(8,128)(2,1)S(1)} %get-tuple-element.30), channel_id=1, source_target_pairs={{1,0},{2,1},{3,2},{4,3},{5,4},{6,5},{7,6},{8,7},{9,8},{10,9},{11,1... | collective-permute-start | bytes 2359304 | tf_op jit(solution)/shard_map/ppermute | solution.py:606
  6.0 57.7 %collective-permute-start = (bf16[2,512,384]{2,1,0:T(8,128)(2,1)S(1)}, bf16[2,512,384]{2,1,0:T(8,128)(2,1)S(1)}, u32[]{:S(2)}, u32[]{:S(2)}) collective-permute-start(bf16[2,512,384]{2,1,0:T(8,128)(2,1)S(1)} %get-tuple-element.31), channel_id=1, source_target_pairs={{0,1},{1,2},{2,3},{3,4},{4,5},{5,6},{6,7},{7,8},{8,9},{9,10},{10,1... | collective-permute-start | bytes 2359304 | tf_op jit(solution)/shard_map/ppermute | solution.py:605
  13.5 50.3 %collective-permute-start.2 = (bf16[2,384,512]{2,1,0:T(8,128)(2,1)}, bf16[2,384,512]{2,1,0:T(8,128)(2,1)S(1)}, u32[]{:S(2)}, u32[]{:S(2)}) collective-permute-start(bf16[2,384,512]{2,1,0:T(8,128)(2,1)} %get-tuple-element.16), channel_id=1, source_target_pairs={{16,32},{48,64},{80,96},{112,128},{144,160},{176,192},{208,224},{3... | collective-permute-start | bytes 2359304 | tf_op jit(solution)/shard_map/ppermute | solution.py:608
  19.6 44.2 %collective-permute-start.3 = (bf16[2,384,384]{2,1,0:T(8,128)(2,1)}, bf16[2,384,384]{2,1,0:T(8,128)(2,1)S(1)}, u32[]{:S(2)}, u32[]{:S(2)}) collective-permute-start(bf16[2,384,384]{2,1,0:T(8,128)(2,1)} %get-tuple-element.17), channel_id=1, source_target_pairs={{16,33},{17,34},{18,35},{19,36},{20,37},{21,38},{22,39},{23,40},{2... | collective-permute-start | bytes 1769480 | tf_op jit(solution)/shard_map/ppermute | solution.py:609
  22.3 41.4 %collective-permute-start.4 = (bf16[2,384,384]{2,1,0:T(8,128)(2,1)}, bf16[2,384,384]{2,1,0:T(8,128)(2,1)S(1)}, u32[]{:S(2)}, u32[]{:S(2)}) collective-permute-start(bf16[2,384,384]{2,1,0:T(8,128)(2,1)} %get-tuple-element.18), channel_id=1, source_target_pairs={{17,32},{18,33},{19,34},{20,35},{21,36},{22,37},{23,38},{24,39},{2... | collective-permute-start | bytes 1769480 | tf_op jit(solution)/shard_map/ppermute | solution.py:610
  23.6 2.2 copy-start.4
  25.8 0.6 copy-start.26
  26.4 7.8 %copy-start.6 = (bf16[1024,1024]{1,0:T(8,128)(2,1)S(1)}, bf16[1024,1024]{1,0:T(8,128)(2,1)}, u32[]{:S(2)}) copy-start(bf16[1024,1024]{1,0:T(8,128)(2,1)} %amp_ref.1) | copy-start | bytes 6291460
  26.4 7.8 %copy-start.7 = (bf16[1024,1024]{1,0:T(8,128)(2,1)S(1)}, bf16[1024,1024]{1,0:T(8,128)(2,1)}, u32[]{:S(2)}) copy-start(bf16[1024,1024]{1,0:T(8,128)(2,1)} %constant.54.clone.perm_ref) | copy-start | bytes 6291460
  34.2 29.6 %copy-start = (bf16[2,1024,1024]{2,1,0:T(8,128)(2,1)}, bf16[2,1024,1024]{2,1,0:T(8,128)(2,1)S(1)}, u32[]{:S(2)}) copy-start(bf16[2,1024,1024]{2,1,0:T(8,128)(2,1)S(1)} %turn.1.refs_0_.p_ref) | copy-start | bytes 12582916
  34.2 29.6 %copy-start.1 = (bf16[2,512,512]{2,1,0:T(8,128)(2,1)S(1)}, bf16[2,512,512]{2,1,0:T(8,128)(2,1)}, u32[]{:S(2)}) copy-start(bf16[2,512,512]{2,1,0:T(8,128)(2,1)} %own_ref.3) | copy-start | bytes 3145732
  38.8 25.8 %copy-start.2 = (bf16[1024,1024]{1,0:T(8,128)(2,1)}, bf16[1024,1024]{1,0:T(8,128)(2,1)S(1)}, u32[]{:S(2)}) copy-start(bf16[1024,1024]{1,0:T(8,128)(2,1)S(1)} %order.1.refs_1_.amp_ref) | copy-start | bytes 6291460
  38.8 32.1 %copy-start.27 = (s32[3]{0:T(128)S(1)}, s32[3]{0:T(128)}, u32[]{:S(2)}) copy-start(s32[3]{0:T(128)} %pad_add_fusion.pos_ref) | copy-start | bytes 40
  38.8 32.1 %copy-start.28 = (bf16[256,768]{1,0:T(8,128)(2,1)S(1)}, bf16[256,768]{1,0:T(8,128)(2,1)}, u32[]{:S(2)}) copy-start(bf16[256,768]{1,0:T(8,128)(2,1)} %constant.51.clone.rf_ref) | copy-start | bytes 1179652
  38.8 32.0 %copy-start.29 = (bf16[768,256]{1,0:T(8,128)(2,1)S(1)}, bf16[768,256]{1,0:T(8,128)(2,1)}, u32[]{:S(2)}) copy-start(bf16[768,256]{1,0:T(8,128)(2,1)} %constant.50.clone.lf_ref) | copy-start | bytes 1179652
  38.8 32.0 %copy-start.30 = (bf16[256,768]{1,0:T(8,128)(2,1)S(1)}, bf16[256,768]{1,0:T(8,128)(2,1)}, u32[]{:S(2)}) copy-start(bf16[256,768]{1,0:T(8,128)(2,1)} %constant.49.clone.ri_ref) | copy-start | bytes 1179652
  38.8 32.0 %copy-start.31 = (bf16[768,256]{1,0:T(8,128)(2,1)S(1)}, bf16[768,256]{1,0:T(8,128)(2,1)}, u32[]{:S(2)}) copy-start(bf16[768,256]{1,0:T(8,128)(2,1)} %constant.48.clone.li_ref) | copy-start | bytes 1179652
  38.8 32.0 %copy-start.32 = (f32[2,8,1,128]{3,2,1,0:T(1,128)S(1)}, f32[2,8,1,128]{3,2,1,0:T(1,128)}, u32[]{:S(2)}) copy-start(f32[2,8,1,128]{3,2,1,0:T(1,128)} %constant.52.clone.twl_ref) | copy-start | bytes 24580
  63.7 0.8 copy-start.24
  63.7 1.0 copy-start.25
  63.7 1.2 copy-start.15
  63.8 1.5 copy-start.16
  63.8 1.7 copy-start.17
  65.5 4.0 %collective-permute-start.5 = (bf16[2,384,1280]{2,1,0:T(8,128)(2,1)S(1)}, bf16[2,384,1280]{2,1,0:T(8,128)(2,1)S(1)}, u32[]{:S(2)}, u32[]{:S(2)}) collective-permute-start(bf16[2,384,1280]{2,1,0:T(8,128)(2,1)S(1)} %cut.1), channel_id=1, source_target_pairs={{0,16},{16,0},{1,17},{17,1},{2,18},{18,2},{3,19},{19,3},{4,20},{20... | collective-permute-start | bytes 5898248 | tf_op jit(solution)/shard_map/ppermute | solution.py:613
  69.5 1.4 copy-start.34
  113.7 7.3 %collective-permute-start.12 = (bf16[1024,1024]{1,0:T(8,128)(2,1)}, bf16[1024,1024]{1,0:T(8,128)(2,1)S(1)}, u32[]{:S(2)}, u32[]{:S(2)}) collective-permute-start(bf16[1024,1024]{1,0:T(8,128)(2,1)} %get-tuple-element.29), channel_id=1, source_target_pairs={{0,16},{16,0},{1,17},{17,1},{2,18},{18,2},{3,19},{19,3},{4,20},{20... | collective-permute-start | bytes 6291464 | tf_op jit(solution)/shard_map/ppermute | solution.py:621
  113.9 7.0 %collective-permute-start.6 = (bf16[2,384,1280]{2,1,0:T(8,128)(2,1)}, bf16[2,384,1280]{2,1,0:T(8,128)(2,1)S(1)}, u32[]{:S(2)}, u32[]{:S(2)}) collective-permute-start(bf16[2,384,1280]{2,1,0:T(8,128)(2,1)} %get-tuple-element.20), channel_id=1, source_target_pairs={{0,16},{16,0},{1,17},{17,1},{2,18},{18,2},{3,19},{19,3},{4,20},{20... | collective-permute-start | bytes 5898248 | tf_op jit(solution)/shard_map/ppermute | solution.py:617
  121.0 2.2 copy-start.5
  123.5 1.3 copy-start.3
  124.9 19.1 %copy-start.18 = (bf16[2,512,384]{2,1,0:T(8,128)(2,1)S(1)}, bf16[2,512,384]{2,1,0:T(8,128)(2,1)}, u32[]{:S(2)}) copy-start(bf16[2,512,384]{2,1,0:T(8,128)(2,1)} %get-tuple-element.22.l_ref) | copy-start | bytes 2359300
  124.9 19.1 %copy-start.19 = (bf16[2,512,384]{2,1,0:T(8,128)(2,1)S(1)}, bf16[2,512,384]{2,1,0:T(8,128)(2,1)}, u32[]{:S(2)}) copy-start(bf16[2,512,384]{2,1,0:T(8,128)(2,1)} %get-tuple-element.23.r_ref) | copy-start | bytes 2359300
  124.9 63.6 %all-to-all-start = ((bf16[32,32,1024]{2,1,0:T(8,128)(2,1)}), bf16[32,32,1024]{2,1,0:T(8,128)(2,1)}, u32[]{:S(2)}, u32[]{:S(2)}) async-start(bf16[32,32,1024]{2,1,0:T(8,128)(2,1)} %bitcast.13), calls=%async_computation | async-start | bytes 4194304 | tf_op jit(solution)/shard_map/all_to_all | solution.py:626
  139.5 11.1 %copy-start.36 = (bf16[2,384,384]{2,1,0:T(8,128)(2,1)S(1)}, bf16[2,384,384]{2,1,0:T(8,128)(2,1)}, u32[]{:S(2)}) copy-start(bf16[2,384,384]{2,1,0:T(8,128)(2,1)} %get-tuple-element.26) | copy-start | bytes 1769476
  139.5 12.4 %copy-start.35 = (bf16[2,384,384]{2,1,0:T(8,128)(2,1)S(1)}, bf16[2,384,384]{2,1,0:T(8,128)(2,1)}, u32[]{:S(2)}) copy-start(bf16[2,384,384]{2,1,0:T(8,128)(2,1)} %get-tuple-element.27) | copy-start | bytes 1769476
  139.5 36.6 %collective-permute-start.7 = (bf16[2,384,512]{2,1,0:T(8,128)(2,1)}, bf16[2,384,512]{2,1,0:T(8,128)(2,1)S(1)}, u32[]{:S(2)}, u32[]{:S(2)}) collective-permute-start(bf16[2,384,512]{2,1,0:T(8,128)(2,1)} %get-tuple-element.21), channel_id=1, source_target_pairs={{16,32},{48,64},{80,96},{112,128},{144,160},{176,192},{208,224},{3... | collective-permute-start | bytes 2359304 | tf_op jit(solution)/shard_map/ppermute | solution.py:618
  145.1 83.1 %copy-start.8 = (bf16[2,512,512]{2,1,0:T(8,128)(2,1)S(1)}, bf16[2,512,512]{2,1,0:T(8,128)(2,1)}, u32[]{:S(2)}) copy-start(bf16[2,512,512]{2,1,0:T(8,128)(2,1)} %get-tuple-element.19.c_ref) | copy-start | bytes 3145732
  145.1 33.6 %collective-permute-start.8 = (bf16[2,512,384]{2,1,0:T(8,128)(2,1)S(1)}, bf16[2,512,384]{2,1,0:T(8,128)(2,1)S(1)}, u32[]{:S(2)}, u32[]{:S(2)}) collective-permute-start(bf16[2,512,384]{2,1,0:T(8,128)(2,1)S(1)} %get-tuple-element.24), channel_id=1, source_target_pairs={{1,0},{2,1},{3,2},{4,3},{5,4},{6,5},{7,6},{8,7},{9,8},{10,9},{11,1... | collective-permute-start | bytes 2359304 | tf_op jit(solution)/shard_map/ppermute | solution.py:623
  146.6 32.2 %collective-permute-start.9 = (bf16[2,512,384]{2,1,0:T(8,128)(2,1)S(1)}, bf16[2,512,384]{2,1,0:T(8,128)(2,1)S(1)}, u32[]{:S(2)}, u32[]{:S(2)}) collective-permute-start(bf16[2,512,384]{2,1,0:T(8,128)(2,1)S(1)} %get-tuple-element.25), channel_id=1, source_target_pairs={{0,1},{1,2},{2,3},{3,4},{4,5},{5,6},{6,7},{7,8},{8,9},{9,10},{10,1... | collective-permute-start | bytes 2359304 | tf_op jit(solution)/shard_map/ppermute | solution.py:624
  150.6 12.8 %collective-permute-start.10 = (bf16[2,384,384]{2,1,0:T(8,128)(2,1)S(1)}, bf16[2,384,384]{2,1,0:T(8,128)(2,1)S(1)}, u32[]{:S(2)}, u32[]{:S(2)}) collective-permute-start(bf16[2,384,384]{2,1,0:T(8,128)(2,1)S(1)} %copy-done.36), channel_id=1, source_target_pairs={{17,32},{18,33},{19,34},{20,35},{21,36},{22,37},{23,38},{24,39},{2... | collective-permute-start | bytes 1769480 | tf_op jit(solution)/shard_map/ppermute | solution.py:619
  151.9 24.2 %collective-permute-start.11 = (bf16[2,384,384]{2,1,0:T(8,128)(2,1)S(1)}, bf16[2,384,384]{2,1,0:T(8,128)(2,1)S(1)}, u32[]{:S(2)}, u32[]{:S(2)}) collective-permute-start(bf16[2,384,384]{2,1,0:T(8,128)(2,1)S(1)} %copy-done.35), channel_id=1, source_target_pairs={{16,33},{17,34},{18,35},{19,36},{20,37},{21,38},{22,39},{23,40},{2... | collective-permute-start | bytes 1769480 | tf_op jit(solution)/shard_map/ppermute | solution.py:620
  179.4 0.9 copy-start.9
  180.2 0.9 copy-start.11
  181.1 0.9 copy-start.13
  182.0 0.9 copy-start.20
  182.9 0.8 copy-start.22
  191.0 45.3 %all-to-all-start.1 = ((f32[4,8,1024]{2,1,0:T(8,128)}), f32[4,8,1024]{2,1,0:T(8,128)S(1)}, u32[]{:S(2)}, u32[]{:S(2)}) async-start(f32[4,8,1024]{2,1,0:T(8,128)} %bitcast.14), calls=%async_computation.1 | async-start | bytes 262144 | tf_op jit(solution)/shard_map/all_to_all | solution.py:629
  228.2 1.1 copy-start.10
  229.4 1.1 copy-start.12
  230.5 1.1 copy-start.14
  231.6 1.1 copy-start.21
  232.7 1.1 copy-start.23

commit v7 on v6

--- a/solution.py
+++ b/solution.py
@@ -550,26 +550,29 @@
     )(mine, other, token)
 
 
-def gather_body(x_ref, *refs):
-    out_ref = refs[-1]
+def gather_body(pos_ref, x_ref, token_ref, *refs):
+    sum_ref = refs[-1]
     for i in range(2):
         rows = pl.ds(i * 16, 16)
         total = x_ref[0, rows, :].astype(F32)
         for k in range(1, 32):
             total += x_ref[k, rows, :].astype(F32)
-        out_ref[rows, :] = total
-
-
-def gather_sum(x, *tokens):
+        sum_ref[rows, :] = total
+    for k, out_ref in enumerate(refs[:-1]):
+        out_ref[...] = sum_ref[pl.ds(pl.multiple_of(jnp.bitwise_xor(pos_ref[3], k) * 8, 8), 8), :]
+
+
+def gather_sum(pos, x, token):
     vm = pl.BlockSpec(memory_space=pltpu.VMEM)
     return pl.pallas_call(
         gather_body,
-        out_shape=jax.ShapeDtypeStruct((32, N), F32),
-        in_specs=[vm] + [pl.BlockSpec(memory_space=pl.ANY)] * len(tokens),
-        out_specs=vm,
+        out_shape=[jax.ShapeDtypeStruct((8, N), F32)] * 4,
+        in_specs=[pl.BlockSpec(memory_space=pltpu.SMEM), vm, pl.BlockSpec(memory_space=pl.ANY)],
+        out_specs=[vm] * 4,
+        scratch_shapes=[pltpu.VMEM((32, N), F32)],
         cost_estimate=FREE,
         name="gather_sum",
-    )(x, *tokens)
+    )(pos, x, token)
 
 
 KY, KX = ("x", "yh", "core"), ("z", "yl")
@@ -596,7 +599,7 @@
     first = core == 0
     r0 = offsets[0, 0, 0] - (iy * TILE - RIM)
     c0 = offsets[0, 0, 1] - (ix * TILE - RIM)
-    pos = jnp.stack([r0, c0, core])
+    pos = jnp.stack([r0, c0, core, lax.axis_index(("yh", "yl"))])
     right, left = chain(n_kx)
     vert = between_chips(n_ky)
     vert_l, vert_r = both(vert, left, n_kx), both(vert, right, n_kx)
@@ -624,10 +627,10 @@
     r = lax.ppermute(r, KX, right)
     tile = tile_sum(pos, (c, i, v, l, r, vl, vr))
     total = lax.all_to_all(total.reshape(32, 32, N), ("x", "z"), 0, 0)
-    corner = sum(x[0, :16, :128].astype(F32) for x in (l, r, v, vl, vr))
-    total = gather_sum(total, corner).reshape(4, 8, N)
-    total = lax.all_to_all(total, ("yh", "yl"), 0, 0)
-    return tile, jnp.sum(total, axis=0).reshape(-1)
+    mine, *others = gather_sum(pos, total, tile)
+    for k, other in enumerate(others, 1):
+        mine = mine + lax.ppermute(other, ("yh", "yl"), [(i, i ^ k) for i in range(4)])
+    return tile, mine.reshape(-1)
 
 
 def solution(mesh):

time: 238 us -> 232 us (0.975)
  local copies, waits for them, and re-layouts: 21.4 us -> 11.4 us
  waiting for transfers between devices: 61.6 us -> 68.3 us
  starting transfers between devices: 85.3 us -> 82.7 us
    all_to_all x1 -> x0, starting transfers between devices: 37.2 us -> none  [body(): total = lax.all_to_all(total, ('yh', 'yl'), 0, 0)]
    ppermute x0 -> x3, starting transfers between devices: none -> 34.8 us  [body(): lax.ppermute(other, ('yh', 'yl'), [(i, i ^ k) for i in range(4)])]
    unnamed x75 -> x55, local copies, waits for them, and re-layouts: 19.2 us -> 9.25 us
    ppermute x0 -> x3, waiting for transfers between devices: none -> 4.18 us  [body(): lax.ppermute(other, ('yh', 'yl'), [(i, i ^ k) for i in range(4)])]
    all_to_all x1, waiting for transfers between devices: 4.76 us -> 7.16 us  [body(): total = lax.all_to_all(total.reshape(32, 32, N), ('x', 'z'), 0, 0)]
  transfers between devices with their start and end apart: 15 -> 17, of which waited for: 7 -> 9; matrix products, arithmetic and copies ran while one was open for 1% -> 1% of each run, Pallas kernels for 8% -> 8%
where the time goes in v7:
time: 232 us; the launch traced here: 231 us
  starting transfers between devices  82.7 us (36%)
  waiting for transfers between devices  68.3 us (29%)
  Pallas kernels  65.1 us (28%)
  local copies, waits for them, and re-layouts  11.4 us (5%)
  between operations  2.34 us (1%)
    pallas_call x1, Pallas kernels, led(): pl.pallas_call(led_body, out_shape=rims(TILE) + rims(RIM) + [jax.ShapeDty...  42.9 us
    ppermute x3, starting transfers between devices, body(): lax.ppermute(other, ('yh', 'yl'), [(i, i ^ k) for i in range(4)])  34.8 us
    ppermute x1, waiting for transfers between devices, body(): in_vl = lax.ppermute(out_vl, ALL, vert_r)  24.9 us
    all_to_all x1, starting transfers between devices, body(): total = lax.all_to_all(total.reshape(32, 32, N), ('x', 'z'), 0, 0)  14.6 us
    ppermute x1, waiting for transfers between devices, body(): vr = lax.ppermute(vr, ALL, vert_r)  12.8 us
    unnamed x55, local copies, waits for them, and re-layouts  9.25 us
    pallas_call x1, Pallas kernels, turn(): pl.pallas_call(turn_body, out_shape=jax.ShapeDtypeStruct((2, N, N), BF16)...  7.75 us
    all_to_all x1, waiting for transfers between devices, body(): total = lax.all_to_all(total.reshape(32, 32, N), ('x', 'z'), 0, 0)  7.16 us
  transfers between devices with their start and end apart: 17, of which 9 were waited for; matrix products, arithmetic and copies ran while one was open for 1% of the time, Pallas kernels for 8%

profile of v7, /device:TPU:1, one launch (start us, length us, event | category | flops | bytes accessed | tf_op | source)
XLA Modules:
  0.0 231.3 jit_solution(9754525692662714041)
XLA Ops:
  0.6 1.5 fusion
  2.2 1.3 collective-permute-start.1
  3.5 0.6 fusion.1
  5.4 0.6 pad_add_fusion.pos_ref
  6.0 4.7 %collective-permute-start = (bf16[2,512,384]{2,1,0:T(8,128)(2,1)S(1)}, bf16[2,512,384]{2,1,0:T(8,128)(2,1)S(1)}, u32[]{:S(2)}, u32[]{:S(2)}) collective-permute-start(bf16[2,512,384]{2,1,0:T(8,128)(2,1)S(1)} %get-tuple-element.39), channel_id=1, source_target_pairs={{0,1},{1,2},{2,3},{3,4},{4,5},{5,6},{6,7},{7,8},{8,9},{9,10},{10,1... | collective-permute-start | bytes 2359304 | tf_op jit(solution)/shard_map/ppermute | solution.py:608
  10.7 2.8 %ends.1 = (bf16[2,384,512]{2,1,0:T(8,128)(2,1)}, bf16[2,384,384]{2,1,0:T(8,128)(2,1)}, bf16[2,384,384]{2,1,0:T(8,128)(2,1)}) custom-call(s32[4]{0:T(128)} %pad_add_fusion.pos_ref, bf16[2,512,512]{2,1,0:T(8,128)(2,1)} %own_ref.3), custom_call_target="tpu_custom_call" | custom-call | flops 1 | bytes 1 | tf_op jit(solution)/shard_map/ends/pallas_call | solution.py:431
  13.4 6.1 %collective-permute-start.2 = (bf16[2,384,512]{2,1,0:T(8,128)(2,1)}, bf16[2,384,512]{2,1,0:T(8,128)(2,1)S(1)}, u32[]{:S(2)}, u32[]{:S(2)}) collective-permute-start(bf16[2,384,512]{2,1,0:T(8,128)(2,1)} %get-tuple-element.20), channel_id=1, source_target_pairs={{16,32},{48,64},{80,96},{112,128},{144,160},{176,192},{208,224},{3... | collective-permute-start | bytes 2359304 | tf_op jit(solution)/shard_map/ppermute | solution.py:611
  19.5 2.7 %collective-permute-start.3 = (bf16[2,384,384]{2,1,0:T(8,128)(2,1)}, bf16[2,384,384]{2,1,0:T(8,128)(2,1)S(1)}, u32[]{:S(2)}, u32[]{:S(2)}) collective-permute-start(bf16[2,384,384]{2,1,0:T(8,128)(2,1)} %get-tuple-element.21), channel_id=1, source_target_pairs={{16,33},{17,34},{18,35},{19,36},{20,37},{21,38},{22,39},{23,40},{2... | collective-permute-start | bytes 1769480 | tf_op jit(solution)/shard_map/ppermute | solution.py:612
  22.3 1.3 collective-permute-start.4
  23.6 0.0 copy-start.4
  23.6 2.2 copy-done.4
  25.8 0.6 copy-done.16
  26.4 7.7 %turn.1.refs_0_.p_ref = bf16[2,1024,1024]{2,1,0:T(8,128)(2,1)S(1)} custom-call(s32[4]{0:T(128)S(1)} %copy-done.16, bf16[2,1024,1024]{2,1,0:T(8,128)(2,1)S(1)} %copy-done.4), custom_call_target="tpu_custom_call" | custom-call | flops 1 | bytes 1 | tf_op jit(solution)/shard_map/turn/pallas_call | solution.py:382
  34.2 0.0 copy-start.1
  34.2 4.5 %order.1.refs_1_.amp_ref = bf16[1024,1024]{1,0:T(8,128)(2,1)S(1)} custom-call(bf16[1024,1024]{1,0:T(8,128)(2,1)S(1)} %copy-done.6, bf16[1024,1024]{1,0:T(8,128)(2,1)S(1)} %copy-done.7), custom_call_target="tpu_custom_call" | custom-call | flops 1 | bytes 1 | tf_op jit(solution)/shard_map/order/pallas_call | solution.py:403
  38.7 0.0 copy-start.2
  38.7 0.0 copy-start.18
  38.7 0.0 copy-start.19
  38.8 0.0 copy-start.20
  38.8 0.0 copy-start.21
  38.8 0.0 copy-start.22
  38.8 24.9 %collective-permute-done.3.refs_3_.vl_ref = bf16[2,384,384]{2,1,0:T(8,128)(2,1)S(1)} collective-permute-done((bf16[2,384,384]{2,1,0:T(8,128)(2,1)}, bf16[2,384,384]{2,1,0:T(8,128)(2,1)S(1)}, u32[]{:S(2)}, u32[]{:S(2)}) %collective-permute-start.3) | collective-permute-done | bytes 589856 | tf_op jit(solution)/shard_map/ppermute | solution.py:612
  63.7 0.0 collective-permute-done.4.refs_4_.vr_ref
  63.7 0.0 collective-permute-done.1.r_ref
  63.7 0.0 collective-permute-done.l_ref
  63.7 0.0 collective-permute-done.2.refs_2_.v_ref
  63.8 0.7 cut.1
  64.6 0.2 copy-done.15
  64.7 0.3 copy-done.9
  65.0 0.2 copy-done.10
  65.2 0.2 copy-done.11
  65.5 0.0 collective-permute-start.5
  65.5 4.0 %collective-permute-done.5.c_ref = bf16[2,384,1280]{2,1,0:T(8,128)(2,1)S(1)} collective-permute-done((bf16[2,384,1280]{2,1,0:T(8,128)(2,1)S(1)}, bf16[2,384,1280]{2,1,0:T(8,128)(2,1)S(1)}, u32[]{:S(2)}, u32[]{:S(2)}) %collective-permute-start.5) | collective-permute-done | bytes 1966112 | tf_op jit(solution)/shard_map/ppermute | solution.py:616
  69.4 1.3 copy-done.24
  70.8 42.9 %led.1 = (bf16[2,512,512]{2,1,0:T(8,128)(2,1)}, bf16[2,512,384]{2,1,0:T(8,128)(2,1)}, bf16[2,512,384]{2,1,0:T(8,128)(2,1)}, bf16[2,384,512]{2,1,0:T(8,128)(2,1)}...) custom-call(s32[4]{0:T(128)S(1)} %copy-done.17, ...), custom_call_target="tpu_custom_call" | custom-call | flops 12999999488 | bytes 31457280 | tf_op jit(solution)/shard_map/led/pallas_call | solution.py:330
  113.7 0.2 collective-permute-start.12
  113.9 0.4 collective-permute-start.6
  114.3 6.7 %collective-permute-done.6.i_ref.token_ref = bf16[2,384,1280]{2,1,0:T(8,128)(2,1)S(1)} collective-permute-done((bf16[2,384,1280]{2,1,0:T(8,128)(2,1)}, bf16[2,384,1280]{2,1,0:T(8,128)(2,1)S(1)}, u32[]{:S(2)}, u32[]{:S(2)}) %collective-permute-start.6) | collective-permute-done | bytes 1966112 | tf_op jit(solution)/shard_map/ppermute | solution.py:620
  120.9 0.0 collective-permute-done.12.other_ref
  121.0 2.2 copy-done.5
  123.1 0.4 pair_sum.1
  123.5 1.3 copy-done.3
  124.8 14.6 %all-to-all-start = ((bf16[32,32,1024]{2,1,0:T(8,128)(2,1)}), bf16[32,32,1024]{2,1,0:T(8,128)(2,1)}, u32[]{:S(2)}, u32[]{:S(2)}) async-start(bf16[32,32,1024]{2,1,0:T(8,128)(2,1)} %bitcast.12), calls=%async_computation | async-start | bytes 4194304 | tf_op jit(solution)/shard_map/all_to_all | solution.py:629
  139.5 4.5 %collective-permute-start.7 = (bf16[2,384,512]{2,1,0:T(8,128)(2,1)}, bf16[2,384,512]{2,1,0:T(8,128)(2,1)S(1)}, u32[]{:S(2)}, u32[]{:S(2)}) collective-permute-start(bf16[2,384,512]{2,1,0:T(8,128)(2,1)} %get-tuple-element.25), channel_id=1, source_target_pairs={{16,32},{48,64},{80,96},{112,128},{144,160},{176,192},{208,224},{3... | collective-permute-start | bytes 2359304 | tf_op jit(solution)/shard_map/ppermute | solution.py:621
  144.0 1.1 sides.1
  145.1 1.3 collective-permute-start.8
  146.4 4.0 %collective-permute-start.9 = (bf16[2,512,384]{2,1,0:T(8,128)(2,1)S(1)}, bf16[2,512,384]{2,1,0:T(8,128)(2,1)S(1)}, u32[]{:S(2)}, u32[]{:S(2)}) collective-permute-start(bf16[2,512,384]{2,1,0:T(8,128)(2,1)S(1)} %get-tuple-element.29), channel_id=1, source_target_pairs={{0,1},{1,2},{2,3},{3,4},{4,5},{5,6},{6,7},{7,8},{8,9},{9,10},{10,1... | collective-permute-start | bytes 2359304 | tf_op jit(solution)/shard_map/ppermute | solution.py:627
  150.5 1.3 collective-permute-start.10
  151.8 5.5 %collective-permute-start.11 = (bf16[2,384,384]{2,1,0:T(8,128)(2,1)S(1)}, bf16[2,384,384]{2,1,0:T(8,128)(2,1)S(1)}, u32[]{:S(2)}, u32[]{:S(2)}) collective-permute-start(bf16[2,384,384]{2,1,0:T(8,128)(2,1)S(1)} %copy-done.25), channel_id=1, source_target_pairs={{16,33},{17,34},{18,35},{19,36},{20,37},{21,38},{22,39},{23,40},{2... | collective-permute-start | bytes 1769480 | tf_op jit(solution)/shard_map/ppermute | solution.py:623
  157.3 6.0 %collective-permute-done.10.vl_ref = bf16[2,384,384]{2,1,0:T(8,128)(2,1)S(1)} collective-permute-done((bf16[2,384,384]{2,1,0:T(8,128)(2,1)S(1)}, bf16[2,384,384]{2,1,0:T(8,128)(2,1)S(1)}, u32[]{:S(2)}, u32[]{:S(2)}) %collective-permute-start.10) | collective-permute-done | bytes 589856 | tf_op jit(solution)/shard_map/ppermute | solution.py:622
  163.3 12.8 %collective-permute-done.11.vr_ref = bf16[2,384,384]{2,1,0:T(8,128)(2,1)S(1)} collective-permute-done((bf16[2,384,384]{2,1,0:T(8,128)(2,1)S(1)}, bf16[2,384,384]{2,1,0:T(8,128)(2,1)S(1)}, u32[]{:S(2)}, u32[]{:S(2)}) %collective-permute-start.11) | collective-permute-done | bytes 589856 | tf_op jit(solution)/shard_map/ppermute | solution.py:623
  176.1 0.0 collective-permute-done.7.v_ref
  176.1 2.6 %collective-permute-done.8.l_ref = bf16[2,512,384]{2,1,0:T(8,128)(2,1)S(1)} collective-permute-done((bf16[2,512,384]{2,1,0:T(8,128)(2,1)S(1)}, bf16[2,512,384]{2,1,0:T(8,128)(2,1)S(1)}, u32[]{:S(2)}, u32[]{:S(2)}) %collective-permute-start.8) | collective-permute-done | bytes 786464 | tf_op jit(solution)/shard_map/ppermute | solution.py:626
  178.7 0.0 collective-permute-done.9.r_ref
  178.7 2.6 %tile_sum.1.token_ref = f32[2,512,512]{2,1,0:T(8,128)} custom-call(s32[4]{0:T(128)S(1)} %copy-done.17, bf16[2,512,512]{2,1,0:T(8,128)(2,1)S(1)} %copy-done.8, bf16[2,384,1280]{2,1,0:T(8,128)(2,1)S(1)} %collective-permute-done.6.i_ref.token_ref, bf16[2,384,512]{2,1,0:T(8,128)(2,1)S(1)} %collective-permute-done.7.v_ref, ...), custom_call_target="tpu_custom_call" | custom-call | flops 1 | bytes 1 | tf_op jit(solution)/shard_map/tile_sum/pallas_call | solution.py:519
  181.3 7.2 %all-to-all-done.x_ref = bf16[32,32,1024]{2,1,0:T(8,128)(2,1)} async-done(((bf16[32,32,1024]{2,1,0:T(8,128)(2,1)}), bf16[32,32,1024]{2,1,0:T(8,128)(2,1)}, u32[]{:S(2)}, u32[]{:S(2)}) %all-to-all-start) | async-done | bytes 2097184 | tf_op jit(solution)/shard_map/all_to_all | solution.py:629
  188.4 2.5 %gather_sum.1 = (f32[8,1024]{1,0:T(8,128)}, f32[8,1024]{1,0:T(8,128)}, f32[8,1024]{1,0:T(8,128)}, f32[8,1024]{1,0:T(8,128)}) custom-call(s32[4]{0:T(128)} %pad_add_fusion.pos_ref, bf16[32,32,1024]{2,1,0:T(8,128)(2,1)} %all-to-all-done.x_ref, f32[2,512,512]{2,1,0:T(8,128)} %tile_sum.1.token_ref), custom_call_target="tpu_custom_call" | custom-call | flops 1 | bytes 1 | tf_op jit(solution)/shard_map/gather_sum/pallas_call | solution.py:567
  190.9 31.6 %collective-permute-start.13 = (f32[8,1024]{1,0:T(8,128)}, f32[8,1024]{1,0:T(8,128)S(1)}, u32[]{:S(2)}, u32[]{:S(2)}) collective-permute-start(f32[8,1024]{1,0:T(8,128)} %get-tuple-element.35), channel_id=1, source_target_pairs={{0,1},{1,0},{32,33},{33,32},{2,3},{3,2},{34,35},{35,34},{4,5},{5,4... | collective-permute-start | bytes 98312 | tf_op jit(solution)/shard_map/ppermute | solution.py:632
  222.5 3.2 %collective-permute-start.14 = (f32[8,1024]{1,0:T(8,128)}, f32[8,1024]{1,0:T(8,128)S(1)}, u32[]{:S(2)}, u32[]{:S(2)}) collective-permute-start(f32[8,1024]{1,0:T(8,128)} %get-tuple-element.36), channel_id=1, source_target_pairs={{0,32},{1,33},{32,0},{33,1},{2,34},{3,35},{34,2},{35,3},{4,36},{5,... | collective-permute-start | bytes 98312 | tf_op jit(solution)/shard_map/ppermute | solution.py:632
  225.7 0.0 collective-permute-start.15
  225.7 1.9 collective-permute-done.14
  227.6 2.3 %collective-permute-done.15 = f32[8,1024]{1,0:T(8,128)S(1)} collective-permute-done((f32[8,1024]{1,0:T(8,128)}, f32[8,1024]{1,0:T(8,128)S(1)}, u32[]{:S(2)}, u32[]{:S(2)}) %collective-permute-start.15) | collective-permute-done | bytes 32800 | tf_op jit(solution)/shard_map/ppermute | solution.py:632
  229.9 0.8 add_bitcast_fusion
  230.7 0.6 copy.15
  (38 shorter events, 0.1 us)
Async XLA Ops:
  0.6 2.9 %copy-start.23 = (s32[1,1,2]{2,1,0:T(1,128)S(1)}, s32[1,1,2]{2,1,0:T(1,128)}, u32[]{:S(2)}) copy-start(s32[1,1,2]{2,1,0:T(1,128)} %param.14) | copy-start | bytes 28
  2.2 61.5 %collective-permute-start.1 = (bf16[2,512,384]{2,1,0:T(8,128)(2,1)S(1)}, bf16[2,512,384]{2,1,0:T(8,128)(2,1)S(1)}, u32[]{:S(2)}, u32[]{:S(2)}) collective-permute-start(bf16[2,512,384]{2,1,0:T(8,128)(2,1)S(1)} %get-tuple-element.38), channel_id=1, source_target_pairs={{1,0},{2,1},{3,2},{4,3},{5,4},{6,5},{7,6},{8,7},{9,8},{10,9},{11,1... | collective-permute-start | bytes 2359304 | tf_op jit(solution)/shard_map/ppermute | solution.py:609
  6.0 57.7 %collective-permute-start = (bf16[2,512,384]{2,1,0:T(8,128)(2,1)S(1)}, bf16[2,512,384]{2,1,0:T(8,128)(2,1)S(1)}, u32[]{:S(2)}, u32[]{:S(2)}) collective-permute-start(bf16[2,512,384]{2,1,0:T(8,128)(2,1)S(1)} %get-tuple-element.39), channel_id=1, source_target_pairs={{0,1},{1,2},{2,3},{3,4},{4,5},{5,6},{6,7},{7,8},{8,9},{9,10},{10,1... | collective-permute-start | bytes 2359304 | tf_op jit(solution)/shard_map/ppermute | solution.py:608
  13.4 50.3 %collective-permute-start.2 = (bf16[2,384,512]{2,1,0:T(8,128)(2,1)}, bf16[2,384,512]{2,1,0:T(8,128)(2,1)S(1)}, u32[]{:S(2)}, u32[]{:S(2)}) collective-permute-start(bf16[2,384,512]{2,1,0:T(8,128)(2,1)} %get-tuple-element.20), channel_id=1, source_target_pairs={{16,32},{48,64},{80,96},{112,128},{144,160},{176,192},{208,224},{3... | collective-permute-start | bytes 2359304 | tf_op jit(solution)/shard_map/ppermute | solution.py:611
  19.5 44.2 %collective-permute-start.3 = (bf16[2,384,384]{2,1,0:T(8,128)(2,1)}, bf16[2,384,384]{2,1,0:T(8,128)(2,1)S(1)}, u32[]{:S(2)}, u32[]{:S(2)}) collective-permute-start(bf16[2,384,384]{2,1,0:T(8,128)(2,1)} %get-tuple-element.21), channel_id=1, source_target_pairs={{16,33},{17,34},{18,35},{19,36},{20,37},{21,38},{22,39},{23,40},{2... | collective-permute-start | bytes 1769480 | tf_op jit(solution)/shard_map/ppermute | solution.py:612
  22.3 41.4 %collective-permute-start.4 = (bf16[2,384,384]{2,1,0:T(8,128)(2,1)}, bf16[2,384,384]{2,1,0:T(8,128)(2,1)S(1)}, u32[]{:S(2)}, u32[]{:S(2)}) collective-permute-start(bf16[2,384,384]{2,1,0:T(8,128)(2,1)} %get-tuple-element.22), channel_id=1, source_target_pairs={{17,32},{18,33},{19,34},{20,35},{21,36},{22,37},{23,38},{24,39},{2... | collective-permute-start | bytes 1769480 | tf_op jit(solution)/shard_map/ppermute | solution.py:613
  23.6 2.2 copy-start.4
  25.8 0.6 copy-start.16
  26.4 7.8 %copy-start.6 = (bf16[1024,1024]{1,0:T(8,128)(2,1)S(1)}, bf16[1024,1024]{1,0:T(8,128)(2,1)}, u32[]{:S(2)}) copy-start(bf16[1024,1024]{1,0:T(8,128)(2,1)} %amp_ref.1) | copy-start | bytes 6291460
  26.4 7.8 %copy-start.7 = (bf16[1024,1024]{1,0:T(8,128)(2,1)S(1)}, bf16[1024,1024]{1,0:T(8,128)(2,1)}, u32[]{:S(2)}) copy-start(bf16[1024,1024]{1,0:T(8,128)(2,1)} %constant.52.clone.perm_ref) | copy-start | bytes 6291460
  34.1 29.6 %copy-start = (bf16[2,1024,1024]{2,1,0:T(8,128)(2,1)}, bf16[2,1024,1024]{2,1,0:T(8,128)(2,1)S(1)}, u32[]{:S(2)}) copy-start(bf16[2,1024,1024]{2,1,0:T(8,128)(2,1)S(1)} %turn.1.refs_0_.p_ref) | copy-start | bytes 12582916
  34.2 29.6 %copy-start.1 = (bf16[2,512,512]{2,1,0:T(8,128)(2,1)S(1)}, bf16[2,512,512]{2,1,0:T(8,128)(2,1)}, u32[]{:S(2)}) copy-start(bf16[2,512,512]{2,1,0:T(8,128)(2,1)} %own_ref.3) | copy-start | bytes 3145732
  38.7 25.8 %copy-start.2 = (bf16[1024,1024]{1,0:T(8,128)(2,1)}, bf16[1024,1024]{1,0:T(8,128)(2,1)S(1)}, u32[]{:S(2)}) copy-start(bf16[1024,1024]{1,0:T(8,128)(2,1)S(1)} %order.1.refs_1_.amp_ref) | copy-start | bytes 6291460
  38.7 32.1 %copy-start.17 = (s32[4]{0:T(128)S(1)}, s32[4]{0:T(128)}, u32[]{:S(2)}) copy-start(s32[4]{0:T(128)} %pad_add_fusion.pos_ref) | copy-start | bytes 52
  38.7 32.1 %copy-start.18 = (bf16[256,768]{1,0:T(8,128)(2,1)S(1)}, bf16[256,768]{1,0:T(8,128)(2,1)}, u32[]{:S(2)}) copy-start(bf16[256,768]{1,0:T(8,128)(2,1)} %constant.49.clone.rf_ref) | copy-start | bytes 1179652
  38.7 32.0 %copy-start.19 = (bf16[768,256]{1,0:T(8,128)(2,1)S(1)}, bf16[768,256]{1,0:T(8,128)(2,1)}, u32[]{:S(2)}) copy-start(bf16[768,256]{1,0:T(8,128)(2,1)} %constant.48.clone.lf_ref) | copy-start | bytes 1179652
  38.8 32.0 %copy-start.20 = (bf16[256,768]{1,0:T(8,128)(2,1)S(1)}, bf16[256,768]{1,0:T(8,128)(2,1)}, u32[]{:S(2)}) copy-start(bf16[256,768]{1,0:T(8,128)(2,1)} %constant.47.clone.ri_ref) | copy-start | bytes 1179652
  38.8 32.0 %copy-start.21 = (bf16[768,256]{1,0:T(8,128)(2,1)S(1)}, bf16[768,256]{1,0:T(8,128)(2,1)}, u32[]{:S(2)}) copy-start(bf16[768,256]{1,0:T(8,128)(2,1)} %constant.46.clone.li_ref) | copy-start | bytes 1179652
  38.8 32.0 %copy-start.22 = (f32[2,8,1,128]{3,2,1,0:T(1,128)S(1)}, f32[2,8,1,128]{3,2,1,0:T(1,128)}, u32[]{:S(2)}) copy-start(f32[2,8,1,128]{3,2,1,0:T(1,128)} %constant.50.clone.twl_ref) | copy-start | bytes 24580
  63.7 0.8 copy-start.14
  63.7 1.0 copy-start.15
  63.7 1.3 copy-start.9
  63.7 1.5 copy-start.10
  63.8 1.7 copy-start.11
  65.5 4.0 %collective-permute-start.5 = (bf16[2,384,1280]{2,1,0:T(8,128)(2,1)S(1)}, bf16[2,384,1280]{2,1,0:T(8,128)(2,1)S(1)}, u32[]{:S(2)}, u32[]{:S(2)}) collective-permute-start(bf16[2,384,1280]{2,1,0:T(8,128)(2,1)S(1)} %cut.1), channel_id=1, source_target_pairs={{0,16},{16,0},{1,17},{17,1},{2,18},{18,2},{3,19},{19,3},{4,20},{20... | collective-permute-start | bytes 5898248 | tf_op jit(solution)/shard_map/ppermute | solution.py:616
  69.4 1.3 copy-start.24
  113.7 7.3 %collective-permute-start.12 = (bf16[1024,1024]{1,0:T(8,128)(2,1)}, bf16[1024,1024]{1,0:T(8,128)(2,1)S(1)}, u32[]{:S(2)}, u32[]{:S(2)}) collective-permute-start(bf16[1024,1024]{1,0:T(8,128)(2,1)} %get-tuple-element.33), channel_id=1, source_target_pairs={{0,16},{16,0},{1,17},{17,1},{2,18},{18,2},{3,19},{19,3},{4,20},{20... | collective-permute-start | bytes 6291464 | tf_op jit(solution)/shard_map/ppermute | solution.py:624
  113.9 7.0 %collective-permute-start.6 = (bf16[2,384,1280]{2,1,0:T(8,128)(2,1)}, bf16[2,384,1280]{2,1,0:T(8,128)(2,1)S(1)}, u32[]{:S(2)}, u32[]{:S(2)}) collective-permute-start(bf16[2,384,1280]{2,1,0:T(8,128)(2,1)} %get-tuple-element.24), channel_id=1, source_target_pairs={{0,16},{16,0},{1,17},{17,1},{2,18},{18,2},{3,19},{19,3},{4,20},{20... | collective-permute-start | bytes 5898248 | tf_op jit(solution)/shard_map/ppermute | solution.py:620
  120.9 2.2 copy-start.5
  123.5 1.3 copy-start.3
  124.8 19.2 %copy-start.12 = (bf16[2,512,384]{2,1,0:T(8,128)(2,1)S(1)}, bf16[2,512,384]{2,1,0:T(8,128)(2,1)}, u32[]{:S(2)}) copy-start(bf16[2,512,384]{2,1,0:T(8,128)(2,1)} %get-tuple-element.26.l_ref) | copy-start | bytes 2359300
  124.8 19.2 %copy-start.13 = (bf16[2,512,384]{2,1,0:T(8,128)(2,1)S(1)}, bf16[2,512,384]{2,1,0:T(8,128)(2,1)}, u32[]{:S(2)}) copy-start(bf16[2,512,384]{2,1,0:T(8,128)(2,1)} %get-tuple-element.27.r_ref) | copy-start | bytes 2359300
  124.8 63.6 %all-to-all-start = ((bf16[32,32,1024]{2,1,0:T(8,128)(2,1)}), bf16[32,32,1024]{2,1,0:T(8,128)(2,1)}, u32[]{:S(2)}, u32[]{:S(2)}) async-start(bf16[32,32,1024]{2,1,0:T(8,128)(2,1)} %bitcast.12), calls=%async_computation | async-start | bytes 4194304 | tf_op jit(solution)/shard_map/all_to_all | solution.py:629
  139.5 11.0 %copy-start.26 = (bf16[2,384,384]{2,1,0:T(8,128)(2,1)S(1)}, bf16[2,384,384]{2,1,0:T(8,128)(2,1)}, u32[]{:S(2)}) copy-start(bf16[2,384,384]{2,1,0:T(8,128)(2,1)} %get-tuple-element.30) | copy-start | bytes 1769476
  139.5 12.3 %copy-start.25 = (bf16[2,384,384]{2,1,0:T(8,128)(2,1)S(1)}, bf16[2,384,384]{2,1,0:T(8,128)(2,1)}, u32[]{:S(2)}) copy-start(bf16[2,384,384]{2,1,0:T(8,128)(2,1)} %get-tuple-element.31) | copy-start | bytes 1769476
  139.5 39.2 %copy-start.8 = (bf16[2,512,512]{2,1,0:T(8,128)(2,1)S(1)}, bf16[2,512,512]{2,1,0:T(8,128)(2,1)}, u32[]{:S(2)}) copy-start(bf16[2,512,512]{2,1,0:T(8,128)(2,1)} %get-tuple-element.23.c_ref) | copy-start | bytes 3145732
  139.5 36.6 %collective-permute-start.7 = (bf16[2,384,512]{2,1,0:T(8,128)(2,1)}, bf16[2,384,512]{2,1,0:T(8,128)(2,1)S(1)}, u32[]{:S(2)}, u32[]{:S(2)}) collective-permute-start(bf16[2,384,512]{2,1,0:T(8,128)(2,1)} %get-tuple-element.25), channel_id=1, source_target_pairs={{16,32},{48,64},{80,96},{112,128},{144,160},{176,192},{208,224},{3... | collective-permute-start | bytes 2359304 | tf_op jit(solution)/shard_map/ppermute | solution.py:621
  145.1 33.6 %collective-permute-start.8 = (bf16[2,512,384]{2,1,0:T(8,128)(2,1)S(1)}, bf16[2,512,384]{2,1,0:T(8,128)(2,1)S(1)}, u32[]{:S(2)}, u32[]{:S(2)}) collective-permute-start(bf16[2,512,384]{2,1,0:T(8,128)(2,1)S(1)} %get-tuple-element.28), channel_id=1, source_target_pairs={{1,0},{2,1},{3,2},{4,3},{5,4},{6,5},{7,6},{8,7},{9,8},{10,9},{11,1... | collective-permute-start | bytes 2359304 | tf_op jit(solution)/shard_map/ppermute | solution.py:626
  146.4 32.3 %collective-permute-start.9 = (bf16[2,512,384]{2,1,0:T(8,128)(2,1)S(1)}, bf16[2,512,384]{2,1,0:T(8,128)(2,1)S(1)}, u32[]{:S(2)}, u32[]{:S(2)}) collective-permute-start(bf16[2,512,384]{2,1,0:T(8,128)(2,1)S(1)} %get-tuple-element.29), channel_id=1, source_target_pairs={{0,1},{1,2},{2,3},{3,4},{4,5},{5,6},{6,7},{7,8},{8,9},{9,10},{10,1... | collective-permute-start | bytes 2359304 | tf_op jit(solution)/shard_map/ppermute | solution.py:627
  150.5 12.8 %collective-permute-start.10 = (bf16[2,384,384]{2,1,0:T(8,128)(2,1)S(1)}, bf16[2,384,384]{2,1,0:T(8,128)(2,1)S(1)}, u32[]{:S(2)}, u32[]{:S(2)}) collective-permute-start(bf16[2,384,384]{2,1,0:T(8,128)(2,1)S(1)} %copy-done.26), channel_id=1, source_target_pairs={{17,32},{18,33},{19,34},{20,35},{21,36},{22,37},{23,38},{24,39},{2... | collective-permute-start | bytes 1769480 | tf_op jit(solution)/shard_map/ppermute | solution.py:622
  151.8 24.3 %collective-permute-start.11 = (bf16[2,384,384]{2,1,0:T(8,128)(2,1)S(1)}, bf16[2,384,384]{2,1,0:T(8,128)(2,1)S(1)}, u32[]{:S(2)}, u32[]{:S(2)}) collective-permute-start(bf16[2,384,384]{2,1,0:T(8,128)(2,1)S(1)} %copy-done.25), channel_id=1, source_target_pairs={{16,33},{17,34},{18,35},{19,36},{20,37},{21,38},{22,39},{23,40},{2... | collective-permute-start | bytes 1769480 | tf_op jit(solution)/shard_map/ppermute | solution.py:623
  190.9 34.8 %collective-permute-start.13 = (f32[8,1024]{1,0:T(8,128)}, f32[8,1024]{1,0:T(8,128)S(1)}, u32[]{:S(2)}, u32[]{:S(2)}) collective-permute-start(f32[8,1024]{1,0:T(8,128)} %get-tuple-element.35), channel_id=1, source_target_pairs={{0,1},{1,0},{32,33},{33,32},{2,3},{3,2},{34,35},{35,34},{4,5},{5,4... | collective-permute-start | bytes 98312 | tf_op jit(solution)/shard_map/ppermute | solution.py:632
  222.5 5.1 %collective-permute-start.14 = (f32[8,1024]{1,0:T(8,128)}, f32[8,1024]{1,0:T(8,128)S(1)}, u32[]{:S(2)}, u32[]{:S(2)}) collective-permute-start(f32[8,1024]{1,0:T(8,128)} %get-tuple-element.36), channel_id=1, source_target_pairs={{0,32},{1,33},{32,0},{33,1},{2,34},{3,35},{34,2},{35,3},{4,36},{5,... | collective-permute-start | bytes 98312 | tf_op jit(solution)/shard_map/ppermute | solution.py:632
  225.7 4.2 %collective-permute-start.15 = (f32[8,1024]{1,0:T(8,128)}, f32[8,1024]{1,0:T(8,128)S(1)}, u32[]{:S(2)}, u32[]{:S(2)}) collective-permute-start(f32[8,1024]{1,0:T(8,128)} %get-tuple-element.37), channel_id=1, source_target_pairs={{0,33},{1,32},{32,1},{33,0},{2,35},{3,34},{34,3},{35,2},{4,37},{5,... | collective-permute-start | bytes 98312 | tf_op jit(solution)/shard_map/ppermute | solution.py:632
